TPU v7x, 128 devices: a whole 4x4x4 slice. The times are simulated.
128 devices in a mesh: group: 4 (over z), shard: 4 (over y_hi, core), tensor: 8 (over y_lo, x).
Axes of the slice: x: 4, y: 4 (y_hi: 2, y_lo: 2; y = y_hi * 2 + y_lo), z: 4, core: 2. Of those that a mesh axis runs over, the one named last changes fastest.
Arguments:
- prompt_states: bfloat16 [8192, 8192], P(('group', 'shard')), may hold values from -6 to 6
- prompt_lens: int32 [4, 3], replicated, may hold values from 1 to 1024, 2048 in all within a row
- w_query: bfloat16 [8192, 8192], P('shard', 'tensor'), may hold values from -0.06629126 to 0.06629126
- w_keyval: bfloat16 [8192, 2, 1024], P('shard', None, 'tensor'), may hold values from -0.06629126 to 0.06629126
- w_out: bfloat16 [8192, 8192], P('tensor', 'shard'), may hold values from -0.0625 to 0.0625
- decode_states: bfloat16 [64, 8192], P(('group', 'shard')), may hold values from -6 to 6
- kv_cache: bfloat16 [64, 2048, 2, 1024], P(('group', 'shard'), None, None, 'tensor'), may hold values from -6 to 6
- cache_len: int32 [64], P(('group', 'shard')), may hold values from 512 to 2044
- row_prompt: int32 [64], P(('group', 'shard')), may hold values from 0 to 12, as said below
Outputs:
- prompt_context: bfloat16 [8192, 8192], P(('group', 'shard'), 'tensor')
- decode_updates: bfloat16 [4, 64, 8192], P(None, ('group', 'shard'))
Inputs may be any that keep to these rules, and one draw needn't show every extreme that they name: `row_prompt`: each prompt 0 to 11 is named by exactly one row; the 4 rows k*4 to (k+1)*4 - 1 of one device name at most one prompt; every other row holds 12.
All inputs are finite; a program needn't handle non-finite values.
Results may differ from a plain program's by a relative error of at most 0.023.
Values may be sent and summed in bfloat16 or wider, within the bound.
A program may use at most 192 MiB of HBM per device.

v0:
```python
import jax
import jax.numpy as jnp
from jax import lax
from jax.sharding import PartitionSpec as P

HD = 128
CACHE = 2048
STEPS = 4


EPSILON = 1e-05


def normalize(states):
    values = states.astype(jnp.float32)
    return (values * lax.rsqrt(jnp.mean(values * values, axis=-1, keepdims=True) + EPSILON)).astype(
        jnp.bfloat16
    )


def body(
    prompt_states,
    prompt_lens,
    w_query,
    w_keyval,
    w_out,
    decode_states,
    kv_cache,
    cache_len,
    row_prompt,
):
    shard_index = lax.axis_index("shard")
    group_index = lax.axis_index("group")
    d_part = w_query.shape[0]
    q_cols = w_query.shape[1]
    kv_cols = w_keyval.shape[2]
    heads_local = q_cols // HD
    kv_local = kv_cols // HD
    groups = heads_local // kv_local
    tok_local = prompt_states.shape[0]
    rows_local = decode_states.shape[0]
    inv_root = HD ** (-0.5)
    w_joined = jnp.concatenate([w_query, w_keyval.reshape(d_part, 2 * kv_cols)], axis=1)
    prompt_normed = normalize(prompt_states)
    query_piece = lax.all_gather(w_query, "shard", axis=0, tiled=True)
    keyval_piece = lax.all_gather(w_keyval, "shard", axis=0, tiled=True)
    amount = query_piece.shape[0]
    query_sum = jnp.dot(prompt_normed, query_piece, preferred_element_type=jnp.float32)
    keyval_sum = jnp.dot(
        prompt_normed, keyval_piece.reshape(amount, 2 * kv_cols), preferred_element_type=jnp.float32
    )
    queries = query_sum.astype(jnp.bfloat16)
    keyvals = keyval_sum.astype(jnp.bfloat16)
    keyvals = keyvals.reshape(tok_local, 2, kv_cols)
    query_heads = queries.reshape(tok_local, kv_local, groups, HD)
    group_pick = jnp.arange(prompt_lens.shape[0], dtype=jnp.int32) == group_index
    lens_mine = jnp.sum(jnp.where(group_pick[:, None], prompt_lens, 0), axis=0)
    bounds = jnp.cumsum(lens_mine)
    query_pos = shard_index * tok_local + jnp.arange(tok_local, dtype=jnp.int32)
    query_seg = jnp.sum((query_pos[:, None] >= bounds[None, :]).astype(jnp.int32), axis=1)
    piece = lax.all_gather(keyvals, "shard", axis=0, tiled=True)
    highest = jnp.full((kv_local, groups, tok_local), -1e30, jnp.float32)
    amount = piece.shape[0]
    key_pos = jnp.arange(amount, dtype=jnp.int32)
    key_seg = jnp.sum((key_pos[:, None] >= bounds[None, :]).astype(jnp.int32), axis=1)
    allowed = (query_seg[:, None] == key_seg[None, :]) & (key_pos[None, :] <= query_pos[:, None])
    keys = piece[:, 0].reshape(amount, kv_local, HD)
    values = piece[:, 1].reshape(amount, kv_local, HD)
    scores = (
        jnp.einsum("qkgd,nkd->kgqn", query_heads, keys, preferred_element_type=jnp.float32)
        * inv_root
    )
    masked = jnp.where(allowed, scores, -1e30)
    new_high = jnp.maximum(highest, jnp.max(masked, axis=-1))
    weights = jnp.where(allowed, jnp.exp(masked - new_high[..., None]), 0.0)
    totals = jnp.sum(weights, axis=-1)
    mixed = jnp.einsum(
        "kgqn,nkd->kgqd", weights.astype(jnp.bfloat16), values, preferred_element_type=jnp.float32
    )
    highest, totals, mixed = (new_high, totals, mixed)
    context = (mixed / totals[..., None]).astype(jnp.bfloat16)
    prompt_context = jnp.transpose(context, (2, 0, 1, 3)).reshape(tok_local, q_cols)
    lens_flat = prompt_lens.reshape(-1)
    prompt_count = lens_flat.shape[0]
    starts = jnp.cumsum(lens_flat) - lens_flat
    onehot = row_prompt[:, None] == jnp.arange(prompt_count, dtype=jnp.int32)[None, :]
    is_new = jnp.any(onehot, axis=1)
    row_start = jnp.sum(jnp.where(onehot, starts[None, :], 0), axis=1)
    new_len = jnp.sum(jnp.where(onehot, lens_flat[None, :], 0), axis=1)
    lengths = jnp.where(is_new, new_len, cache_len)
    all_keyvals = lax.all_gather(keyvals, ("group", "shard"), axis=0, tiled=True)
    padded = jnp.concatenate([all_keyvals, jnp.zeros((CACHE, 2, kv_cols), jnp.bfloat16)], axis=0)
    taken = jax.vmap(lambda first_pos: lax.dynamic_slice_in_dim(padded, first_pos, CACHE, 0))(
        row_start
    )
    cache_rows = jnp.where(is_new[:, None, None, None], taken, kv_cache)
    cache_keys = cache_rows[:, :, 0].reshape(rows_local, CACHE, kv_local, HD)
    cache_vals = cache_rows[:, :, 1].reshape(rows_local, CACHE, kv_local, HD)
    valid = jnp.arange(CACHE, dtype=jnp.int32)[None, :] < lengths[:, None]
    state = decode_states.astype(jnp.float32)
    fresh_list = []
    updates = []
    for step in range(STEPS):
        normed = normalize(state)
        row_block = lax.all_gather(normed, "shard", axis=0, tiled=True)
        own_rows = lax.dynamic_slice_in_dim(row_block, shard_index * d_part, d_part, 1)
        fresh_proj = lax.psum_scatter(
            jnp.dot(own_rows, w_joined, preferred_element_type=jnp.float32),
            "shard",
            scatter_dimension=0,
            tiled=True,
        ).astype(jnp.bfloat16)
        step_queries = fresh_proj[:, :q_cols].reshape(rows_local, kv_local, groups, HD)
        fresh_list.append(fresh_proj[:, q_cols:].reshape(rows_local, 2, kv_local, HD))
        fresh_all = jnp.stack(fresh_list, axis=1)
        old_scores = (
            jnp.einsum(
                "rkgd,rckd->rkgc", step_queries, cache_keys, preferred_element_type=jnp.float32
            )
            * inv_root
        )
        new_scores = (
            jnp.einsum(
                "rkgd,rckd->rkgc",
                step_queries,
                fresh_all[:, :, 0],
                preferred_element_type=jnp.float32,
            )
            * inv_root
        )
        old_masked = jnp.where(valid[:, None, None, :], old_scores, -1e30)
        top_score = jnp.maximum(jnp.max(old_masked, axis=-1), jnp.max(new_scores, axis=-1))[
            ..., None
        ]
        old_weights = jnp.where(valid[:, None, None, :], jnp.exp(old_masked - top_score), 0.0)
        new_weights = jnp.exp(new_scores - top_score)
        weight_sum = jnp.sum(old_weights, axis=-1) + jnp.sum(new_weights, axis=-1)
        blended = jnp.einsum(
            "rkgc,rckd->rkgd",
            old_weights.astype(jnp.bfloat16),
            cache_vals,
            preferred_element_type=jnp.float32,
        )
        blended = blended + jnp.einsum(
            "rkgc,rckd->rkgd",
            new_weights.astype(jnp.bfloat16),
            fresh_all[:, :, 1],
            preferred_element_type=jnp.float32,
        )
        row_context = (
            (blended / weight_sum[..., None]).astype(jnp.bfloat16).reshape(rows_local, q_cols)
        )
        context_block = lax.all_gather(row_context, "shard", axis=0, tiled=True)
        partial_out = jnp.dot(context_block, w_out, preferred_element_type=jnp.float32)
        head_total = lax.psum(partial_out.astype(jnp.bfloat16), "tensor").astype(jnp.float32)
        update = lax.all_to_all(head_total, "shard", split_axis=0, concat_axis=1, tiled=True)
        updates.append(update.astype(jnp.bfloat16))
        state = state + update
    return (prompt_context, jnp.stack(updates, axis=0))


def solution(mesh):
    in_specs = (
        P(("group", "shard"), None),
        P(),
        P("shard", "tensor"),
        P("shard", None, "tensor"),
        P("tensor", "shard"),
        P(("group", "shard"), None),
        P(("group", "shard"), None, None, "tensor"),
        P(("group", "shard")),
        P(("group", "shard")),
    )
    out_specs = (P(("group", "shard"), "tensor"), P(None, ("group", "shard"), None))
    return jax.shard_map(body, mesh=mesh, in_specs=in_specs, out_specs=out_specs, check_vma=False)
```

profile of v0, /device:TPU:1, one launch (start us, length us, event | category | flops | bytes accessed | tf_op | source)
XLA Modules:
  0.0 783.8 jit_solution(11002473445038311786)
XLA Ops:
  7.9 5.1 fusion.3
  13.1 38.8 %all-gather.13.cloned.1.call-done = bf16[8192,2,128]{2,1,0:T(2,128)(2,1)} async-done(((bf16[2048,2,128]{2,1,0:T(2,128)(2,1)}), bf16[8192,2,128]{2,1,0:T(2,128)(2,1)}) %all-gather.13.cloned.1.call-update) | async-done | bytes 4194320 | tf_op jit(solution)/shard_map/all_gather | solution.py:46
  51.9 7.3 fusion.30
  61.1 7.4 all-gather
  76.2 13.9 %all-reduce.2 = bf16[16,1280]{1,0:T(8,128)(2,1)S(1)} all-reduce(f32[16,1280]{1,0:T(8,128)S(1)} %fusion.88), channel_id=2, replica_groups=mesh['group'=4,'shard'=4,'tensor'=8] {'shard'}, use_global_device_ids=true, to_apply=%region_10.11.clone | all-reduce | flops 20480 | bytes 122880
  90.3 24.8 %all-gather.19.cloned.1.call-done = bf16[8192,2,128]{2,1,0:T(2,128)(2,1)} async-done(((bf16[512,2,128]{2,1,0:T(2,128)(2,1)}), bf16[8192,2,128]{2,1,0:T(2,128)(2,1)}) %all-gather.19.cloned.1.call-update) | async-done | bytes 4194320 | tf_op jit(solution)/shard_map/all_gather | solution.py:91
  115.1 10.1 %concatenate.10 = bf16[10240,2,128]{2,1,0:T(2,128)(2,1)} pad(bf16[8192,2,128]{2,1,0:T(2,128)(2,1)} %all-gather.19.cloned.1.call-done, bf16[]{:T(256)} %constant.28.clone.1), padding=0_2048x0_0x0_0 | pad | bytes 9437186 | tf_op jit(solution)/shard_map/concatenate | solution.py:92
  125.2 11.9 %while.1 = (s32[]{:T(128)}, bf16[10240,2,128]{2,1,0:T(2,128)(2,1)}, s32[4,3]{1,0:T(4,128)S(1)}, bf16[4,2048,2,128]{3,1,0,2:T(8,128)(2,1)}, s32[]{:T(128)}) while((s32[]{:T(128)}, bf16[10240,2,128]{2,1,0:T(2,128)(2,1)}, s32[4,3]{1,0:T(4,128)S(1)}, bf16[4,2048,2,128]{3,1,0,2:T(8,128)(2,1)}, s32[]{:T(128)}) %tuple.43), condition=%wide.while_cond, body=%wide.while_body.sunk | while | flops 2 | bytes 4194409 | solution.py:93
  143.7 6.8 all-gather.1
  154.0 65.3 %all-reduce.11.cloned.1.call-done = bf16[4,4,2048]{2,1,0:T(4,128)(2,1)} async-done(((bf16[4,4,2048]{2,1,0:T(4,128)(2,1)}), bf16[4,4,2048]{2,1,0:T(4,128)(2,1)}) %all-reduce.11.cloned.1.call-update) | async-done | bytes 65552 | tf_op jit(solution)/shard_map/psum | solution.py:155
  220.8 9.5 %all-to-all-start = ((f32[4,4,2048]{2,1,0:T(4,128)}), f32[4,4,2048]{2,1,0:T(4,128)S(1)}, u32[]{:S(2)}, u32[]{:S(2)}) async-start(f32[4,4,2048]{2,1,0:T(4,128)} %all_to_all.61), calls=%async_computation | async-start | bytes 262144 | tf_op jit(solution)/shard_map/all_to_all | solution.py:156
  235.6 8.3 %all-gather.2 = bf16[4,4,8192]{2,1,0:T(4,128)(2,1)S(1)} all-gather(bf16[1,4,8192]{2,1,0:T(4,128)(2,1)S(1)} %fusion.78), channel_id=1, replica_groups=mesh['group'=4,'shard'=4,'tensor'=8] {'shard'}, dimensions={0}, use_global_device_ids=true | all-gather | bytes 327680 | tf_op jit(solution)/shard_map/all_gather | solution.py:105
  247.3 14.1 %all-reduce.3 = bf16[16,1280]{1,0:T(8,128)(2,1)S(1)} all-reduce(f32[16,1280]{1,0:T(8,128)S(1)} %fusion.86), channel_id=3, replica_groups=mesh['group'=4,'shard'=4,'tensor'=8] {'shard'}, use_global_device_ids=true, to_apply=%region_17.18.clone | all-reduce | flops 20480 | bytes 122880
  266.5 6.9 all-gather.3
  277.0 67.4 %all-reduce.13.cloned.1.call-done = bf16[4,4,2048]{2,1,0:T(4,128)(2,1)} async-done(((bf16[4,4,2048]{2,1,0:T(4,128)(2,1)}), bf16[4,4,2048]{2,1,0:T(4,128)(2,1)}) %all-reduce.13.cloned.1.call-update) | async-done | bytes 65552 | tf_op jit(solution)/shard_map/psum | solution.py:155
  345.2 14.4 %all_to_all.82 = f32[4,4,2048]{2,1,0:T(4,128)S(1)} all-to-all(f32[4,4,2048]{2,1,0:T(4,128)S(1)} %all_to_all.66), channel_id=1, replica_groups=mesh['group'=4,'shard'=4,'tensor'=8] {'shard'}, dimensions={0} | all-to-all | bytes 262144 | tf_op jit(solution)/shard_map/all_to_all | solution.py:156
  359.9 8.2 %all-gather.4 = bf16[4,4,8192]{2,1,0:T(4,128)(2,1)S(1)} all-gather(bf16[1,4,8192]{2,1,0:T(4,128)(2,1)S(1)} %fusion.79), channel_id=1, replica_groups=mesh['group'=4,'shard'=4,'tensor'=8] {'shard'}, dimensions={0}, use_global_device_ids=true | all-gather | bytes 327680 | tf_op jit(solution)/shard_map/all_gather | solution.py:105
  371.4 14.1 %all-reduce.4 = bf16[16,1280]{1,0:T(8,128)(2,1)S(1)} all-reduce(f32[16,1280]{1,0:T(8,128)S(1)} %fusion.84), channel_id=4, replica_groups=mesh['group'=4,'shard'=4,'tensor'=8] {'shard'}, use_global_device_ids=true, to_apply=%region_24.25.clone | all-reduce | flops 20480 | bytes 122880
  390.6 6.9 all-gather.5
  401.1 67.4 %all-reduce.15.cloned.1.call-done = bf16[4,4,2048]{2,1,0:T(4,128)(2,1)} async-done(((bf16[4,4,2048]{2,1,0:T(4,128)(2,1)}), bf16[4,4,2048]{2,1,0:T(4,128)(2,1)}) %all-reduce.15.cloned.1.call-update) | async-done | bytes 65552 | tf_op jit(solution)/shard_map/psum | solution.py:155
  469.3 14.4 %all_to_all.83 = f32[4,4,2048]{2,1,0:T(4,128)S(1)} all-to-all(f32[4,4,2048]{2,1,0:T(4,128)S(1)} %all_to_all.71), channel_id=1, replica_groups=mesh['group'=4,'shard'=4,'tensor'=8] {'shard'}, dimensions={0} | all-to-all | bytes 262144 | tf_op jit(solution)/shard_map/all_to_all | solution.py:156
  484.0 8.2 %all-gather.6 = bf16[4,4,8192]{2,1,0:T(4,128)(2,1)S(1)} all-gather(bf16[1,4,8192]{2,1,0:T(4,128)(2,1)S(1)} %fusion.80), channel_id=1, replica_groups=mesh['group'=4,'shard'=4,'tensor'=8] {'shard'}, dimensions={0}, use_global_device_ids=true | all-gather | bytes 327680 | tf_op jit(solution)/shard_map/all_gather | solution.py:105
  495.5 14.1 %all-reduce.5 = bf16[16,1280]{1,0:T(8,128)(2,1)S(1)} all-reduce(f32[16,1280]{1,0:T(8,128)S(1)} %fusion.82), channel_id=5, replica_groups=mesh['group'=4,'shard'=4,'tensor'=8] {'shard'}, use_global_device_ids=true, to_apply=%region_31.32.clone | all-reduce | flops 20480 | bytes 122880
  514.7 6.9 all-gather.7
  528.3 64.3 %all-reduce.17.cloned.1.call-done = bf16[4,4,2048]{2,1,0:T(4,128)(2,1)} async-done(((bf16[4,4,2048]{2,1,0:T(4,128)(2,1)}), bf16[4,4,2048]{2,1,0:T(4,128)(2,1)}) %all-reduce.17.cloned.1.call-update) | async-done | bytes 65552 | tf_op jit(solution)/shard_map/psum | solution.py:155
  592.6 9.5 %all-to-all-start.3 = ((bf16[4,4,2048]{2,1,0:T(4,128)(2,1)}), bf16[4,4,2048]{2,1,0:T(4,128)(2,1)S(1)}, u32[]{:S(2)}, u32[]{:S(2)}) async-start(bf16[4,4,2048]{2,1,0:T(4,128)(2,1)} %all-reduce.17.cloned.1.call-done), calls=%async_computation.3 | async-start | bytes 131072 | tf_op jit(solution)/shard_map/all_to_all | solution.py:156
  607.8 101.2 %all-gather.17.cloned.1.call-done = bf16[8192,1024]{1,0:T(8,128)(2,1)} async-done(((bf16[2048,1024]{1,0:T(8,128)(2,1)}), bf16[8192,1024]{1,0:T(8,128)(2,1)}) %all-gather.17.cloned.1.call-update) | async-done | bytes 16777232 | tf_op jit(solution)/shard_map/all_gather | solution.py:45
  709.1 14.9 %fusion.23 = bf16[64,8,8,128]{3,2,1,0:T(8,128)(2,1)S(1)} fusion(bf16[8192,1024]{1,0:T(8,128)(2,1)} %all-gather.17.cloned.1.call-done, bf16[512,8192]{1,0:T(8,128)(2,1)} %param.9, f32[512]{0:T(512)S(1)} %add_rsqrt_fusion), kind=kOutput, calls=%fused_computation.38 | convolution fusion | flops 8603041792 | bytes 26216448 | tf_op jit(solution)/shard_map/dot_general | solution.py:48
  724.0 7.5 all-gather.15.cloned.1.call-done
  731.5 14.6 %fusion = (f32[8,512]{1,0:T(8,128)S(1)}, f32[2048,512,8]{1,0,2:T(8,128)}) fusion(pred[512,2048]{0,1:T(8,128)(4,1)S(1)} %fusion.12, bf16[64,8,8,128]{3,2,1,0:T(8,128)(2,1)S(1)} %fusion.23, bf16[2048,2,128]{2,0,1:T(8,128)(2,1)} %all-gather.15.cloned.1.call-done), kind=kOutput, calls=%fused_computation.5 | convolution fusion | flops 2172645376 | bytes 36192256 | tf_op jit(solution)/shard_map/qkgd,nkd->kgqn/dot_general | solution.py:70
  746.1 14.9 %fusion.1 = f32[8,512]{1,0:T(8,128)S(1)} fusion(f32[2048,512,8]{1,0,2:T(8,128)} %get-tuple-element.59, f32[8,512]{1,0:T(8,128)S(1)} %broadcast_maximum_fusion, pred[512,2048]{0,1:T(8,128)(4,1)S(1)} %fusion.12), kind=kLoop, calls=%fused_computation.6 | loop fusion | flops 41938944 | bytes 34635776 | tf_op jit(solution)/shard_map/reduce_sum | solution.py:76
  761.1 14.6 %divide_convert_fusion = bf16[8,512,128]{1,2,0:T(8,128)(2,1)S(1)} fusion(f32[8,512]{1,0:T(8,128)S(1)} %fusion.1, f32[2048,512,8]{1,0,2:T(8,128)} %get-tuple-element.59, f32[8,512]{1,0:T(8,128)S(1)} %broadcast_maximum_fusion, pred[512,2048]{0,1:T(8,128)(4,1)S(1)} %fusion.12, bf16[2048,2,128]{2,0,1:T(8,128)(2,1)S(1)} %copy-done.4), kind=kOutput, calls=%fused_computation.36 | convolution fusion | flops 2190475264 | bytes 36208640 | tf_op jit(solution)/shard_map/kgqn,nkd->kgqd/dot_general | solution.py:77
  (168 shorter events, 86.8 us)
Async XLA Ops:
  7.2 44.7 %all-gather.13.cloned.1.call-start = ((), (), s32[]{:S(2)}) async-start(), calls=%async_computation.4 | async-start | bytes 5242880 | tf_op jit(solution)/shard_map/all_gather | solution.py:46
  7.9 107.2 %all-gather.19.cloned.1.call-start = ((), (), s32[]{:S(2)}) async-start(), calls=%async_computation.7 | async-start | bytes 4456448 | tf_op jit(solution)/shard_map/all_gather | solution.py:91
  51.9 8.2 %copy-start.5 = (s32[4,3]{1,0:T(4,128)S(1)}, s32[4,3]{1,0:T(4,128)}, u32[]{:S(2)}) copy-start(s32[4,3]{1,0:T(4,128)} %param.10) | copy-start | bytes 148
  51.9 8.6 %copy-start.6 = (s32[4]{0:T(128)S(1)}, s32[4]{0:T(128)}, u32[]{:S(2)}) copy-start(s32[4]{0:T(128)} %param.17) | copy-start | bytes 52
  51.9 8.9 %copy-start.3 = (bf16[4,8192]{1,0:T(4,128)(2,1)S(1)}, bf16[4,8192]{1,0:T(4,128)(2,1)}, u32[]{:S(2)}) copy-start(bf16[4,8192]{1,0:T(4,128)(2,1)} %param.14) | copy-start | bytes 196612
  51.9 16.7 %copy-start.8 = (u32[128]{0:T(128)S(1)}, u32[128]{0:T(128)}, u32[]{:S(2)}) copy-start(u32[128]{0:T(128)} %constant.81) | copy-start | bytes 1540
  51.9 18.2 %copy-start.7 = (s32[4]{0:T(128)S(1)}, s32[4]{0:T(128)}, u32[]{:S(2)}) copy-start(s32[4]{0:T(128)} %param.16) | copy-start | bytes 52
  60.0 159.2 %all-reduce.11.cloned.1.call-start = ((), (), s32[]{:S(2)}) async-start(), calls=%async_computation.8 | async-start | bytes 131072 | tf_op jit(solution)/shard_map/psum | solution.py:155
  70.1 2.7 copy-start.2
  73.1 2.3 copy-start
  141.2 2.0 copy-start.1
  220.8 14.6 %all-to-all-start = ((f32[4,4,2048]{2,1,0:T(4,128)}), f32[4,4,2048]{2,1,0:T(4,128)S(1)}, u32[]{:S(2)}, u32[]{:S(2)}) async-start(f32[4,4,2048]{2,1,0:T(4,128)} %all_to_all.61), calls=%async_computation | async-start | bytes 262144 | tf_op jit(solution)/shard_map/all_to_all | solution.py:156
  230.2 114.1 %all-reduce.13.cloned.1.call-start = ((), (), s32[]{:S(2)}) async-start(), calls=%async_computation.9 | async-start | bytes 131072 | tf_op jit(solution)/shard_map/psum | solution.py:155
  276.9 191.6 %all-reduce.15.cloned.1.call-start = ((), (), s32[]{:S(2)}) async-start(), calls=%async_computation.10 | async-start | bytes 131072 | tf_op jit(solution)/shard_map/psum | solution.py:155
  401.0 191.6 %all-reduce.17.cloned.1.call-start = ((), (), s32[]{:S(2)}) async-start(), calls=%async_computation.11 | async-start | bytes 131072 | tf_op jit(solution)/shard_map/psum | solution.py:155
  525.2 183.9 %all-gather.17.cloned.1.call-start = ((), (), s32[]{:S(2)}) async-start(), calls=%async_computation.6 | async-start | bytes 20971520 | tf_op jit(solution)/shard_map/all_gather | solution.py:45
  525.9 205.6 %all-gather.15.cloned.1.call-start = ((), (), s32[]{:S(2)}) async-start(), calls=%async_computation.5 | async-start | bytes 1310720 | tf_op jit(solution)/shard_map/all_gather | solution.py:61
  592.6 14.2 %all-to-all-start.3 = ((bf16[4,4,2048]{2,1,0:T(4,128)(2,1)}), bf16[4,4,2048]{2,1,0:T(4,128)(2,1)S(1)}, u32[]{:S(2)}, u32[]{:S(2)}) async-start(bf16[4,4,2048]{2,1,0:T(4,128)(2,1)} %all-reduce.17.cloned.1.call-done), calls=%async_computation.3 | async-start | bytes 131072 | tf_op jit(solution)/shard_map/all_to_all | solution.py:156
  746.1 15.0 %copy-start.4 = (bf16[2048,2,128]{2,0,1:T(8,128)(2,1)S(1)}, bf16[2048,2,128]{2,0,1:T(8,128)(2,1)}, u32[]{:S(2)}) copy-start(bf16[2048,2,128]{2,0,1:T(8,128)(2,1)} %all-gather.15.cloned.1.call-done) | copy-start | bytes 3145732
Sparse Core Ops, SparseCore 0:
  9.7 42.1 all-gather.12
  60.2 54.8 all-gather.18
  154.1 65.0 all-reduce.10
  277.0 67.2 all-reduce.12
  401.2 67.2 all-reduce.14
  525.3 67.3 all-reduce.16
  594.3 114.7 all-gather.16
  711.3 20.1 all-gather.14
where the time goes:
time: 785 us; the launch traced here: 784 us
  waiting for transfers between devices  448 us (57%)
  blocking collectives  144 us (18%)
  matrix products  88.7 us (11%)
  local copies, waits for them, and re-layouts  35.4 us (5%)
  other arithmetic  32.6 us (4%)
  starting transfers between devices  19.2 us (2%)
  between operations  15.3 us (2%)
    psum x4, waiting for transfers between devices, body(): lax.psum(partial_out.astype(jnp.bfloat16), 'tensor').astype(jnp.float32)  264 us
    all_gather x1, waiting for transfers between devices, body(): query_piece = lax.all_gather(w_query, 'shard', axis=0, tiled=True)  101 us
    unnamed x4, blocking collectives  56.1 us
    all_gather x1, waiting for transfers between devices, body(): keyval_piece = lax.all_gather(w_keyval, 'shard', axis=0, tiled=True)  38.8 us
    all_gather x4, blocking collectives, body(): row_block = lax.all_gather(normed, 'shard', axis=0, tiled=True)  32.1 us
    all_to_all x2, blocking collectives, body(): lax.all_to_all(head_total, 'shard', split_axis=0, concat_axis=1, tiled=True)  28.7 us
    all_gather x4, blocking collectives, body(): context_block = lax.all_gather(row_context, 'shard', axis=0, tiled=True)  27.5 us
    all_gather x1, waiting for transfers between devices, body(): lax.all_gather(keyvals, ('group', 'shard'), axis=0, tiled=True)  24.8 us
  transfers between devices with their start and end apart: 10, of which 10 were waited for; matrix products, arithmetic and copies ran while one was open for 4% of the time, Pallas kernels for 0%

commit v1 on v0

v1 whole, which is shorter than its diff:
```python
import jax
import jax.numpy as jnp
from jax import lax
from jax.experimental import pallas as pl
from jax.experimental.pallas import tpu as pltpu
from jax.sharding import PartitionSpec as P

HD = 128
CACHE = 2048
STEPS = 4


EPSILON = 1e-05


def normalize(states):
    values = states.astype(jnp.float32)
    return (values * lax.rsqrt(jnp.mean(values * values, axis=-1, keepdims=True) + EPSILON)).astype(
        jnp.bfloat16
    )


MESH = pl.DeviceIdType.MESH
NS = 4
NT = 8
WIN = 1152


def decode_kernel(
    meta_ref,
    ds_ref,
    wq_hbm,
    wkv_hbm,
    wo_hbm,
    cache_hbm,
    win_hbm,
    out_ref,
    wq,
    wkv,
    wo,
    cache,
    win,
    a_recv,
    xu,
    xu_send,
    state,
    b_send,
    b_recv,
    qs,
    fkv,
    c_send,
    c_recv,
    d_send,
    d_recv,
    e_send,
    e_recv,
    lsem,
    a_ss,
    a_rs,
    b_ss,
    b_rs,
    c_ss,
    c_rs,
    d_ss,
    d_rs,
    x_ss,
    x_rs,
    e_ss,
    e_rs,
):
    f32, bf16 = jnp.float32, jnp.bfloat16
    s = lax.axis_index("shard")
    t = lax.axis_index("tensor")
    rows = ds_ref.shape[1]
    dblk = wq.shape[0]
    qcols = wq.shape[1]
    piece = dblk // NT
    heads = qcols // HD
    width = NS * dblk

    loads = [
        pltpu.make_async_copy(a, b, lsem.at[i])
        for i, (a, b) in enumerate(
            [(wq_hbm, wq), (wkv_hbm, wkv), (wo_hbm, wo), (cache_hbm, cache), (win_hbm, win)]
        )
    ]
    for load in loads:
        load.start()

    def shard_peer(d):
        return lax.rem(s + d, NS)

    def tensor_peer(d):
        return lax.rem(t + d, NT)

    def remote(src, dst, ssem, rsem, **where):
        return pltpu.make_async_remote_copy(
            src_ref=src,
            dst_ref=dst,
            send_sem=ssem,
            recv_sem=rsem,
            device_id=where,
            device_id_type=MESH,
        )

    barrier = pltpu.get_barrier_semaphore()
    for d in range(1, NS):
        pl.semaphore_signal(barrier, inc=1, device_id={"shard": shard_peer(d)}, device_id_type=MESH)
    for d in range(1, NT):
        pl.semaphore_signal(
            barrier, inc=1, device_id={"tensor": tensor_peer(d)}, device_id_type=MESH
        )
    pl.semaphore_wait(barrier, NS - 1 + NT - 1)

    a_copies = []
    for d in range(1, NS):
        p = shard_peer(d)
        c = remote(ds_ref.at[p], a_recv.at[s], a_ss.at[d - 1], a_rs.at[s], shard=p)
        c.start()
        a_copies.append(c)
    a_recv[s] = ds_ref[s]
    fkv[...] = jnp.zeros_like(fkv)

    for d in range(1, NS):
        src = lax.rem(s + NS - d, NS)
        remote(ds_ref.at[s], a_recv.at[src], a_ss.at[d - 1], a_rs.at[src], shard=src).wait_recv()
    for c in a_copies:
        c.wait_send()
    x0 = jnp.concatenate([a_recv[i] for i in range(NS)], axis=0)
    for i in range(NT):
        xu[i, :, :piece] = x0[:, i * piece : (i + 1) * piece].astype(bf16)
    mine = pl.ds(pl.multiple_of(t * piece, piece), piece)
    state[...] = jnp.concatenate([a_recv[i, :, mine] for i in range(NS)], axis=0)

    for load in loads:
        load.wait()

    cpos = lax.broadcasted_iota(jnp.int32, (heads, cache.shape[1]), 1)
    wpos = lax.broadcasted_iota(jnp.int32, (heads, WIN), 1)
    wvalid = (wpos >= meta_ref[2 * rows : 2 * rows + 1, :1]) & (
        wpos < meta_ref[2 * rows + 1 : 2 * rows + 2, :1]
    )
    fresh_row = [meta_ref[r : r + 1, :] > 0 for r in range(rows)]
    inv_root = HD ** (-0.5)
    nt = (((1,), (1,)), ((), ()))

    def step(k, carry):
        acc = jnp.zeros((NS * rows, qcols + 2 * HD), f32)
        square = jnp.zeros((NS * rows, 1), f32)
        acc_q = jnp.zeros((NS * rows, qcols), f32)
        acc_kv = jnp.zeros((NS * rows, 2 * HD), f32)
        for i in range(NT):
            xi = xu[i, :, :piece]
            acc_q += jnp.dot(xi, wq[i * piece : (i + 1) * piece, :], preferred_element_type=f32)
            acc_kv += jnp.dot(xi, wkv[i * piece : (i + 1) * piece, :], preferred_element_type=f32)
            xf = xi.astype(f32)
            square += jnp.sum(xf * xf, axis=1, keepdims=True)
        squares = jnp.broadcast_to(square, (NS * rows, HD))
        for i in range(NS):
            b_send[i, :, :qcols] = acc_q[i * rows : (i + 1) * rows]
            b_send[i, :, qcols : qcols + 2 * HD] = acc_kv[i * rows : (i + 1) * rows]
            b_send[i, :, qcols + 2 * HD :] = squares[i * rows : (i + 1) * rows]
        copies = []
        for d in range(1, NS):
            p = shard_peer(d)
            c = remote(b_send.at[p], b_recv.at[s], b_ss.at[d - 1], b_rs.at[s], shard=p)
            c.start()
            copies.append(c)
        total = b_send[s]
        for d in range(1, NS):
            src = lax.rem(s + NS - d, NS)
            remote(
                b_send.at[s], b_recv.at[src], b_ss.at[d - 1], b_rs.at[src], shard=src
            ).wait_recv()
            total = total + b_recv[src]
        for c in copies:
            c.wait_send()
        scale = lax.rsqrt(total[:, qcols + 2 * HD : qcols + 2 * HD + 1] / width + EPSILON)
        fresh = (total[:, : qcols + 2 * HD] * scale).astype(bf16).astype(f32)
        fkv[k] = fresh[:, qcols:]
        for r in range(rows):
            for h in range(heads):
                qs[r, h : h + 1, :] = fresh[r : r + 1, h * HD : (h + 1) * HD]

        q_new = jnp.zeros((heads, HD), f32)
        for r in range(rows):
            q_new = jnp.where(fresh_row[r], qs[r], q_new)
        w_scores = (
            lax.dot_general(q_new.astype(bf16), win[:, :HD], nt, preferred_element_type=f32)
            * inv_root
        )
        w_scores = jnp.where(wvalid, w_scores, -1e30)
        w_high = jnp.max(w_scores, axis=1, keepdims=True)
        w_exp = jnp.where(wvalid, jnp.exp(w_scores - w_high), 0.0)
        w_total = jnp.sum(w_exp, axis=1, keepdims=True)
        w_mixed = jnp.dot(w_exp.astype(bf16), win[:, HD:], preferred_element_type=f32)
        for r in range(rows):
            q = qs[r]
            valid = cpos < meta_ref[rows + r : rows + r + 1, :1]
            scores = (
                lax.dot_general(q.astype(bf16), cache[r, :, :HD], nt, preferred_element_type=f32)
                * inv_root
            )
            scores = jnp.where(valid, scores, -1e30)
            high = jnp.max(scores, axis=1, keepdims=True)
            weights = jnp.where(valid, jnp.exp(scores - high), 0.0)
            summed = jnp.sum(weights, axis=1, keepdims=True)
            mixed = jnp.dot(weights.astype(bf16), cache[r, :, HD:], preferred_element_type=f32)
            high = jnp.where(fresh_row[r][:, :1], w_high, high)
            summed = jnp.where(fresh_row[r][:, :1], w_total, summed)
            mixed = jnp.where(fresh_row[r], w_mixed, mixed)
            news = []
            top = high
            for j in range(STEPS):
                new = jnp.sum(q * fkv[j, r : r + 1, :HD], axis=1, keepdims=True) * inv_root
                new = jnp.where(j <= k, new, -1e30)
                news.append(new)
                top = jnp.maximum(top, new)
            rescale = jnp.exp(high - top)
            summed = summed * rescale
            mixed = mixed * rescale
            for j in range(STEPS):
                weight = jnp.where(j <= k, jnp.exp(news[j] - top), 0.0)
                summed = summed + weight
                mixed = mixed + weight.astype(bf16).astype(f32) * fkv[j, r : r + 1, HD:]
            context = (mixed / summed).astype(bf16).astype(f32)
            for h in range(heads):
                c_send[r : r + 1, h * HD : (h + 1) * HD] = context[h : h + 1]

        copies = []
        for d in range(1, NS):
            p = shard_peer(d)
            c = remote(c_send, c_recv.at[s], c_ss.at[d - 1], c_rs.at[s], shard=p)
            c.start()
            copies.append(c)
        c_recv[s] = c_send[...]
        for d in range(1, NS):
            src = lax.rem(s + NS - d, NS)
            remote(c_send, c_recv.at[src], c_ss.at[d - 1], c_rs.at[src], shard=src).wait_recv()
        for c in copies:
            c.wait_send()
        block = jnp.concatenate([c_recv[i] for i in range(NS)], axis=0).astype(bf16)
        for i in range(NT):
            d_send[i] = jnp.dot(
                block, wo[:, i * piece : (i + 1) * piece], preferred_element_type=f32
            ).astype(bf16)

        copies = []
        for d in range(1, NT):
            p = tensor_peer(d)
            c = remote(d_send.at[p], d_recv.at[t], d_ss.at[d - 1], d_rs.at[t], tensor=p)
            c.start()
            copies.append(c)
        update = d_send[t].astype(f32)
        for d in range(1, NT):
            src = lax.rem(t + NT - d, NT)
            remote(
                d_send.at[t], d_recv.at[src], d_ss.at[d - 1], d_rs.at[src], tensor=src
            ).wait_recv()
            update = update + d_recv[src].astype(f32)
        for c in copies:
            c.wait_send()
        after = state[...] + update
        state[...] = after
        xu_send[:, :piece] = after.astype(bf16)
        xu_send[:, piece:] = update.astype(bf16)
        copies = []
        for d in range(1, NT):
            p = tensor_peer(d)
            c = remote(xu_send, xu.at[t], x_ss.at[d - 1], x_rs.at[t], tensor=p)
            c.start()
            copies.append(c)
        xu[t] = xu_send[...]
        for d in range(1, NT):
            src = lax.rem(t + NT - d, NT)
            remote(xu_send, xu.at[src], x_ss.at[d - 1], x_rs.at[src], tensor=src).wait_recv()
        for c in copies:
            c.wait_send()

        for i in range(NT):
            u = xu[i, :, piece:].astype(f32)
            for j in range(NS):
                e_send[k, j, :, i * piece : (i + 1) * piece] = u[j * rows : (j + 1) * rows]
        for d in range(1, NS):
            p = shard_peer(d)
            remote(
                e_send.at[k, p], e_recv.at[k, s], e_ss.at[k, d - 1], e_rs.at[k, s], shard=p
            ).start()
        e_recv[k, s] = e_send[k, s]
        return carry

    lax.fori_loop(0, STEPS, step, 0)

    for k in range(STEPS):
        for d in range(1, NS):
            src = lax.rem(s + NS - d, NS)
            c = remote(
                e_send.at[k, src], e_recv.at[k, src], e_ss.at[k, d - 1], e_rs.at[k, src], shard=src
            )
            c.wait_recv()
            c.wait_send()
        for i in range(NS):
            out_ref[k, :, i * dblk : (i + 1) * dblk] = e_recv[k, i].astype(bf16)


def decode(meta, decode_states, wq, wkv, wo, cache, window):
    rows, width = decode_states.shape
    dblk, qcols = wq.shape
    piece = dblk // NT
    f32, bf16 = jnp.float32, jnp.bfloat16
    states = jnp.transpose(decode_states.astype(f32).reshape(rows, NS, dblk), (1, 0, 2))
    vmem = pl.BlockSpec(memory_space=pltpu.VMEM)
    hbm = pl.BlockSpec(memory_space=pl.ANY)
    dma = pltpu.SemaphoreType.DMA
    bw = qcols + 3 * HD
    return pl.pallas_call(
        decode_kernel,
        out_shape=jax.ShapeDtypeStruct((STEPS, rows, width), bf16),
        in_specs=[vmem, vmem, hbm, hbm, hbm, hbm, hbm],
        out_specs=vmem,
        scratch_shapes=[
            pltpu.VMEM(wq.shape, bf16),
            pltpu.VMEM(wkv.shape, bf16),
            pltpu.VMEM(wo.shape, bf16),
            pltpu.VMEM(cache.shape, bf16),
            pltpu.VMEM(window.shape, bf16),
            pltpu.VMEM((NS, rows, dblk), f32),
            pltpu.VMEM((NT, NS * rows, 2 * piece), bf16),
            pltpu.VMEM((NS * rows, 2 * piece), bf16),
            pltpu.VMEM((NS * rows, piece), f32),
            pltpu.VMEM((NS, rows, bw), f32),
            pltpu.VMEM((NS, rows, bw), f32),
            pltpu.VMEM((rows, qcols // HD, HD), f32),
            pltpu.VMEM((STEPS, rows, 2 * HD), f32),
            pltpu.VMEM((rows, qcols), f32),
            pltpu.VMEM((NS, rows, qcols), f32),
            pltpu.VMEM((NT, NS * rows, piece), bf16),
            pltpu.VMEM((NT, NS * rows, piece), bf16),
            pltpu.VMEM((STEPS, NS, rows, dblk), f32),
            pltpu.VMEM((STEPS, NS, rows, dblk), f32),
            dma((5,)),
            dma((NS - 1,)),
            dma((NS,)),
            dma((NS - 1,)),
            dma((NS,)),
            dma((NS - 1,)),
            dma((NS,)),
            dma((NT - 1,)),
            dma((NT,)),
            dma((NT - 1,)),
            dma((NT,)),
            dma((STEPS, NS - 1)),
            dma((STEPS, NS)),
        ],
        compiler_params=pltpu.CompilerParams(
            collective_id=0, has_side_effects=True, vmem_limit_bytes=50 * 1024 * 1024
        ),
        name="decode",
    )(meta, states, wq, wkv, wo, cache, window)


def body(
    prompt_states,
    prompt_lens,
    w_query,
    w_keyval,
    w_out,
    decode_states,
    kv_cache,
    cache_len,
    row_prompt,
):
    shard_index = lax.axis_index("shard")
    group_index = lax.axis_index("group")
    d_part = w_query.shape[0]
    q_cols = w_query.shape[1]
    kv_cols = w_keyval.shape[2]
    heads_local = q_cols // HD
    kv_local = kv_cols // HD
    groups = heads_local // kv_local
    tok_local = prompt_states.shape[0]
    rows_local = decode_states.shape[0]
    inv_root = HD ** (-0.5)
    prompt_normed = normalize(prompt_states)
    query_piece = lax.all_gather(w_query, "shard", axis=0, tiled=True)
    keyval_piece = lax.all_gather(w_keyval, "shard", axis=0, tiled=True)
    amount = query_piece.shape[0]
    query_sum = jnp.dot(prompt_normed, query_piece, preferred_element_type=jnp.float32)
    keyval_sum = jnp.dot(
        prompt_normed, keyval_piece.reshape(amount, 2 * kv_cols), preferred_element_type=jnp.float32
    )
    queries = query_sum.astype(jnp.bfloat16)
    keyvals = keyval_sum.astype(jnp.bfloat16)
    keyvals = keyvals.reshape(tok_local, 2, kv_cols)
    query_heads = queries.reshape(tok_local, kv_local, groups, HD)
    group_pick = jnp.arange(prompt_lens.shape[0], dtype=jnp.int32) == group_index
    lens_mine = jnp.sum(jnp.where(group_pick[:, None], prompt_lens, 0), axis=0)
    bounds = jnp.cumsum(lens_mine)
    query_pos = shard_index * tok_local + jnp.arange(tok_local, dtype=jnp.int32)
    query_seg = jnp.sum((query_pos[:, None] >= bounds[None, :]).astype(jnp.int32), axis=1)
    piece = lax.all_gather(keyvals, "shard", axis=0, tiled=True)
    highest = jnp.full((kv_local, groups, tok_local), -1e30, jnp.float32)
    amount = piece.shape[0]
    key_pos = jnp.arange(amount, dtype=jnp.int32)
    key_seg = jnp.sum((key_pos[:, None] >= bounds[None, :]).astype(jnp.int32), axis=1)
    allowed = (query_seg[:, None] == key_seg[None, :]) & (key_pos[None, :] <= query_pos[:, None])
    keys = piece[:, 0].reshape(amount, kv_local, HD)
    values = piece[:, 1].reshape(amount, kv_local, HD)
    scores = (
        jnp.einsum("qkgd,nkd->kgqn", query_heads, keys, preferred_element_type=jnp.float32)
        * inv_root
    )
    masked = jnp.where(allowed, scores, -1e30)
    new_high = jnp.maximum(highest, jnp.max(masked, axis=-1))
    weights = jnp.where(allowed, jnp.exp(masked - new_high[..., None]), 0.0)
    totals = jnp.sum(weights, axis=-1)
    mixed = jnp.einsum(
        "kgqn,nkd->kgqd", weights.astype(jnp.bfloat16), values, preferred_element_type=jnp.float32
    )
    highest, totals, mixed = (new_high, totals, mixed)
    context = (mixed / totals[..., None]).astype(jnp.bfloat16)
    prompt_context = jnp.transpose(context, (2, 0, 1, 3)).reshape(tok_local, q_cols)
    lens_flat = prompt_lens.reshape(-1)
    kv_all = lax.all_gather(
        keyvals.reshape(tok_local, 2 * kv_cols), ("group", "shard"), axis=0, tiled=True
    )
    starts = jnp.cumsum(lens_flat) - lens_flat
    onehot = row_prompt[:, None] == jnp.arange(lens_flat.shape[0], dtype=jnp.int32)[None, :]
    is_new = jnp.any(onehot, axis=1)
    first = jnp.sum(jnp.where(onehot, starts[None, :], 0))
    count = jnp.sum(jnp.where(onehot, lens_flat[None, :], 0))
    base = jnp.minimum((first // 16) * 16, kv_all.shape[0] - WIN)
    window = lax.dynamic_slice_in_dim(kv_all, base, WIN, 0)
    bounds_new = jnp.stack([first - base, first - base + count])
    meta = jnp.concatenate([is_new.astype(jnp.int32), cache_len, bounds_new])
    meta = jnp.pad(meta, (0, 16 - meta.shape[0]))
    updates = decode(
        jnp.broadcast_to(meta[:, None], (16, HD)),
        decode_states,
        w_query,
        w_keyval.reshape(d_part, 2 * kv_cols),
        w_out,
        kv_cache.reshape(rows_local, CACHE, 2 * kv_cols),
        window,
    )
    return (prompt_context, updates)


def solution(mesh):
    in_specs = (
        P(("group", "shard"), None),
        P(),
        P("shard", "tensor"),
        P("shard", None, "tensor"),
        P("tensor", "shard"),
        P(("group", "shard"), None),
        P(("group", "shard"), None, None, "tensor"),
        P(("group", "shard")),
        P(("group", "shard")),
    )
    out_specs = (P(("group", "shard"), "tensor"), P(None, ("group", "shard"), None))
    return jax.shard_map(body, mesh=mesh, in_specs=in_specs, out_specs=out_specs, check_vma=False)
```

time: 785 us -> 319 us (0.41)
  waiting for transfers between devices: 448 us -> 110 us
  blocking collectives: 144 us -> 0 us
  Pallas kernels: 0 us -> 102 us
  matrix products: 88.7 us -> 52 us
  local copies, waits for them, and re-layouts: 35.4 us -> 13 us
  starting transfers between devices: 19.2 us -> 0.34 us
  other arithmetic: 32.6 us -> 22.8 us
    psum x4 -> x0, waiting for transfers between devices: 264 us -> none  [body(): lax.psum(partial_out.astype(jnp.bfloat16), 'tensor').astype(jnp.float32)]
    pallas_call x0 -> x1, Pallas kernels: none -> 102 us  [decode(): pl.pallas_call(decode_kernel, out_shape=jax.ShapeDtypeStruct((STEPS, rows...]
    all_gather x1, waiting for transfers between devices: 101 us -> 25.6 us  [body(): query_piece = lax.all_gather(w_query, 'shard', axis=0, tiled=True)]
    all_gather x8 -> x0, blocking collectives: 59.6 us -> none  [the longest x4 32.1 us: body(): row_block = lax.all_gather(normed, 'shard', axis=0, tiled=True)]
    unnamed x4 -> x0, blocking collectives: 56.1 us -> none
    dot_general x23 -> x0, matrix products: 37.4 us -> none  [the longest x4 11.4 us: body(): jnp.dot(context_block, w_out, preferred_element_type=jnp.float32)]
    all_to_all x2 -> x0, blocking collectives: 28.7 us -> none  [body(): lax.all_to_all(head_total, 'shard', split_axis=0, concat_axis=1, tiled=True)]
    all_to_all x2 -> x0, starting transfers between devices: 18.9 us -> none  [body(): lax.all_to_all(head_total, 'shard', split_axis=0, concat_axis=1, tiled=True)]
  transfers between devices with their start and end apart: 10 -> 4, of which waited for: 10 -> 4; matrix products, arithmetic and copies ran while one was open for 4% -> 11% of each run, Pallas kernels for 0% -> 32%
where the time goes in v1:
time: 319 us; the launch traced here: 318 us
  waiting for transfers between devices  110 us (34%)
  Pallas kernels  102 us (32%)
  matrix products  52 us (16%)
  other arithmetic  22.8 us (7%)
  between operations  17.6 us (6%)
  local copies, waits for them, and re-layouts  13 us (4%)
    pallas_call x1, Pallas kernels, decode(): pl.pallas_call(decode_kernel, out_shape=jax.ShapeDtypeStruct((STEPS, rows...  102 us
    all_gather x1, waiting for transfers between devices, body(): keyval_piece = lax.all_gather(w_keyval, 'shard', axis=0, tiled=True)  38.7 us
    all_gather x1, waiting for transfers between devices, body(): lax.all_gather(keyvals.reshape(tok_local, 2 * kv_cols), ('group', 'shard'...  38 us
    all_gather x1, waiting for transfers between devices, body(): query_piece = lax.all_gather(w_query, 'shard', axis=0, tiled=True)  25.6 us
    reduce_sum x1, other arithmetic, body(): totals = jnp.sum(weights, axis=-1)  14.9 us
    dot_general x1, matrix products, body(): jnp.dot(prompt_normed, query_piece, preferred_element_type=jnp.float32)  14.9 us
    dot_general x1, matrix products, body(): jnp.einsum('kgqn,nkd->kgqd', weights.astype(jnp.bfloat16), values, prefer...  14.8 us
    dot_general x1, matrix products, body(): jnp.einsum('qkgd,nkd->kgqn', query_heads, keys, preferred_element_type=jn...  14.6 us
  transfers between devices with their start and end apart: 4, of which 4 were waited for; matrix products, arithmetic and copies ran while one was open for 11% of the time, Pallas kernels for 32%

profile of v1, /device:TPU:1, one launch (start us, length us, event | category | flops | bytes accessed | tf_op | source)
XLA Modules:
  0.0 318.3 jit_solution(8064379570364147305)
XLA Ops:
  7.2 0.7 all-gather.5.cloned.1.call-update
  8.0 5.2 %fusion.3 = f32[512]{0:T(512)S(1)} fusion(bf16[512,8192]{1,0:T(8,128)(2,1)} %param.9), kind=kLoop, calls=%fused_computation.7 | loop fusion | flops 12582400 | bytes 8390656 | tf_op jit(solution)/shard_map/reduce_sum | solution.py:18
  13.2 38.7 %all-gather.5.cloned.1.call-done = bf16[8192,2,128]{2,1,0:T(2,128)(2,1)} async-done(((bf16[2048,2,128]{2,1,0:T(2,128)(2,1)}), bf16[8192,2,128]{2,1,0:T(2,128)(2,1)}) %all-gather.5.cloned.1.call-update) | async-done | bytes 4194320 | tf_op jit(solution)/shard_map/all_gather | solution.py:386
  51.9 7.7 %fusion.22 = bf16[512,256]{1,0:T(8,128)(2,1)} fusion(bf16[1024,8,2,128]{3,2,1,0:T(2,128)(2,1)} %bitcast.78, bf16[512,8192]{1,0:T(8,128)(2,1)} %param.9, f32[512]{0:T(512)S(1)} %add_rsqrt_fusion), kind=kOutput, calls=%fused_computation.21 | convolution fusion | flops 2160197632 | bytes 12847104 | tf_op jit(solution)/shard_map/dot_general | solution.py:389
  59.6 0.7 all-gather.9.cloned.1.call-update
  60.3 0.2 all-gather.7.cloned.1.call-start
  60.5 0.1 reshape.148
  60.6 0.1 reshape.146
  60.7 0.2 reduce-window.17
  60.9 0.7 select_reduce_fusion
  64.7 0.1 select_reduce_fusion.2
  64.8 0.2 reduce-window.16
  65.0 0.2 fusion.32
  65.9 0.1 pad_add_fusion
  65.9 0.1 copy.51
  66.1 7.7 %reshape.151.cache_hbm = bf16[4,2048,256]{2,1,0:T(8,128)(2,1)} reshape(bf16[4,2048,2,128]{3,2,1,0:T(2,128)(2,1)} %param.15) | data formatting | bytes 8388608 | tf_op jit(solution)/shard_map/reshape | solution.py:443
  73.7 0.1 convert_reduce_fusion
  73.8 0.1 convert_reduce_fusion.1
  73.9 1.0 fusion.12
  74.9 1.7 copy_bitcast_fusion.1
  76.6 38.0 %all-gather.11.cloned.1.call-done = bf16[8192,256]{1,0:T(8,128)(2,1)} async-done(((bf16[512,256]{1,0:T(8,128)(2,1)}), bf16[8192,256]{1,0:T(8,128)(2,1)}) %all-gather.11.cloned.1.call-update) | async-done | bytes 4194320 | tf_op jit(solution)/shard_map/all_gather | solution.py:424
  114.6 1.2 constant_dynamic-slice_fusion.win_hbm
  115.8 0.1 broadcast_in_dim.75.meta_ref
  115.9 102.2 %decode.1 = bf16[4,4,8192]{2,1,0:T(4,128)(2,1)S(1)} custom-call(s32[16,128]{1,0:T(8,128)S(1)} %broadcast_in_dim.75.meta_ref, f32[4,4,2048]{2,1,0:T(4,128)S(1)} %convert_bitcast_fusion.ds_ref, bf16[2048,1024]{1,0:T(8,128)(2,1)} %wq_hbm.1, bf16[2048,256]{1,0:T(8,128)(2,1)S(1)} %bitcast.71, bf16[1024,2048]{1,0:T(8,128)(2,1)} %wo_hbm.1, ...), custom_call_target="tpu_custom_call" | custom-call | tf_op jit(solution)/shard_map/decode/pallas_call | solution.py:316
  218.1 25.6 %all-gather.9.cloned.1.call-done = bf16[8192,1024]{1,0:T(8,128)(2,1)} async-done(((bf16[2048,1024]{1,0:T(8,128)(2,1)}), bf16[8192,1024]{1,0:T(8,128)(2,1)}) %all-gather.9.cloned.1.call-update) | async-done | bytes 16777232 | tf_op jit(solution)/shard_map/all_gather | solution.py:385
  243.7 14.9 %fusion.19 = bf16[64,8,8,128]{3,2,1,0:T(8,128)(2,1)S(1)} fusion(bf16[8192,1024]{1,0:T(8,128)(2,1)} %all-gather.9.cloned.1.call-done, bf16[512,8192]{1,0:T(8,128)(2,1)} %param.9, f32[512]{0:T(512)S(1)} %add_rsqrt_fusion), kind=kOutput, calls=%fused_computation.20 | convolution fusion | flops 8603041792 | bytes 26216448 | tf_op jit(solution)/shard_map/dot_general | solution.py:388
  258.6 6.7 %all-gather.7.cloned.1.call-done = bf16[2048,2,128]{2,0,1:T(8,128)(2,1)} async-done(((bf16[512,2,128]{2,0,1:T(8,128)(2,1)}), bf16[2048,2,128]{2,0,1:T(8,128)(2,1)}) %all-gather.7.cloned.1.call-update) | async-done | bytes 1048592 | tf_op jit(solution)/shard_map/all_gather | solution.py:401
  265.3 14.6 %fusion = (f32[8,512]{1,0:T(8,128)S(1)}, f32[2048,512,8]{1,0,2:T(8,128)}) fusion(pred[512,2048]{0,1:T(8,128)(4,1)S(1)} %fusion.12, bf16[64,8,8,128]{3,2,1,0:T(8,128)(2,1)S(1)} %fusion.19, bf16[2048,2,128]{2,0,1:T(8,128)(2,1)} %all-gather.7.cloned.1.call-done), kind=kOutput, calls=%fused_computation.2 | convolution fusion | flops 2172645376 | bytes 36192256 | tf_op jit(solution)/shard_map/qkgd,nkd->kgqn/dot_general | solution.py:410
  279.9 14.9 %fusion.1 = f32[8,512]{1,0:T(8,128)S(1)} fusion(f32[2048,512,8]{1,0,2:T(8,128)} %get-tuple-element.11, f32[8,512]{1,0:T(8,128)S(1)} %broadcast_maximum_fusion, pred[512,2048]{0,1:T(8,128)(4,1)S(1)} %fusion.12), kind=kLoop, calls=%fused_computation.3 | loop fusion | flops 41938944 | bytes 34635776 | tf_op jit(solution)/shard_map/reduce_sum | solution.py:416
  294.9 14.8 %divide_convert_fusion = bf16[8,512,128]{1,2,0:T(8,128)(2,1)S(1)} fusion(f32[8,512]{1,0:T(8,128)S(1)} %fusion.1, f32[2048,512,8]{1,0,2:T(8,128)} %get-tuple-element.11, f32[8,512]{1,0:T(8,128)S(1)} %broadcast_maximum_fusion, pred[512,2048]{0,1:T(8,128)(4,1)S(1)} %fusion.12, bf16[2048,2,128]{2,0,1:T(8,128)(2,1)S(1)} %copy-done.1), kind=kOutput, calls=%fused_computation.18 | convolution fusion | flops 2190475264 | bytes 36208640 | tf_op jit(solution)/shard_map/kgqn,nkd->kgqd/dot_general | solution.py:417
  309.7 1.3 copy.28
  311.0 0.7 copy.53
  (25 shorter events, 0.2 us)
Async XLA Ops:
  7.2 44.7 %all-gather.5.cloned.1.call-start = ((), (), s32[]{:S(2)}) async-start(), calls=%async_computation | async-start | bytes 5242880 | tf_op jit(solution)/shard_map/all_gather | solution.py:386
  7.9 52.6 %copy-start.3 = (s32[4,3]{1,0:T(4,128)S(1)}, s32[4,3]{1,0:T(4,128)}, u32[]{:S(2)}) copy-start(s32[4,3]{1,0:T(4,128)} %param.10) | copy-start | bytes 148
  7.9 53.0 %copy-start.4 = (s32[4]{0:T(128)S(1)}, s32[4]{0:T(128)}, u32[]{:S(2)}) copy-start(s32[4]{0:T(128)} %param.17) | copy-start | bytes 52
  7.9 57.9 %copy-start.5 = (s32[4]{0:T(128)S(1)}, s32[4]{0:T(128)}, u32[]{:S(2)}) copy-start(s32[4]{0:T(128)} %param.16) | copy-start | bytes 52
  7.9 58.0 %copy-start = (bf16[2048,2,128]{2,1,0:T(2,128)(2,1)S(1)}, bf16[2048,2,128]{2,1,0:T(2,128)(2,1)}, u32[]{:S(2)}) copy-start(bf16[2048,2,128]{2,1,0:T(2,128)(2,1)} %param.12) | copy-start | bytes 3145732
  7.9 106.7 %all-gather.11.cloned.1.call-start = ((), (), s32[]{:S(2)}) async-start(), calls=%async_computation.3 | async-start | bytes 4456448 | tf_op jit(solution)/shard_map/all_gather | solution.py:424
  51.9 22.1 %copy-start.2 = (bf16[4,8192]{1,0:T(4,128)(2,1)S(1)}, bf16[4,8192]{1,0:T(4,128)(2,1)}, u32[]{:S(2)}) copy-start(bf16[4,8192]{1,0:T(4,128)(2,1)} %param.14) | copy-start | bytes 196612
  59.6 184.2 %all-gather.9.cloned.1.call-start = ((), (), s32[]{:S(2)}) async-start(), calls=%async_computation.2 | async-start | bytes 20971520 | tf_op jit(solution)/shard_map/all_gather | solution.py:385
  60.3 205.0 %all-gather.7.cloned.1.call-start = ((), (), s32[]{:S(2)}) async-start(), calls=%async_computation.1 | async-start | bytes 1310720 | tf_op jit(solution)/shard_map/all_gather | solution.py:401
  279.9 15.0 %copy-start.1 = (bf16[2048,2,128]{2,0,1:T(8,128)(2,1)S(1)}, bf16[2048,2,128]{2,0,1:T(8,128)(2,1)}, u32[]{:S(2)}) copy-start(bf16[2048,2,128]{2,0,1:T(8,128)(2,1)} %all-gather.7.cloned.1.call-done) | copy-start | bytes 3145732
Sparse Core Ops, SparseCore 0:
  9.7 42.1 all-gather.4
  59.7 54.8 all-gather.10
  116.3 127.4 all-gather.8
  245.8 19.4 all-gather.6

commit v2 on v0

v2 whole, which is shorter than its diff:
```python
import functools

import jax
import jax.numpy as jnp
from jax import lax
from jax.experimental import pallas as pl
from jax.experimental.pallas import tpu as pltpu
from jax.sharding import PartitionSpec as P

HD = 128
CACHE = 2048
STEPS = 4
EPSILON = 1e-05
MESH = pl.DeviceIdType.MESH
NG = 4
NS = 4
NT = 8
MOST = 1024
QT = 256
KW = QT + MOST
INV_ROOT = HD**-0.5
LOG2E = 1.4426950408889634
TRANS = (((1,), (1,)), ((), ()))
f32 = jnp.float32
bf16 = jnp.bfloat16


def kernel(names, meta_ref, ds_ref, x_hbm, wkv_hbm, wq_hbm, wo_hbm, cache_hbm, ctx_ref, out_ref, *scratch):
    r = dict(zip(names, scratch))
    xv, wkv, wq, wo, raw, ck, cv = (r[n] for n in ("xv", "wkv", "wq", "wo", "raw", "ck", "cv"))
    kv, qh, acc_q, acc_kv, scale, bias = (r[n] for n in ("kv", "qh", "acc_q", "acc_kv", "scale", "bias"))
    a_recv, xu, xu_send, state = (r[n] for n in ("a_recv", "xu", "xu_send", "state"))
    b_send, b_recv, qs, fkv = (r[n] for n in ("b_send", "b_recv", "qs", "fkv"))
    c_send, c_recv, d_send, d_recv = (r[n] for n in ("c_send", "c_recv", "d_send", "d_recv"))
    e_send, e_recv = r["e_send"], r["e_recv"]

    g = lax.axis_index("group")
    s = lax.axis_index("shard")
    t = lax.axis_index("tensor")
    sc = s + 1 - 2 * lax.rem(s, 2)
    s2 = lax.rem(s + 2, NS)
    s3 = lax.rem(sc + 2, NS)
    tok = xv.shape[0]
    rows = ds_ref.shape[1]
    dblk, qcols = wq.shape[1:]
    piece = dblk // NT
    heads = qcols // HD
    width = NS * dblk
    quarter = dblk // NG
    half = quarter // 2

    def up(base, d, n):
        return lax.rem(base + d, n)

    def remote(src, dst, ssem, rsem, **where):
        return pltpu.make_async_remote_copy(
            src_ref=src, dst_ref=dst, send_sem=ssem, recv_sem=rsem, device_id=where, device_id_type=MESH
        )

    sent = []

    def send(src, dst, ssem, rsem, **where):
        c = remote(src, dst, ssem, rsem, **where)
        c.start()
        sent.append(c)
        return c

    def arrive(dst, ssem, rsem, **where):
        remote(dst, dst, ssem, rsem, **where).wait_recv()

    def load(a, b, i):
        c = pltpu.make_async_copy(a, b, r["lsem"].at[i])
        c.start()
        return c

    load_x = load(x_hbm, xv, 0)
    load_wkv = load(wkv_hbm, wkv.at[s], 1)
    load_wq = load(wq_hbm, wq.at[s], 2)
    load_raw = load(cache_hbm, raw, 3)
    load_wo = load(wo_hbm, wo, 4)

    barrier = pltpu.get_barrier_semaphore()
    for d in range(1, NS):
        pl.semaphore_signal(barrier, inc=1, device_id={"shard": up(s, d, NS)}, device_id_type=MESH)
    for d in range(1, NG):
        pl.semaphore_signal(barrier, inc=1, device_id={"group": up(g, d, NG)}, device_id_type=MESH)
    for d in range(1, NT):
        pl.semaphore_signal(barrier, inc=1, device_id={"tensor": up(t, d, NT)}, device_id_type=MESH)
    pl.semaphore_wait(barrier, NS - 1 + NG - 1 + NT - 1)

    def krows(blk, q):
        return wkv.at[blk, pl.ds(pl.multiple_of(q * quarter, quarter), quarter)]

    def qrows(blk, q, h):
        return wq.at[blk, pl.ds(pl.multiple_of(q * quarter + h * half, half), half)]

    q_of = [g, up(g, 2, NG), up(g, 3, NG), up(g, 1, NG)]
    ky_s, ky_r, kz_s, kz_r, kc_s, kc_r = (r[n] for n in ("ky_s", "ky_r", "kz_s", "kz_r", "kc_s", "kc_r"))
    qy_s, qy_r, qz_s, qz_r, qc_s, qc_r = (r[n] for n in ("qy_s", "qy_r", "qz_s", "qz_r", "qc_s", "qc_r"))

    for i in range(2):
        src = wkv_hbm.at[pl.ds(pl.multiple_of(q_of[i] * quarter, quarter), quarter)]
        send(src, krows(s, q_of[i]), ky_s.at[i], ky_r.at[i], shard=s2)
    send(wkv_hbm, wkv.at[s], kc_s.at[4], kc_r.at[4], shard=sc)
    for d in range(1, NS):
        p = up(s, d, NS)
        send(ds_ref.at[p], a_recv.at[s], r["a_s"].at[d - 1], r["a_r"].at[s], shard=p)
    send(wq_hbm, wq.at[s], qc_s.at[8], qc_r.at[8], shard=sc)
    a_recv[s] = ds_ref[s]
    r["fkv"][...] = jnp.zeros_like(fkv)
    kv[:MOST, :] = jnp.zeros((MOST, 2 * HD), bf16)

    def k_arrive_y(i):
        arrive(krows(s2, q_of[i]), ky_s.at[i], ky_r.at[i], shard=s2)

    def k_arrive_z(i):
        arrive(krows(s2, q_of[2 + i]), kz_s.at[i], kz_r.at[i], group=q_of[2 + i])

    def k_forward(role):
        ref = krows(s2, q_of[role])
        send(ref, ref, kc_s.at[role], kc_r.at[role], shard=sc)

    def k_forward_z():
        ref = krows(s2, g)
        send(ref, ref, kz_s.at[0], kz_r.at[0], group=up(g, 1, NG))
        send(ref, ref, kz_s.at[1], kz_r.at[1], group=up(g, 3, NG))

    def q_send_y(i):
        src = wq_hbm.at[pl.ds(pl.multiple_of(q_of[i // 2] * quarter + i % 2 * half, half), half)]
        send(src, qrows(s, q_of[i // 2], i % 2), qy_s.at[i], qy_r.at[i], shard=s2)

    def q_arrive_y(i):
        arrive(qrows(s2, q_of[i // 2], i % 2), qy_s.at[i], qy_r.at[i], shard=s2)

    def q_forward_z(h):
        ref = qrows(s2, g, h)
        send(ref, ref, qz_s.at[h], qz_r.at[h], group=up(g, 1, NG))
        send(ref, ref, qz_s.at[2 + h], qz_r.at[2 + h], group=up(g, 3, NG))

    def q_arrive_z(i):
        arrive(qrows(s2, q_of[2 + i // 2], i % 2), qz_s.at[i], qz_r.at[i], group=q_of[2 + i // 2])

    def q_forward(i):
        ref = qrows(s2, q_of[i // 2], i % 2)
        send(ref, ref, qc_s.at[i], qc_r.at[i], shard=sc)

    def q_arrive_core(i):
        arrive(qrows(s3, q_of[i // 2], i % 2), qc_s.at[i], qc_r.at[i], shard=sc)

    def x_block(blk):
        return xv[:, pl.ds(pl.multiple_of(blk * dblk, dblk), dblk)]

    def kv_block(blk, first):
        prod = jnp.dot(x_block(blk), wkv[blk], preferred_element_type=f32)
        acc_kv[...] = prod if first else acc_kv[...] + prod

    def q_block(blk, first, lo=0, hi=None):
        hi = qcols // 256 if hi is None else hi

        def part(n, c):
            cols = pl.ds(pl.multiple_of(n * 256, 256), 256)
            prod = jnp.dot(x_block(blk), wq[blk, :, cols], preferred_element_type=f32)
            acc_q[:, cols] = prod if first else acc_q[:, cols] + prod
            return c

        lax.fori_loop(lo, hi, part, 0)

    load_x.wait()

    def squares(i, c):
        part = pl.ds(pl.multiple_of(i * 32, 32), 32)
        v = xv[part, :].astype(f32)
        mean = jnp.sum(v * v, axis=1, keepdims=True) / width
        scale[part, :] = jnp.broadcast_to(lax.rsqrt(mean + EPSILON), (32, HD))
        return c

    lax.fori_loop(0, tok // 32, squares, 0)
    load_wkv.wait()
    kv_block(s, True)

    k_arrive_y(0)
    k_forward_z()
    k_forward(0)

    for d in range(1, NS):
        src = up(s, NS - d, NS)
        arrive(a_recv.at[src], r["a_s"].at[d - 1], r["a_r"].at[src], shard=src)
    x0 = jnp.concatenate([a_recv[i] for i in range(NS)], axis=0)
    for i in range(NT):
        xu[i, :, :piece] = x0[:, i * piece : (i + 1) * piece].astype(bf16)
    mine = pl.ds(pl.multiple_of(t * piece, piece), piece)
    state[...] = jnp.concatenate([a_recv[i, :, mine] for i in range(NS)], axis=0)

    load_wq.wait()
    q_block(s, True)

    k_arrive_y(1)
    k_forward(1)
    q_send_y(0)
    arrive(wkv.at[sc], kc_s.at[4], kc_r.at[4], shard=sc)
    kv_block(sc, False)
    k_arrive_z(0)
    k_forward(2)
    k_arrive_z(1)
    k_forward(3)
    kv_block(s2, False)
    for role in range(4):
        arrive(krows(s3, q_of[role]), kc_s.at[role], kc_r.at[role], shard=sc)
    kv_block(s3, False)

    def slot(gg, ss):
        return kv.at[pl.ds(pl.multiple_of(MOST + (gg * NS + ss) * tok, tok), tok)]

    both = jnp.concatenate([scale[...], scale[...]], axis=1)
    kv[pl.ds(pl.multiple_of(MOST + (g * NS + s) * tok, tok), tok), :] = (acc_kv[...] * both).astype(bf16)
    vy_s, vy_r, vz_s, vz_r, vc_s, vc_r = (r[n] for n in ("vy_s", "vy_r", "vz_s", "vz_r", "vc_s", "vc_r"))
    own = slot(g, s)
    send(own, own, vy_s.at[0], vy_r.at[0], shard=s2)
    for d in (1, 3, 2):
        send(own, own, vz_s.at[d - 1], vz_r.at[d - 1], group=up(g, d, NG))
    send(own, own, vc_s.at[0], vc_r.at[0], shard=sc)

    def decode_project():
        acc = jnp.zeros((NS * rows, qcols), f32)
        acc2 = jnp.zeros((NS * rows, 2 * HD), f32)
        square = jnp.zeros((NS * rows, 1), f32)
        for i in range(NT):
            xi = xu[i, :, :piece]
            acc += jnp.dot(xi, wq[s, i * piece : (i + 1) * piece, :], preferred_element_type=f32)
            acc2 += jnp.dot(xi, wkv[s, i * piece : (i + 1) * piece, :], preferred_element_type=f32)
            xf = xi.astype(f32)
            square += jnp.sum(xf * xf, axis=1, keepdims=True)
        wide = jnp.broadcast_to(square, (NS * rows, HD))
        for i in range(NS):
            b_send[i, :, :qcols] = acc[i * rows : (i + 1) * rows]
            b_send[i, :, qcols : qcols + 2 * HD] = acc2[i * rows : (i + 1) * rows]
            b_send[i, :, qcols + 2 * HD :] = wide[i * rows : (i + 1) * rows]
        copies = []
        for d in range(1, NS):
            p = up(s, d, NS)
            c = remote(b_send.at[p], b_recv.at[s], r["b_s"].at[d - 1], r["b_r"].at[s], shard=p)
            c.start()
            copies.append(c)
        return copies

    b_copies = decode_project()

    load_raw.wait()
    out_i = lax.broadcasted_iota(jnp.int32, (256, 256), 0)
    in_i = lax.broadcasted_iota(jnp.int32, (256, 256), 1)
    want = jnp.where(out_i < 128, 2 * out_i, 2 * (out_i - 128) + 1)
    pick = (in_i == want).astype(bf16)

    def separate(i, c):
        src = pl.ds(pl.multiple_of(i * 256, 256), 256)
        dst = pl.ds(pl.multiple_of(i * 128, 128), 128)
        for row in range(0, rows, 2):
            pair = jnp.concatenate([raw[row, src, :], raw[row + 1, src, :]], axis=1)
            split = jnp.dot(pick, pair, preferred_element_type=f32).astype(bf16)
            for j in range(2):
                ck[row + j, dst, :] = split[:128, j * HD : (j + 1) * HD]
                cv[row + j, dst, :] = split[128:, j * HD : (j + 1) * HD]
        return c

    lax.fori_loop(0, 2 * ck.shape[1] // 256, separate, 0)
    arrive(wq.at[sc], qc_s.at[8], qc_r.at[8], shard=sc)
    q_block(sc, False)

    for i in range(tok // QT):
        q_pos = s * tok + i * QT + lax.broadcasted_iota(jnp.int32, (QT, KW), 0)
        k_pos = s * tok + i * QT - MOST + lax.broadcasted_iota(jnp.int32, (QT, KW), 1)
        b0 = meta_ref[3 * rows : 3 * rows + 1, :1]
        b1 = meta_ref[3 * rows + 1 : 3 * rows + 2, :1]
        start = jnp.where(q_pos >= b1, b1, jnp.where(q_pos >= b0, b0, 0))
        bias[i] = jnp.where((k_pos >= start) & (k_pos <= q_pos), 0.0, -1e30)

    arrive(slot(g, s2), vy_s.at[0], vy_r.at[0], shard=s2)
    theirs = slot(g, s2)
    for d in (1, 3, 2):
        send(theirs, theirs, vz_s.at[2 + d], vz_r.at[2 + d], group=up(g, d, NG))
    send(theirs, theirs, vc_s.at[1], vc_r.at[1], shard=sc)
    q_send_y(1)
    for d in range(1, NG):
        ref = slot(up(g, NG - d, NG), s)
        arrive(ref, vz_s.at[d - 1], vz_r.at[d - 1], group=up(g, NG - d, NG))
        send(ref, ref, vc_s.at[1 + d], vc_r.at[1 + d], shard=sc)
    q_send_y(2)
    q_send_y(3)
    for d in range(1, NG):
        ref = slot(up(g, NG - d, NG), s2)
        arrive(ref, vz_s.at[2 + d], vz_r.at[2 + d], group=up(g, NG - d, NG))
        send(ref, ref, vc_s.at[4 + d], vc_r.at[4 + d], shard=sc)
    q_arrive_y(0)
    q_forward_z(0)
    q_forward(0)
    arrive(slot(g, sc), vc_s.at[0], vc_r.at[0], shard=sc)
    arrive(slot(g, s3), vc_s.at[1], vc_r.at[1], shard=sc)
    for d in range(1, NG):
        arrive(slot(up(g, NG - d, NG), sc), vc_s.at[1 + d], vc_r.at[1 + d], shard=sc)
        arrive(slot(up(g, NG - d, NG), s3), vc_s.at[4 + d], vc_r.at[4 + d], shard=sc)

    spots = NG * NS * tok // MOST - 1
    first = 3 * rows + 2
    at_spot = [meta_ref[first + j : first + j + 1, :1].astype(f32).astype(bf16) for j in range(spots)]
    takes = [meta_ref[row : row + 1, :1].astype(f32).astype(bf16) for row in range(rows)]

    def place(i, c):
        dst = pl.ds(pl.multiple_of(i * HD, HD), HD)
        window = jnp.zeros((HD, 2 * HD), bf16)
        for j in range(spots):
            src = pl.ds(pl.multiple_of((1 + j) * MOST + i * HD, HD), HD)
            window = window + kv[src, :] * at_spot[j]
        for row in range(rows):
            old = 1 - takes[row]
            ck[row, dst, :] = ck[row, dst, :] * old + window[:, :HD] * takes[row]
            cv[row, dst, :] = cv[row, dst, :] * old + window[:, HD:] * takes[row]
        return c

    lax.fori_loop(0, 2 * MOST // HD, place, 0)

    def attend(u, c):
        h = lax.rem(u, heads)
        i = u // heads
        part = pl.ds(pl.multiple_of(i * QT, QT), QT)
        keys = pl.ds(pl.multiple_of((g * NS + s) * tok + i * QT, QT), KW)
        scores = lax.dot_general(qh[h, part, :], kv[keys, :HD], TRANS, preferred_element_type=f32)
        scores = scores + bias[i]
        high = jnp.max(scores, axis=1, keepdims=True)
        weights = jnp.exp2((scores - high) * (INV_ROOT * LOG2E))
        summed = jnp.sum(weights, axis=1, keepdims=True)
        mixed = jnp.dot(weights.astype(bf16), kv[keys, HD:], preferred_element_type=f32)
        cols = pl.ds(pl.multiple_of(h * HD, HD), HD)
        ctx_ref[part, cols] = (mixed / summed).astype(bf16)
        return c

    def attend_units(lo, hi):
        lax.fori_loop(lo, hi, attend, 0)

    def finish_queries():
        for h in range(heads):
            qh[h] = (acc_q[:, h * HD : (h + 1) * HD] * scale[...]).astype(bf16)

    def s2_early():
        q_arrive_y(1)
        q_forward_z(1)
        q_forward(1)

    def s2_late():
        for i in (2, 3):
            q_arrive_y(i)
            q_forward(i)

    def s2_sides(h):
        for i in (h, 2 + h):
            q_arrive_z(i)
            q_forward(4 + i)

    def s3_ready():
        for i in range(8):
            q_arrive_core(i)

    units = heads * (tok // QT)
    fills = {
        (0, 0): [s2_early],
        (0, 3): [s2_late, lambda: s2_sides(0)],
        (1, 0): [lambda: s2_sides(1)],
        (1, 1): [lambda: q_block(s2, False)],
        (1, 2): [s3_ready, lambda: q_block(s3, False)],
        (1, 3): [finish_queries, lambda: attend_units(0, 1)],
        (2, 0): [lambda: attend_units(1, 3)],
        (2, 1): [lambda: attend_units(3, 5)],
        (2, 2): [lambda: attend_units(5, 7)],
        (2, 3): [lambda: attend_units(7, 9)],
        (3, 0): [lambda: attend_units(9, 11)],
        (3, 1): [lambda: attend_units(11, 13)],
        (3, 2): [lambda: attend_units(13, units)],
    }

    def fill(k, i):
        for task in fills.get((k, i), []):
            task()

    cpos = lax.broadcasted_iota(jnp.int32, (heads, ck.shape[1]), 1)
    load_wo.wait()
    e_copies = []
    for k in range(STEPS):
        total = b_send[s]
        for d in range(1, NS):
            src = up(s, NS - d, NS)
            arrive(b_recv.at[src], r["b_s"].at[d - 1], r["b_r"].at[src], shard=src)
            total = total + b_recv[src]
        for c in b_copies:
            c.wait_send()
        norm = lax.rsqrt(total[:, qcols + 2 * HD : qcols + 2 * HD + 1] / width + EPSILON)
        fresh = (total[:, : qcols + 2 * HD] * norm).astype(bf16).astype(f32)
        fkv[k] = fresh[:, qcols:]
        for row in range(rows):
            for h in range(heads):
                qs[row, h : h + 1, :] = fresh[row : row + 1, h * HD : (h + 1) * HD]
        for row in range(rows):
            q = qs[row]
            valid = (cpos >= meta_ref[rows + row : rows + row + 1, :1]) & (
                cpos < meta_ref[2 * rows + row : 2 * rows + row + 1, :1]
            )
            scores = lax.dot_general(q.astype(bf16), ck[row], TRANS, preferred_element_type=f32) * INV_ROOT
            scores = jnp.where(valid, scores, -1e30)
            top = jnp.max(scores, axis=1, keepdims=True)
            news = []
            for j in range(k + 1):
                new = jnp.sum(q * fkv[j, row : row + 1, :HD], axis=1, keepdims=True) * INV_ROOT
                news.append(new)
                top = jnp.maximum(top, new)
            weights = jnp.where(valid, jnp.exp(scores - top), 0.0)
            summed = jnp.sum(weights, axis=1, keepdims=True)
            mixed = jnp.dot(weights.astype(bf16), cv[row], preferred_element_type=f32)
            for j in range(k + 1):
                weight = jnp.exp(news[j] - top)
                summed = summed + weight
                mixed = mixed + weight.astype(bf16).astype(f32) * fkv[j, row : row + 1, HD:]
            context = (mixed / summed).astype(bf16).astype(f32)
            for h in range(heads):
                c_send[row : row + 1, h * HD : (h + 1) * HD] = context[h : h + 1]

        copies = []
        for d in range(1, NS):
            p = up(s, d, NS)
            c = remote(c_send, c_recv.at[s], r["c_s"].at[d - 1], r["c_r"].at[s], shard=p)
            c.start()
            copies.append(c)
        c_recv[s] = c_send[...]
        fill(k, 0)
        for d in range(1, NS):
            src = up(s, NS - d, NS)
            arrive(c_recv.at[src], r["c_s"].at[d - 1], r["c_r"].at[src], shard=src)
        for c in copies:
            c.wait_send()
        block = jnp.concatenate([c_recv[i] for i in range(NS)], axis=0).astype(bf16)
        for i in range(NT):
            d_send[i] = jnp.dot(block, wo[:, i * piece : (i + 1) * piece], preferred_element_type=f32).astype(bf16)

        copies = []
        for d in range(1, NT):
            p = up(t, d, NT)
            c = remote(d_send.at[p], d_recv.at[t], r["d_s"].at[d - 1], r["d_r"].at[t], tensor=p)
            c.start()
            copies.append(c)
        fill(k, 1)
        update = d_send[t].astype(f32)
        for d in range(1, NT):
            src = up(t, NT - d, NT)
            arrive(d_recv.at[src], r["d_s"].at[d - 1], r["d_r"].at[src], tensor=src)
            update = update + d_recv[src].astype(f32)
        for c in copies:
            c.wait_send()
        after = state[...] + update
        state[...] = after
        xu_send[:, :piece] = after.astype(bf16)
        xu_send[:, piece:] = update.astype(bf16)
        copies = []
        for d in range(1, NT):
            p = up(t, d, NT)
            c = remote(xu_send, xu.at[t], r["x_s"].at[d - 1], r["x_r"].at[t], tensor=p)
            c.start()
            copies.append(c)
        xu[t] = xu_send[...]
        fill(k, 2)
        for d in range(1, NT):
            src = up(t, NT - d, NT)
            arrive(xu.at[src], r["x_s"].at[d - 1], r["x_r"].at[src], tensor=src)
        for c in copies:
            c.wait_send()
        if k < STEPS - 1:
            b_copies = decode_project()
        for i in range(NT):
            u = xu[i, :, piece:].astype(f32)
            for j in range(NS):
                e_send[k, j, :, i * piece : (i + 1) * piece] = u[j * rows : (j + 1) * rows]
        for d in range(1, NS):
            p = up(s, d, NS)
            send(e_send.at[k, p], e_recv.at[k, s], r["e_s"].at[k, d - 1], r["e_r"].at[k, s], shard=p)
        e_recv[k, s] = e_send[k, s]
        fill(k, 3)

    for k in range(STEPS):
        for d in range(1, NS):
            src = up(s, NS - d, NS)
            arrive(e_recv.at[k, src], r["e_s"].at[k, d - 1], r["e_r"].at[k, src], shard=src)
        for i in range(NS):
            out_ref[k, :, i * dblk : (i + 1) * dblk] = e_recv[k, i].astype(bf16)
    for c in sent:
        c.wait_send()


def layer(meta, states, x, wkv, wq, wo, cache):
    rows, dblk = states.shape[1:]
    tok, width = x.shape
    qcols = wq.shape[1]
    piece = dblk // NT
    heads = qcols // HD
    vm = pltpu.VMEM
    dma = pltpu.SemaphoreType.DMA
    bw = qcols + 3 * HD
    scratch = dict(
        xv=vm((tok, width), bf16),
        wkv=vm((NS, dblk, 2 * HD), bf16),
        wq=vm((NS, dblk, qcols), bf16),
        wo=vm(wo.shape, bf16),
        raw=vm(cache.shape, bf16),
        ck=vm((rows, CACHE, HD), bf16),
        cv=vm((rows, CACHE, HD), bf16),
        kv=vm((MOST + NG * NS * tok, 2 * HD), bf16),
        qh=vm((heads, tok, HD), bf16),
        acc_q=vm((tok, qcols), f32),
        acc_kv=vm((tok, 2 * HD), f32),
        scale=vm((tok, HD), f32),
        bias=vm((tok // QT, QT, KW), f32),
        a_recv=vm((NS, rows, dblk), f32),
        xu=vm((NT, NS * rows, 2 * piece), bf16),
        xu_send=vm((NS * rows, 2 * piece), bf16),
        state=vm((NS * rows, piece), f32),
        b_send=vm((NS, rows, bw), f32),
        b_recv=vm((NS, rows, bw), f32),
        qs=vm((rows, heads, HD), f32),
        fkv=vm((STEPS, rows, 2 * HD), f32),
        c_send=vm((rows, qcols), f32),
        c_recv=vm((NS, rows, qcols), f32),
        d_send=vm((NT, NS * rows, piece), bf16),
        d_recv=vm((NT, NS * rows, piece), bf16),
        e_send=vm((STEPS, NS, rows, dblk), f32),
        e_recv=vm((STEPS, NS, rows, dblk), f32),
        lsem=dma((5,)),
        ky_s=dma((2,)),
        ky_r=dma((2,)),
        kz_s=dma((2,)),
        kz_r=dma((2,)),
        kc_s=dma((5,)),
        kc_r=dma((5,)),
        qy_s=dma((4,)),
        qy_r=dma((4,)),
        qz_s=dma((4,)),
        qz_r=dma((4,)),
        qc_s=dma((9,)),
        qc_r=dma((9,)),
        vy_s=dma((1,)),
        vy_r=dma((1,)),
        vz_s=dma((6,)),
        vz_r=dma((6,)),
        vc_s=dma((8,)),
        vc_r=dma((8,)),
        a_s=dma((NS - 1,)),
        a_r=dma((NS,)),
        b_s=dma((NS - 1,)),
        b_r=dma((NS,)),
        c_s=dma((NS - 1,)),
        c_r=dma((NS,)),
        d_s=dma((NT - 1,)),
        d_r=dma((NT,)),
        x_s=dma((NT - 1,)),
        x_r=dma((NT,)),
        e_s=dma((STEPS, NS - 1)),
        e_r=dma((STEPS, NS)),
    )
    vmem = pl.BlockSpec(memory_space=pltpu.VMEM)
    hbm = pl.BlockSpec(memory_space=pl.ANY)
    return pl.pallas_call(
        functools.partial(kernel, tuple(scratch)),
        out_shape=(
            jax.ShapeDtypeStruct((tok, qcols), bf16),
            jax.ShapeDtypeStruct((STEPS, rows, width), bf16),
        ),
        in_specs=[vmem, vmem, hbm, hbm, hbm, hbm, hbm],
        out_specs=(vmem, vmem),
        scratch_shapes=list(scratch.values()),
        compiler_params=pltpu.CompilerParams(
            collective_id=0, has_side_effects=True, vmem_limit_bytes=62 * 1024 * 1024
        ),
        name="attention_layer",
    )(meta, states, x, wkv, wq, wo, cache)


def body(
    prompt_states,
    prompt_lens,
    w_query,
    w_keyval,
    w_out,
    decode_states,
    kv_cache,
    cache_len,
    row_prompt,
):
    group_index = lax.axis_index("group")
    dblk = w_query.shape[0]
    rows, width = decode_states.shape
    kv_cols = w_keyval.shape[2]
    tokens = NG * NS * prompt_states.shape[0]
    lens = prompt_lens.reshape(-1)
    count = lens.shape[0]
    index = jnp.arange(count, dtype=jnp.int32)
    starts = jnp.sum(jnp.where(index[None, :] < index[:, None], lens[None, :], 0), axis=1)
    onehot = row_prompt[:, None] == index[None, :]
    is_new = jnp.any(onehot, axis=1)
    first = jnp.sum(jnp.where(onehot, starts[None, :], 0))
    length = jnp.sum(jnp.where(onehot, lens[None, :], 0))
    spots = tokens // MOST - 1
    spot = jnp.minimum(first // MOST, spots - 1)
    base = spot * MOST
    low = jnp.where(is_new, first - base, 0)
    high = jnp.where(is_new, first - base + length, cache_len)
    mine = jnp.arange(prompt_lens.shape[0], dtype=jnp.int32) == group_index
    own = jnp.sum(jnp.where(mine[:, None], prompt_lens, 0), axis=0)
    bounds = jnp.stack([own[0], own[0] + own[1]])
    at_spot = (jnp.arange(spots, dtype=jnp.int32) == spot).astype(jnp.int32)
    meta = jnp.concatenate([is_new.astype(jnp.int32), low, high, bounds, at_spot])
    meta = jnp.pad(meta, (0, 24 - meta.shape[0]))
    states = jnp.transpose(decode_states.astype(f32).reshape(rows, NS, dblk), (1, 0, 2))
    return layer(
        jnp.broadcast_to(meta[:, None], (24, HD)),
        states,
        prompt_states,
        w_keyval.reshape(dblk, 2 * kv_cols),
        w_query,
        w_out,
        kv_cache.reshape(rows, 2 * CACHE, kv_cols),
    )


def solution(mesh):
    in_specs = (
        P(("group", "shard"), None),
        P(),
        P("shard", "tensor"),
        P("shard", None, "tensor"),
        P("tensor", "shard"),
        P(("group", "shard"), None),
        P(("group", "shard"), None, None, "tensor"),
        P(("group", "shard")),
        P(("group", "shard")),
    )
    out_specs = (P(("group", "shard"), "tensor"), P(None, ("group", "shard"), None))
    return jax.shard_map(body, mesh=mesh, in_specs=in_specs, out_specs=out_specs, check_vma=False)
```

time: 785 us -> 174 us (0.22)
  waiting for transfers between devices: 448 us -> 0 us
  Pallas kernels: 0 us -> 154 us
  blocking collectives: 144 us -> 0 us
  matrix products: 88.7 us -> 0 us
  other arithmetic: 32.6 us -> 5.27 us
  local copies, waits for them, and re-layouts: 35.4 us -> 9.09 us
  starting transfers between devices: 19.2 us -> 0 us
  between operations: 15.3 us -> 5.86 us
    psum x4 -> x0, waiting for transfers between devices: 264 us -> none  [body(): lax.psum(partial_out.astype(jnp.bfloat16), 'tensor').astype(jnp.float32)]
    all_gather x4 -> x0, waiting for transfers between devices: 172 us -> none  [the longest x1 101 us: body(): query_piece = lax.all_gather(w_query, 'shard', axis=0, tiled=True)]
    pallas_call x0 -> x1, Pallas kernels: none -> 154 us  [layer(): pl.pallas_call(functools.partial(kernel, tuple(scratch)), out_shape=(jax....]
    dot_general x27 -> x0, matrix products: 88.7 us -> none  [the longest x1 14.9 us: body(): jnp.dot(prompt_normed, query_piece, preferred_element_type=jnp.float32)]
    all_gather x8 -> x0, blocking collectives: 59.6 us -> none  [the longest x4 32.1 us: body(): row_block = lax.all_gather(normed, 'shard', axis=0, tiled=True)]
    unnamed x4 -> x0, blocking collectives: 56.1 us -> none
    all_to_all x2 -> x0, blocking collectives: 28.7 us -> none  [body(): lax.all_to_all(head_total, 'shard', split_axis=0, concat_axis=1, tiled=True)]
    reduce_sum x17 -> x3, other arithmetic: 22.2 us -> 2.25 us  [the longest x1 1.37 us: body(): length = jnp.sum(jnp.where(onehot, lens[None, :], 0))]
  transfers between devices with their start and end apart: 10 -> 0, of which waited for: 10 -> 0; matrix products, arithmetic and copies ran while one was open for 4% -> 0% of each run, Pallas kernels for 0% -> 0%
where the time goes in v2:
time: 174 us
  Pallas kernels  154 us (89%)
  local copies, waits for them, and re-layouts  9.09 us (5%)
  between operations  5.86 us (3%)
  other arithmetic  5.27 us (3%)
    pallas_call x1, Pallas kernels, layer(): pl.pallas_call(functools.partial(kernel, tuple(scratch)), out_shape=(jax....  154 us
    unnamed x3, local copies, waits for them, and re-layouts  6.34 us

profile of v2, /device:TPU:1, one launch (start us, length us, event | category | flops | bytes accessed | tf_op | source)
XLA Modules:
  0.0 173.8 jit_solution(11222499083990672204)
XLA Ops:
  0.6 0.8 select_reduce_fusion.1
  1.4 0.8 broadcast_in_dim.68
  2.2 0.8 fusion
  3.0 0.1 select_reduce_fusion
  3.1 1.4 select_reduce_fusion.2
  8.4 0.7 broadcast_select_fusion
  9.1 0.6 fusion.1
  11.0 0.7 concatenate.3
  11.7 0.7 broadcast_in_dim.79.meta_ref
  12.4 1.5 convert_bitcast_fusion.ds_ref
  13.9 2.3 %copy.13 = bf16[256,8,2,128]{3,1,2,0:T(8,128)(2,1)} copy(bf16[256,8,2,128]{3,2,1,0:T(2,128)(2,1)} %bitcast.11) | data formatting | bytes 2097152
  16.2 153.6 %attention_layer.1 = (bf16[512,1024]{1,0:T(8,128)(2,1)}, bf16[4,4,8192]{2,1,0:T(4,128)(2,1)}) custom-call(s32[24,128]{1,0:T(8,128)} %broadcast_in_dim.79.meta_ref, f32[4,4,2048]{2,1,0:T(4,128)} %convert_bitcast_fusion.ds_ref, bf16[512,8192]{1,0:T(8,128)(2,1)} %x_hbm.1, bf16[2048,256]{1,0:T(8,128)(2,1)} %bitcast.9, bf16[2048,1024]{1,0:T(8,128)(2,1)} %wq_hbm.1, ...), custom_call_target="tpu_custom_call" | custom-call | tf_op jit(solution)/shard_map/attention_layer/pallas_call | solution.py:565
  169.8 2.3 %copy.16 = bf16[512,1024]{1,0:T(8,128)(2,1)} copy(bf16[512,1024]{1,0:T(8,128)(2,1)} %get-tuple-element.10) | data formatting | bytes 2097152
  172.0 1.7 %copy.17 = bf16[4,4,8192]{2,1,0:T(4,128)(2,1)} copy(bf16[4,4,8192]{2,1,0:T(4,128)(2,1)} %get-tuple-element.11) | data formatting | bytes 524288
  (4 shorter events, 0.0 us)

commit v3 on v2

--- a/solution.py
+++ b/solution.py
@@ -25,7 +25,7 @@
 bf16 = jnp.bfloat16
 
 
-def kernel(names, meta_ref, ds_ref, x_hbm, wkv_hbm, wq_hbm, wo_hbm, cache_hbm, ctx_ref, out_ref, *scratch):
+def kernel(names, lens_ref, rowp_ref, clen_ref, ds_ref, x_hbm, wkv_hbm, wq_hbm, wo_hbm, cache_hbm, ctx_ref, out_ref, *scratch):
     r = dict(zip(names, scratch))
     xv, wkv, wq, wo, raw, ck, cv = (r[n] for n in ("xv", "wkv", "wq", "wo", "raw", "ck", "cv"))
     kv, qh, acc_q, acc_kv, scale, bias = (r[n] for n in ("kv", "qh", "acc_q", "acc_kv", "scale", "bias"))
@@ -41,7 +41,7 @@
     s2 = lax.rem(s + 2, NS)
     s3 = lax.rem(sc + 2, NS)
     tok = xv.shape[0]
-    rows = ds_ref.shape[1]
+    rows = ds_ref.shape[0]
     dblk, qcols = wq.shape[1:]
     piece = dblk // NT
     heads = qcols // HD
@@ -73,11 +73,9 @@
         c.start()
         return c
 
+    load_wkv = load(wkv_hbm, r["kraw"], 1)
     load_x = load(x_hbm, xv, 0)
-    load_wkv = load(wkv_hbm, wkv.at[s], 1)
     load_wq = load(wq_hbm, wq.at[s], 2)
-    load_raw = load(cache_hbm, raw, 3)
-    load_wo = load(wo_hbm, wo, 4)
 
     barrier = pltpu.get_barrier_semaphore()
     for d in range(1, NS):
@@ -86,6 +84,50 @@
         pl.semaphore_signal(barrier, inc=1, device_id={"group": up(g, d, NG)}, device_id_type=MESH)
     for d in range(1, NT):
         pl.semaphore_signal(barrier, inc=1, device_id={"tensor": up(t, d, NT)}, device_id_type=MESH)
+
+    begin = jnp.int32(0)
+    prompts = NG * lens_ref.shape[1]
+    starts = [jnp.int32(0)] * rows
+    sizes = [jnp.int32(0)] * rows
+    for i in range(prompts):
+        here = lens_ref[i // lens_ref.shape[1], i % lens_ref.shape[1]]
+        for row in range(rows):
+            hit = (rowp_ref[row] == i).astype(jnp.int32)
+            starts[row] = starts[row] + hit * begin
+            sizes[row] = sizes[row] + hit * here
+        begin = begin + here
+    b0 = lens_ref[g, 0]
+    b1 = b0 + lens_ref[g, 1]
+    is_new = [(rowp_ref[row] < prompts).astype(jnp.int32) for row in range(rows)]
+    spots = NG * NS * tok // MOST - 1
+    begin = sum(starts)
+    spot = jnp.minimum(begin // MOST, spots - 1)
+    low = [is_new[row] * (starts[row] - spot * MOST) for row in range(rows)]
+    high = [low[row] + is_new[row] * sizes[row] + (1 - is_new[row]) * clen_ref[row] for row in range(rows)]
+
+    out_i = lax.broadcasted_iota(jnp.int32, (256, 256), 0)
+    in_i = lax.broadcasted_iota(jnp.int32, (256, 256), 1)
+    want = jnp.where(out_i < 128, 2 * out_i, 2 * (out_i - 128) + 1)
+    pick = (in_i == want).astype(bf16)
+
+    load_wkv.wait()
+
+    def separate_weights(i, c):
+        pair = jnp.concatenate(
+            [r["kraw"][pl.ds(pl.multiple_of((2 * i + j) * 256, 256), 256), :] for j in range(2)], axis=1
+        )
+        split = jnp.dot(pick, pair, preferred_element_type=f32).astype(bf16)
+        for j in range(2):
+            dst = pl.ds(pl.multiple_of((2 * i + j) * 128, 128), 128)
+            wkv[s, dst, :] = jnp.concatenate(
+                [split[:128, j * HD : (j + 1) * HD], split[128:, j * HD : (j + 1) * HD]], axis=1
+            )
+        return c
+
+    lax.fori_loop(0, dblk // 256, separate_weights, 0)
+    ds = r["ds"]
+    for i in range(NS):
+        ds[i] = ds_ref[:, i * dblk : (i + 1) * dblk].astype(f32)
     pl.semaphore_wait(barrier, NS - 1 + NG - 1 + NT - 1)
 
     def krows(blk, q):
@@ -99,14 +141,13 @@
     qy_s, qy_r, qz_s, qz_r, qc_s, qc_r = (r[n] for n in ("qy_s", "qy_r", "qz_s", "qz_r", "qc_s", "qc_r"))
 
     for i in range(2):
-        src = wkv_hbm.at[pl.ds(pl.multiple_of(q_of[i] * quarter, quarter), quarter)]
-        send(src, krows(s, q_of[i]), ky_s.at[i], ky_r.at[i], shard=s2)
-    send(wkv_hbm, wkv.at[s], kc_s.at[4], kc_r.at[4], shard=sc)
+        send(krows(s, q_of[i]), krows(s, q_of[i]), ky_s.at[i], ky_r.at[i], shard=s2)
+    send(wkv.at[s], wkv.at[s], kc_s.at[4], kc_r.at[4], shard=sc)
     for d in range(1, NS):
         p = up(s, d, NS)
-        send(ds_ref.at[p], a_recv.at[s], r["a_s"].at[d - 1], r["a_r"].at[s], shard=p)
+        send(ds.at[p], a_recv.at[s], r["a_s"].at[d - 1], r["a_r"].at[s], shard=p)
     send(wq_hbm, wq.at[s], qc_s.at[8], qc_r.at[8], shard=sc)
-    a_recv[s] = ds_ref[s]
+    a_recv[s] = ds[s]
     r["fkv"][...] = jnp.zeros_like(fkv)
     kv[:MOST, :] = jnp.zeros((MOST, 2 * HD), bf16)
 
@@ -126,11 +167,18 @@
         send(ref, ref, kz_s.at[1], kz_r.at[1], group=up(g, 3, NG))
 
     def q_send_y(i):
-        src = wq_hbm.at[pl.ds(pl.multiple_of(q_of[i // 2] * quarter + i % 2 * half, half), half)]
-        send(src, qrows(s, q_of[i // 2], i % 2), qy_s.at[i], qy_r.at[i], shard=s2)
+        ref = qrows(s, g, i)
+        send(ref, ref, qy_s.at[i], qy_r.at[i], shard=s2)
 
     def q_arrive_y(i):
-        arrive(qrows(s2, q_of[i // 2], i % 2), qy_s.at[i], qy_r.at[i], shard=s2)
+        arrive(qrows(s2, g, i), qy_s.at[i], qy_r.at[i], shard=s2)
+
+    def q_second(h):
+        ref = qrows(s2, q_of[2 + h], h)
+        send(ref, ref, qz_s.at[4 + h], qz_r.at[4 + h], group=up(g, 1 + 2 * h, NG))
+
+    def q_arrive_second(h):
+        arrive(qrows(s2, q_of[1], h), qz_s.at[4 + h], qz_r.at[4 + h], group=q_of[2 + h])
 
     def q_forward_z(h):
         ref = qrows(s2, g, h)
@@ -166,6 +214,8 @@
         lax.fori_loop(lo, hi, part, 0)
 
     load_x.wait()
+    load_raw = load(cache_hbm, raw, 3)
+    load_wo = load(wo_hbm, wo, 4)
 
     def squares(i, c):
         part = pl.ds(pl.multiple_of(i * 32, 32), 32)
@@ -175,7 +225,6 @@
         return c
 
     lax.fori_loop(0, tok // 32, squares, 0)
-    load_wkv.wait()
     kv_block(s, True)
 
     k_arrive_y(0)
@@ -187,7 +236,7 @@
         arrive(a_recv.at[src], r["a_s"].at[d - 1], r["a_r"].at[src], shard=src)
     x0 = jnp.concatenate([a_recv[i] for i in range(NS)], axis=0)
     for i in range(NT):
-        xu[i, :, :piece] = x0[:, i * piece : (i + 1) * piece].astype(bf16)
+        xu[i] = x0[:, i * piece : (i + 1) * piece].astype(bf16)
     mine = pl.ds(pl.multiple_of(t * piece, piece), piece)
     state[...] = jnp.concatenate([a_recv[i, :, mine] for i in range(NS)], axis=0)
 
@@ -196,7 +245,6 @@
 
     k_arrive_y(1)
     k_forward(1)
-    q_send_y(0)
     arrive(wkv.at[sc], kc_s.at[4], kc_r.at[4], shard=sc)
     kv_block(sc, False)
     k_arrive_z(0)
@@ -214,18 +262,46 @@
     both = jnp.concatenate([scale[...], scale[...]], axis=1)
     kv[pl.ds(pl.multiple_of(MOST + (g * NS + s) * tok, tok), tok), :] = (acc_kv[...] * both).astype(bf16)
     vy_s, vy_r, vz_s, vz_r, vc_s, vc_r = (r[n] for n in ("vy_s", "vy_r", "vz_s", "vz_r", "vc_s", "vc_r"))
+    below, above = up(g, 3, NG), up(g, 1, NG)
+
+    def half_slot(gg, ss, h):
+        n = tok // 2
+        return kv.at[pl.ds(pl.multiple_of(MOST + (gg * NS + ss) * tok + h * n, n), n)]
+
+    def v_core(ref, i):
+        send(ref, ref, vc_s.at[i], vc_r.at[i], shard=sc)
+
+    def v_sides(ss, i):
+        ref = slot(g, ss)
+        send(ref, ref, vz_s.at[i], vz_r.at[i], group=above)
+        send(ref, ref, vz_s.at[i + 1], vz_r.at[i + 1], group=below)
+
+    def v_pass(ss, i, core):
+        for h, (source, target) in enumerate([(below, above), (above, below)]):
+            arrive(slot(source, ss), vz_s.at[i + h], vz_r.at[i + h], group=source)
+            ref = half_slot(source, ss, h)
+            send(ref, ref, vz_s.at[i + 4 + h], vz_r.at[i + 4 + h], group=target)
+            v_core(slot(source, ss), core + h)
+
+    def v_last(ss, i, core):
+        for h, source in enumerate([below, above]):
+            ref = half_slot(up(g, 2, NG), ss, h)
+            arrive(ref, vz_s.at[i + 4 + h], vz_r.at[i + 4 + h], group=source)
+            v_core(ref, core + h)
+
     own = slot(g, s)
     send(own, own, vy_s.at[0], vy_r.at[0], shard=s2)
-    for d in (1, 3, 2):
-        send(own, own, vz_s.at[d - 1], vz_r.at[d - 1], group=up(g, d, NG))
-    send(own, own, vc_s.at[0], vc_r.at[0], shard=sc)
+    v_sides(s, 0)
+    v_core(own, 0)
+    q_send_y(0)
+    q_send_y(1)
 
     def decode_project():
         acc = jnp.zeros((NS * rows, qcols), f32)
         acc2 = jnp.zeros((NS * rows, 2 * HD), f32)
         square = jnp.zeros((NS * rows, 1), f32)
         for i in range(NT):
-            xi = xu[i, :, :piece]
+            xi = xu[i]
             acc += jnp.dot(xi, wq[s, i * piece : (i + 1) * piece, :], preferred_element_type=f32)
             acc2 += jnp.dot(xi, wkv[s, i * piece : (i + 1) * piece, :], preferred_element_type=f32)
             xf = xi.astype(f32)
@@ -246,11 +322,6 @@
     b_copies = decode_project()
 
     load_raw.wait()
-    out_i = lax.broadcasted_iota(jnp.int32, (256, 256), 0)
-    in_i = lax.broadcasted_iota(jnp.int32, (256, 256), 1)
-    want = jnp.where(out_i < 128, 2 * out_i, 2 * (out_i - 128) + 1)
-    pick = (in_i == want).astype(bf16)
-
     def separate(i, c):
         src = pl.ds(pl.multiple_of(i * 256, 256), 256)
         dst = pl.ds(pl.multiple_of(i * 128, 128), 128)
@@ -269,40 +340,32 @@
     for i in range(tok // QT):
         q_pos = s * tok + i * QT + lax.broadcasted_iota(jnp.int32, (QT, KW), 0)
         k_pos = s * tok + i * QT - MOST + lax.broadcasted_iota(jnp.int32, (QT, KW), 1)
-        b0 = meta_ref[3 * rows : 3 * rows + 1, :1]
-        b1 = meta_ref[3 * rows + 1 : 3 * rows + 2, :1]
         start = jnp.where(q_pos >= b1, b1, jnp.where(q_pos >= b0, b0, 0))
         bias[i] = jnp.where((k_pos >= start) & (k_pos <= q_pos), 0.0, -1e30)
 
     arrive(slot(g, s2), vy_s.at[0], vy_r.at[0], shard=s2)
-    theirs = slot(g, s2)
-    for d in (1, 3, 2):
-        send(theirs, theirs, vz_s.at[2 + d], vz_r.at[2 + d], group=up(g, d, NG))
-    send(theirs, theirs, vc_s.at[1], vc_r.at[1], shard=sc)
-    q_send_y(1)
-    for d in range(1, NG):
-        ref = slot(up(g, NG - d, NG), s)
-        arrive(ref, vz_s.at[d - 1], vz_r.at[d - 1], group=up(g, NG - d, NG))
-        send(ref, ref, vc_s.at[1 + d], vc_r.at[1 + d], shard=sc)
-    q_send_y(2)
-    q_send_y(3)
-    for d in range(1, NG):
-        ref = slot(up(g, NG - d, NG), s2)
-        arrive(ref, vz_s.at[2 + d], vz_r.at[2 + d], group=up(g, NG - d, NG))
-        send(ref, ref, vc_s.at[4 + d], vc_r.at[4 + d], shard=sc)
+    v_sides(s2, 2)
+    v_core(slot(g, s2), 1)
+    v_pass(s, 0, 2)
+    v_pass(s2, 2, 4)
+    v_last(s, 0, 6)
+    v_last(s2, 2, 8)
+    for i, ref in enumerate(
+        [slot(g, sc), slot(g, s3)]
+        + [slot(gg, ss) for ss in (sc, s3) for gg in (below, above)]
+        + [half_slot(up(g, 2, NG), ss, h) for ss in (sc, s3) for h in range(2)]
+    ):
+        arrive(ref, vc_s.at[i], vc_r.at[i], shard=sc)
     q_arrive_y(0)
     q_forward_z(0)
     q_forward(0)
-    arrive(slot(g, sc), vc_s.at[0], vc_r.at[0], shard=sc)
-    arrive(slot(g, s3), vc_s.at[1], vc_r.at[1], shard=sc)
-    for d in range(1, NG):
-        arrive(slot(up(g, NG - d, NG), sc), vc_s.at[1 + d], vc_r.at[1 + d], shard=sc)
-        arrive(slot(up(g, NG - d, NG), s3), vc_s.at[4 + d], vc_r.at[4 + d], shard=sc)
-
-    spots = NG * NS * tok // MOST - 1
-    first = 3 * rows + 2
-    at_spot = [meta_ref[first + j : first + j + 1, :1].astype(f32).astype(bf16) for j in range(spots)]
-    takes = [meta_ref[row : row + 1, :1].astype(f32).astype(bf16) for row in range(rows)]
+
+    def splat(flag):
+        return jnp.broadcast_to(flag, (HD, HD)).astype(f32).astype(bf16)
+
+    at_spot = [splat((spot == j).astype(jnp.int32)) for j in range(spots)]
+    at_spot = [jnp.concatenate([v, v], axis=1) for v in at_spot]
+    takes = [splat(is_new[row]) for row in range(rows)]
 
     def place(i, c):
         dst = pl.ds(pl.multiple_of(i * HD, HD), HD)
@@ -345,15 +408,16 @@
         q_forward_z(1)
         q_forward(1)
 
-    def s2_late():
-        for i in (2, 3):
-            q_arrive_y(i)
-            q_forward(i)
-
     def s2_sides(h):
         for i in (h, 2 + h):
             q_arrive_z(i)
             q_forward(4 + i)
+        q_second(h)
+
+    def s2_last():
+        for h in range(2):
+            q_arrive_second(h)
+            q_forward(2 + h)
 
     def s3_ready():
         for i in range(8):
@@ -361,36 +425,69 @@
 
     units = heads * (tok // QT)
     fills = {
-        (0, 0): [s2_early],
-        (0, 3): [s2_late, lambda: s2_sides(0)],
-        (1, 0): [lambda: s2_sides(1)],
-        (1, 1): [lambda: q_block(s2, False)],
-        (1, 2): [s3_ready, lambda: q_block(s3, False)],
-        (1, 3): [finish_queries, lambda: attend_units(0, 1)],
-        (2, 0): [lambda: attend_units(1, 3)],
-        (2, 1): [lambda: attend_units(3, 5)],
-        (2, 2): [lambda: attend_units(5, 7)],
-        (2, 3): [lambda: attend_units(7, 9)],
-        (3, 0): [lambda: attend_units(9, 11)],
-        (3, 1): [lambda: attend_units(11, 13)],
-        (3, 2): [lambda: attend_units(13, units)],
+        (0, 1): [s2_early],
+        (0, 3): [lambda: s2_sides(0)],
+        (1, 1): [lambda: s2_sides(1)],
+        (2, 0): [s2_last, lambda: q_block(s2, False)],
+        (2, 1): [s3_ready, lambda: q_block(s3, False)],
+        (2, 2): [finish_queries, lambda: attend_units(0, 2)],
+        (2, 3): [lambda: attend_units(2, 5)],
+        (3, 0): [lambda: attend_units(5, 8)],
+        (3, 1): [lambda: attend_units(8, 12)],
+        (3, 2): [lambda: attend_units(12, units)],
     }
 
     def fill(k, i):
         for task in fills.get((k, i), []):
             task()
 
+    def all_shards(src_of, dst, ssem, rsem):
+        copies = []
+        for d in range(1, NS):
+            p = up(s, d, NS)
+            c = remote(src_of(p), dst, ssem.at[d - 1], rsem, shard=p)
+            c.start()
+            copies.append(c)
+        return copies
+
+    def all_tensors(src_of, dst, ssem, rsem):
+        copies = []
+        for d in (4, 6, 2, 5, 3, 7, 1):
+            p = up(t, d, NT)
+            c = remote(src_of(p), dst, ssem.at[d - 1], rsem, tensor=p)
+            c.start()
+            copies.append(c)
+        return copies
+
+    def settle(copies):
+        for c in copies:
+            c.wait_send()
+
+    u_send, u_recv = r["u_send"], r["u_recv"]
+
+    def give_update(k):
+        sent.extend(all_tensors(lambda p: u_send.at[k], u_recv.at[k, t], r["u_s"].at[k], r["u_r"].at[k, t]))
+        u_recv[k, t] = u_send[k]
+
+    def spread_update(k):
+        for d in range(1, NT):
+            src = up(t, NT - d, NT)
+            arrive(u_recv.at[k, src], r["u_s"].at[k, d - 1], r["u_r"].at[k, src], tensor=src)
+        for i in range(NT):
+            u = u_recv[k, i].astype(f32)
+            for j in range(NS):
+                e_send[k, j, :, i * piece : (i + 1) * piece] = u[j * rows : (j + 1) * rows]
+        sent.extend(all_shards(lambda p: e_send.at[k, p], e_recv.at[k, s], r["e_s"].at[k], r["e_r"].at[k, s]))
+        e_recv[k, s] = e_send[k, s]
+
     cpos = lax.broadcasted_iota(jnp.int32, (heads, ck.shape[1]), 1)
     load_wo.wait()
-    e_copies = []
     for k in range(STEPS):
         total = b_send[s]
         for d in range(1, NS):
             src = up(s, NS - d, NS)
             arrive(b_recv.at[src], r["b_s"].at[d - 1], r["b_r"].at[src], shard=src)
             total = total + b_recv[src]
-        for c in b_copies:
-            c.wait_send()
         norm = lax.rsqrt(total[:, qcols + 2 * HD : qcols + 2 * HD + 1] / width + EPSILON)
         fresh = (total[:, : qcols + 2 * HD] * norm).astype(bf16).astype(f32)
         fkv[k] = fresh[:, qcols:]
@@ -399,9 +496,7 @@
                 qs[row, h : h + 1, :] = fresh[row : row + 1, h * HD : (h + 1) * HD]
         for row in range(rows):
             q = qs[row]
-            valid = (cpos >= meta_ref[rows + row : rows + row + 1, :1]) & (
-                cpos < meta_ref[2 * rows + row : 2 * rows + row + 1, :1]
-            )
+            valid = (cpos >= low[row]) & (cpos < high[row])
             scores = lax.dot_general(q.astype(bf16), ck[row], TRANS, preferred_element_type=f32) * INV_ROOT
             scores = jnp.where(valid, scores, -1e30)
             top = jnp.max(scores, axis=1, keepdims=True)
@@ -421,64 +516,47 @@
             for h in range(heads):
                 c_send[row : row + 1, h * HD : (h + 1) * HD] = context[h : h + 1]
 
-        copies = []
-        for d in range(1, NS):
-            p = up(s, d, NS)
-            c = remote(c_send, c_recv.at[s], r["c_s"].at[d - 1], r["c_r"].at[s], shard=p)
-            c.start()
-            copies.append(c)
+        c_copies = all_shards(lambda p: c_send, c_recv.at[s], r["c_s"], r["c_r"].at[s])
         c_recv[s] = c_send[...]
+        settle(b_copies)
         fill(k, 0)
         for d in range(1, NS):
             src = up(s, NS - d, NS)
             arrive(c_recv.at[src], r["c_s"].at[d - 1], r["c_r"].at[src], shard=src)
-        for c in copies:
-            c.wait_send()
         block = jnp.concatenate([c_recv[i] for i in range(NS)], axis=0).astype(bf16)
         for i in range(NT):
             d_send[i] = jnp.dot(block, wo[:, i * piece : (i + 1) * piece], preferred_element_type=f32).astype(bf16)
 
-        copies = []
-        for d in range(1, NT):
-            p = up(t, d, NT)
-            c = remote(d_send.at[p], d_recv.at[t], r["d_s"].at[d - 1], r["d_r"].at[t], tensor=p)
-            c.start()
-            copies.append(c)
+        d_copies = all_tensors(lambda p: d_send.at[p], d_recv.at[t], r["d_s"], r["d_r"].at[t])
+        settle(c_copies)
+        if k > 0:
+            spread_update(k - 1)
         fill(k, 1)
         update = d_send[t].astype(f32)
         for d in range(1, NT):
             src = up(t, NT - d, NT)
             arrive(d_recv.at[src], r["d_s"].at[d - 1], r["d_r"].at[src], tensor=src)
             update = update + d_recv[src].astype(f32)
-        for c in copies:
-            c.wait_send()
+        u_send[k] = update.astype(bf16)
+        if k == STEPS - 1:
+            give_update(k)
+            settle(d_copies)
+            fill(k, 2)
+            spread_update(k)
+            break
         after = state[...] + update
         state[...] = after
-        xu_send[:, :piece] = after.astype(bf16)
-        xu_send[:, piece:] = update.astype(bf16)
-        copies = []
-        for d in range(1, NT):
-            p = up(t, d, NT)
-            c = remote(xu_send, xu.at[t], r["x_s"].at[d - 1], r["x_r"].at[t], tensor=p)
-            c.start()
-            copies.append(c)
+        xu_send[...] = after.astype(bf16)
+        x_copies = all_tensors(lambda p: xu_send, xu.at[t], r["x_s"], r["x_r"].at[t])
         xu[t] = xu_send[...]
+        settle(d_copies)
         fill(k, 2)
         for d in range(1, NT):
             src = up(t, NT - d, NT)
             arrive(xu.at[src], r["x_s"].at[d - 1], r["x_r"].at[src], tensor=src)
-        for c in copies:
-            c.wait_send()
-        if k < STEPS - 1:
-            b_copies = decode_project()
-        for i in range(NT):
-            u = xu[i, :, piece:].astype(f32)
-            for j in range(NS):
-                e_send[k, j, :, i * piece : (i + 1) * piece] = u[j * rows : (j + 1) * rows]
-        for d in range(1, NS):
-            p = up(s, d, NS)
-            send(e_send.at[k, p], e_recv.at[k, s], r["e_s"].at[k, d - 1], r["e_r"].at[k, s], shard=p)
-        e_recv[k, s] = e_send[k, s]
+        b_copies = decode_project()
+        settle(x_copies)
+        give_update(k)
         fill(k, 3)
 
     for k in range(STEPS):
@@ -487,14 +565,13 @@
             arrive(e_recv.at[k, src], r["e_s"].at[k, d - 1], r["e_r"].at[k, src], shard=src)
         for i in range(NS):
             out_ref[k, :, i * dblk : (i + 1) * dblk] = e_recv[k, i].astype(bf16)
-    for c in sent:
-        c.wait_send()
-
-
-def layer(meta, states, x, wkv, wq, wo, cache):
-    rows, dblk = states.shape[1:]
+    settle(sent)
+
+
+def layer(lens, row_prompt, cache_len, states, x, wkv, wq, wo, cache):
+    rows = states.shape[0]
     tok, width = x.shape
-    qcols = wq.shape[1]
+    dblk, qcols = wq.shape
     piece = dblk // NT
     heads = qcols // HD
     vm = pltpu.VMEM
@@ -514,9 +591,13 @@
         acc_kv=vm((tok, 2 * HD), f32),
         scale=vm((tok, HD), f32),
         bias=vm((tok // QT, QT, KW), f32),
+        kraw=vm((2 * dblk, HD), bf16),
+        ds=vm((NS, rows, dblk), f32),
         a_recv=vm((NS, rows, dblk), f32),
-        xu=vm((NT, NS * rows, 2 * piece), bf16),
-        xu_send=vm((NS * rows, 2 * piece), bf16),
+        xu=vm((NT, NS * rows, piece), bf16),
+        xu_send=vm((NS * rows, piece), bf16),
+        u_send=vm((STEPS, NS * rows, piece), bf16),
+        u_recv=vm((STEPS, NT, NS * rows, piece), bf16),
         state=vm((NS * rows, piece), f32),
         b_send=vm((NS, rows, bw), f32),
         b_recv=vm((NS, rows, bw), f32),
@@ -535,18 +616,18 @@
         kz_r=dma((2,)),
         kc_s=dma((5,)),
         kc_r=dma((5,)),
-        qy_s=dma((4,)),
-        qy_r=dma((4,)),
-        qz_s=dma((4,)),
-        qz_r=dma((4,)),
+        qy_s=dma((2,)),
+        qy_r=dma((2,)),
+        qz_s=dma((6,)),
+        qz_r=dma((6,)),
         qc_s=dma((9,)),
         qc_r=dma((9,)),
         vy_s=dma((1,)),
         vy_r=dma((1,)),
-        vz_s=dma((6,)),
-        vz_r=dma((6,)),
-        vc_s=dma((8,)),
-        vc_r=dma((8,)),
+        vz_s=dma((8,)),
+        vz_r=dma((8,)),
+        vc_s=dma((10,)),
+        vc_r=dma((10,)),
         a_s=dma((NS - 1,)),
         a_r=dma((NS,)),
         b_s=dma((NS - 1,)),
@@ -557,9 +638,12 @@
         d_r=dma((NT,)),
         x_s=dma((NT - 1,)),
         x_r=dma((NT,)),
+        u_s=dma((STEPS, NT - 1)),
+        u_r=dma((STEPS, NT)),
         e_s=dma((STEPS, NS - 1)),
         e_r=dma((STEPS, NS)),
     )
+    smem = pl.BlockSpec(memory_space=pltpu.SMEM)
     vmem = pl.BlockSpec(memory_space=pltpu.VMEM)
     hbm = pl.BlockSpec(memory_space=pl.ANY)
     return pl.pallas_call(
@@ -568,14 +652,14 @@
             jax.ShapeDtypeStruct((tok, qcols), bf16),
             jax.ShapeDtypeStruct((STEPS, rows, width), bf16),
         ),
-        in_specs=[vmem, vmem, hbm, hbm, hbm, hbm, hbm],
+        in_specs=[smem, smem, smem, vmem, hbm, hbm, hbm, hbm, hbm],
         out_specs=(vmem, vmem),
         scratch_shapes=list(scratch.values()),
         compiler_params=pltpu.CompilerParams(
             collective_id=0, has_side_effects=True, vmem_limit_bytes=62 * 1024 * 1024
         ),
         name="attention_layer",
-    )(meta, states, x, wkv, wq, wo, cache)
+    )(lens, row_prompt, cache_len, states, x, wkv, wq, wo, cache)
 
 
 def body(
@@ -589,39 +673,18 @@
     cache_len,
     row_prompt,
 ):
-    group_index = lax.axis_index("group")
     dblk = w_query.shape[0]
-    rows, width = decode_states.shape
-    kv_cols = w_keyval.shape[2]
-    tokens = NG * NS * prompt_states.shape[0]
-    lens = prompt_lens.reshape(-1)
-    count = lens.shape[0]
-    index = jnp.arange(count, dtype=jnp.int32)
-    starts = jnp.sum(jnp.where(index[None, :] < index[:, None], lens[None, :], 0), axis=1)
-    onehot = row_prompt[:, None] == index[None, :]
-    is_new = jnp.any(onehot, axis=1)
-    first = jnp.sum(jnp.where(onehot, starts[None, :], 0))
-    length = jnp.sum(jnp.where(onehot, lens[None, :], 0))
-    spots = tokens // MOST - 1
-    spot = jnp.minimum(first // MOST, spots - 1)
-    base = spot * MOST
-    low = jnp.where(is_new, first - base, 0)
-    high = jnp.where(is_new, first - base + length, cache_len)
-    mine = jnp.arange(prompt_lens.shape[0], dtype=jnp.int32) == group_index
-    own = jnp.sum(jnp.where(mine[:, None], prompt_lens, 0), axis=0)
-    bounds = jnp.stack([own[0], own[0] + own[1]])
-    at_spot = (jnp.arange(spots, dtype=jnp.int32) == spot).astype(jnp.int32)
-    meta = jnp.concatenate([is_new.astype(jnp.int32), low, high, bounds, at_spot])
-    meta = jnp.pad(meta, (0, 24 - meta.shape[0]))
-    states = jnp.transpose(decode_states.astype(f32).reshape(rows, NS, dblk), (1, 0, 2))
+    rows = decode_states.shape[0]
     return layer(
-        jnp.broadcast_to(meta[:, None], (24, HD)),
-        states,
+        prompt_lens,
+        row_prompt,
+        cache_len,
+        decode_states,
         prompt_states,
-        w_keyval.reshape(dblk, 2 * kv_cols),
+        w_keyval.reshape(2 * dblk, HD),
         w_query,
         w_out,
-        kv_cache.reshape(rows, 2 * CACHE, kv_cols),
+        kv_cache.reshape(rows, 2 * CACHE, HD),
     )
 
 

time: 174 us -> 142 us (0.82)
  Pallas kernels: 154 us -> 137 us
  other arithmetic: 5.27 us -> 0 us
  between operations: 5.86 us -> 0.64 us
  local copies, waits for them, and re-layouts: 9.09 us -> 4.01 us
    pallas_call x1, Pallas kernels: 154 us -> 137 us  [layer(): pl.pallas_call(functools.partial(kernel, tuple(scratch)), out_shape=(jax....]
    unnamed x3 -> x2, local copies, waits for them, and re-layouts: 6.34 us -> 4.01 us
    reduce_sum x3 -> x0, other arithmetic: 2.25 us -> none  [the longest x1 1.37 us: body(): length = jnp.sum(jnp.where(onehot, lens[None, :], 0))]
where the time goes in v3:
time: 142 us
  Pallas kernels  137 us (96%)
  local copies, waits for them, and re-layouts  4.01 us (3%)
    pallas_call x1, Pallas kernels, layer(): pl.pallas_call(functools.partial(kernel, tuple(scratch)), out_shape=(jax....  137 us
    unnamed x2, local copies, waits for them, and re-layouts  4.01 us

profile of v3, /device:TPU:1, one launch (start us, length us, event | category | flops | bytes accessed | tf_op | source)
XLA Modules:
  0.0 142.1 jit_solution(7438203646133445905)
XLA Ops:
  0.6 137.4 %attention_layer.1 = (bf16[512,1024]{1,0:T(8,128)(2,1)}, bf16[4,4,8192]{2,1,0:T(4,128)(2,1)}) custom-call(s32[4,3]{1,0:T(4,128)} %lens_ref.1, s32[4]{0:T(128)} %rowp_ref.1, s32[4]{0:T(128)} %clen_ref.1, bf16[4,8192]{1,0:T(4,128)(2,1)} %ds_ref.1, bf16[512,8192]{1,0:T(8,128)(2,1)} %x_hbm.1, bf16[4096,128]{1,0:T(8,128)(2,1)} %bitcast.3, ...), custom_call_target="tpu_custom_call" | custom-call | tf_op jit(solution)/shard_map/attention_layer/pallas_call | solution.py:649
  138.1 2.3 %copy.13 = bf16[512,1024]{1,0:T(8,128)(2,1)} copy(bf16[512,1024]{1,0:T(8,128)(2,1)} %get-tuple-element.4) | data formatting | bytes 2097152
  140.3 1.7 %copy.14 = bf16[4,4,8192]{2,1,0:T(4,128)(2,1)} copy(bf16[4,4,8192]{2,1,0:T(4,128)(2,1)} %get-tuple-element.5) | data formatting | bytes 524288

commit v4 on v3

--- a/solution.py
+++ b/solution.py
@@ -27,8 +27,8 @@
 
 def kernel(names, lens_ref, rowp_ref, clen_ref, ds_ref, x_hbm, wkv_hbm, wq_hbm, wo_hbm, cache_hbm, ctx_ref, out_ref, *scratch):
     r = dict(zip(names, scratch))
-    xv, wkv, wq, wo, raw, ck, cv = (r[n] for n in ("xv", "wkv", "wq", "wo", "raw", "ck", "cv"))
-    kv, qh, acc_q, acc_kv, scale, bias = (r[n] for n in ("kv", "qh", "acc_q", "acc_kv", "scale", "bias"))
+    xv, wk, wv, wq, wo, raw, ck, cv = (r[n] for n in ("xv", "wk", "wv", "wq", "wo", "raw", "ck", "cv"))
+    kk, vv, qh, acc_q, acc_kv, scale, bias = (r[n] for n in ("kk", "vv", "qh", "acc_q", "acc_kv", "scale", "bias"))
     a_recv, xu, xu_send, state = (r[n] for n in ("a_recv", "xu", "xu_send", "state"))
     b_send, b_recv, qs, fkv = (r[n] for n in ("b_send", "b_recv", "qs", "fkv"))
     c_send, c_recv, d_send, d_recv = (r[n] for n in ("c_send", "c_recv", "d_send", "d_recv"))
@@ -119,9 +119,8 @@
         split = jnp.dot(pick, pair, preferred_element_type=f32).astype(bf16)
         for j in range(2):
             dst = pl.ds(pl.multiple_of((2 * i + j) * 128, 128), 128)
-            wkv[s, dst, :] = jnp.concatenate(
-                [split[:128, j * HD : (j + 1) * HD], split[128:, j * HD : (j + 1) * HD]], axis=1
-            )
+            wk[s, dst, :] = split[:128, j * HD : (j + 1) * HD]
+            wv[s, dst, :] = split[128:, j * HD : (j + 1) * HD]
         return c
 
     lax.fori_loop(0, dblk // 256, separate_weights, 0)
@@ -130,8 +129,10 @@
         ds[i] = ds_ref[:, i * dblk : (i + 1) * dblk].astype(f32)
     pl.semaphore_wait(barrier, NS - 1 + NG - 1 + NT - 1)
 
-    def krows(blk, q):
-        return wkv.at[blk, pl.ds(pl.multiple_of(q * quarter, quarter), quarter)]
+    weights_of, cached = (wk, wv), (kk, vv)
+
+    def krows(j, blk, q):
+        return weights_of[j].at[blk, pl.ds(pl.multiple_of(q * quarter, quarter), quarter)]
 
     def qrows(blk, q, h):
         return wq.at[blk, pl.ds(pl.multiple_of(q * quarter + h * half, half), half)]
@@ -140,31 +141,46 @@
     ky_s, ky_r, kz_s, kz_r, kc_s, kc_r = (r[n] for n in ("ky_s", "ky_r", "kz_s", "kz_r", "kc_s", "kc_r"))
     qy_s, qy_r, qz_s, qz_r, qc_s, qc_r = (r[n] for n in ("qy_s", "qy_r", "qz_s", "qz_r", "qc_s", "qc_r"))
 
-    for i in range(2):
-        send(krows(s, q_of[i]), krows(s, q_of[i]), ky_s.at[i], ky_r.at[i], shard=s2)
-    send(wkv.at[s], wkv.at[s], kc_s.at[4], kc_r.at[4], shard=sc)
+    for i, j in ((0, 0), (0, 1), (1, 0), (1, 1)):
+        ref = krows(j, s, q_of[i])
+        send(ref, ref, ky_s.at[j, i], ky_r.at[j, i], shard=s2)
+    for j in range(2):
+        ref = weights_of[j].at[s]
+        send(ref, ref, kc_s.at[j, 4], kc_r.at[j, 4], shard=sc)
     for d in range(1, NS):
         p = up(s, d, NS)
         send(ds.at[p], a_recv.at[s], r["a_s"].at[d - 1], r["a_r"].at[s], shard=p)
-    send(wq_hbm, wq.at[s], qc_s.at[8], qc_r.at[8], shard=sc)
     a_recv[s] = ds[s]
     r["fkv"][...] = jnp.zeros_like(fkv)
-    kv[:MOST, :] = jnp.zeros((MOST, 2 * HD), bf16)
-
-    def k_arrive_y(i):
-        arrive(krows(s2, q_of[i]), ky_s.at[i], ky_r.at[i], shard=s2)
-
-    def k_arrive_z(i):
-        arrive(krows(s2, q_of[2 + i]), kz_s.at[i], kz_r.at[i], group=q_of[2 + i])
-
-    def k_forward(role):
-        ref = krows(s2, q_of[role])
-        send(ref, ref, kc_s.at[role], kc_r.at[role], shard=sc)
-
-    def k_forward_z():
-        ref = krows(s2, g)
-        send(ref, ref, kz_s.at[0], kz_r.at[0], group=up(g, 1, NG))
-        send(ref, ref, kz_s.at[1], kz_r.at[1], group=up(g, 3, NG))
+    for ref in cached:
+        ref[:MOST, :] = jnp.zeros((MOST, HD), bf16)
+
+    def k_arrive_y(j, i):
+        arrive(krows(j, s2, q_of[i]), ky_s.at[j, i], ky_r.at[j, i], shard=s2)
+
+    def k_arrive_z(j, i):
+        arrive(krows(j, s2, q_of[2 + i]), kz_s.at[j, i], kz_r.at[j, i], group=q_of[2 + i])
+
+    def k_arrive_core(j, role):
+        arrive(krows(j, s3, q_of[role]), kc_s.at[j, role], kc_r.at[j, role], shard=sc)
+
+    def k_forward(j, role):
+        ref = krows(j, s2, q_of[role])
+        send(ref, ref, kc_s.at[j, role], kc_r.at[j, role], shard=sc)
+
+    def k_forward_z(j):
+        ref = krows(j, s2, g)
+        send(ref, ref, kz_s.at[j, 0], kz_r.at[j, 0], group=up(g, 1, NG))
+        send(ref, ref, kz_s.at[j, 1], kz_r.at[j, 1], group=up(g, 3, NG))
+
+    def q_core(q):
+        ref = wq.at[s, pl.ds(q * quarter, quarter)]
+        send(ref, ref, qc_s.at[8 + q], qc_r.at[8 + q], shard=sc)
+
+    def q_core_ready():
+        for q in range(NG):
+            ref = wq.at[sc, pl.ds(q * quarter, quarter)]
+            arrive(ref, qc_s.at[8 + q], qc_r.at[8 + q], shard=sc)
 
     def q_send_y(i):
         ref = qrows(s, g, i)
@@ -198,9 +214,9 @@
     def x_block(blk):
         return xv[:, pl.ds(pl.multiple_of(blk * dblk, dblk), dblk)]
 
-    def kv_block(blk, first):
-        prod = jnp.dot(x_block(blk), wkv[blk], preferred_element_type=f32)
-        acc_kv[...] = prod if first else acc_kv[...] + prod
+    def kv_block(j, blk, first):
+        prod = jnp.dot(x_block(blk), weights_of[j][blk], preferred_element_type=f32)
+        acc_kv[j] = prod if first else acc_kv[j] + prod
 
     def q_block(blk, first, lo=0, hi=None):
         hi = qcols // 256 if hi is None else hi
@@ -224,12 +240,15 @@
         scale[part, :] = jnp.broadcast_to(lax.rsqrt(mean + EPSILON), (32, HD))
         return c
 
+    for j in range(2):
+        kv_block(j, s, True)
+    k_arrive_y(0, 0)
+    k_forward_z(0)
+    k_forward(0, 0)
     lax.fori_loop(0, tok // 32, squares, 0)
-    kv_block(s, True)
-
-    k_arrive_y(0)
-    k_forward_z()
-    k_forward(0)
+    k_arrive_y(1, 0)
+    k_forward_z(1)
+    k_forward(1, 0)
 
     for d in range(1, NS):
         src = up(s, NS - d, NS)
@@ -240,61 +259,71 @@
     mine = pl.ds(pl.multiple_of(t * piece, piece), piece)
     state[...] = jnp.concatenate([a_recv[i, :, mine] for i in range(NS)], axis=0)
 
-    load_wq.wait()
-    q_block(s, True)
-
-    k_arrive_y(1)
-    k_forward(1)
-    arrive(wkv.at[sc], kc_s.at[4], kc_r.at[4], shard=sc)
-    kv_block(sc, False)
-    k_arrive_z(0)
-    k_forward(2)
-    k_arrive_z(1)
-    k_forward(3)
-    kv_block(s2, False)
-    for role in range(4):
-        arrive(krows(s3, q_of[role]), kc_s.at[role], kc_r.at[role], shard=sc)
-    kv_block(s3, False)
-
-    def slot(gg, ss):
-        return kv.at[pl.ds(pl.multiple_of(MOST + (gg * NS + ss) * tok, tok), tok)]
-
-    both = jnp.concatenate([scale[...], scale[...]], axis=1)
-    kv[pl.ds(pl.multiple_of(MOST + (g * NS + s) * tok, tok), tok), :] = (acc_kv[...] * both).astype(bf16)
+    def slot(j, gg, ss):
+        return cached[j].at[pl.ds(pl.multiple_of(MOST + (gg * NS + ss) * tok, tok), tok)]
+
+    def half_slot(j, gg, ss, h):
+        n = tok // 2
+        return cached[j].at[pl.ds(pl.multiple_of(MOST + (gg * NS + ss) * tok + h * n, n), n)]
+
     vy_s, vy_r, vz_s, vz_r, vc_s, vc_r = (r[n] for n in ("vy_s", "vy_r", "vz_s", "vz_r", "vc_s", "vc_r"))
     below, above = up(g, 3, NG), up(g, 1, NG)
 
-    def half_slot(gg, ss, h):
-        n = tok // 2
-        return kv.at[pl.ds(pl.multiple_of(MOST + (gg * NS + ss) * tok + h * n, n), n)]
-
-    def v_core(ref, i):
-        send(ref, ref, vc_s.at[i], vc_r.at[i], shard=sc)
-
-    def v_sides(ss, i):
-        ref = slot(g, ss)
-        send(ref, ref, vz_s.at[i], vz_r.at[i], group=above)
-        send(ref, ref, vz_s.at[i + 1], vz_r.at[i + 1], group=below)
-
-    def v_pass(ss, i, core):
+    def v_core(j, ref, i):
+        send(ref, ref, vc_s.at[j, i], vc_r.at[j, i], shard=sc)
+
+    def v_sides(j, ss, i):
+        ref = slot(j, g, ss)
+        send(ref, ref, vz_s.at[j, i], vz_r.at[j, i], group=above)
+        send(ref, ref, vz_s.at[j, i + 1], vz_r.at[j, i + 1], group=below)
+
+    def v_pass(j, ss, i, core):
         for h, (source, target) in enumerate([(below, above), (above, below)]):
-            arrive(slot(source, ss), vz_s.at[i + h], vz_r.at[i + h], group=source)
-            ref = half_slot(source, ss, h)
-            send(ref, ref, vz_s.at[i + 4 + h], vz_r.at[i + 4 + h], group=target)
-            v_core(slot(source, ss), core + h)
-
-    def v_last(ss, i, core):
+            arrive(slot(j, source, ss), vz_s.at[j, i + h], vz_r.at[j, i + h], group=source)
+            ref = half_slot(j, source, ss, h)
+            send(ref, ref, vz_s.at[j, i + 4 + h], vz_r.at[j, i + 4 + h], group=target)
+            v_core(j, slot(j, source, ss), core + h)
+
+    def v_last(j, ss, i, core):
         for h, source in enumerate([below, above]):
-            ref = half_slot(up(g, 2, NG), ss, h)
-            arrive(ref, vz_s.at[i + 4 + h], vz_r.at[i + 4 + h], group=source)
-            v_core(ref, core + h)
-
-    own = slot(g, s)
-    send(own, own, vy_s.at[0], vy_r.at[0], shard=s2)
-    v_sides(s, 0)
-    v_core(own, 0)
-    q_send_y(0)
-    q_send_y(1)
+            ref = half_slot(j, up(g, 2, NG), ss, h)
+            arrive(ref, vz_s.at[j, i + 4 + h], vz_r.at[j, i + 4 + h], group=source)
+            v_core(j, ref, core + h)
+
+    def v_theirs(j):
+        ref = slot(j, g, s2)
+        arrive(ref, vy_s.at[j], vy_r.at[j], shard=s2)
+        v_sides(j, s2, 2)
+        v_core(j, ref, 1)
+
+    def v_core_ready(j):
+        for i, ref in enumerate(
+            [slot(j, g, sc), slot(j, g, s3)]
+            + [slot(j, gg, ss) for ss in (sc, s3) for gg in (below, above)]
+            + [half_slot(j, up(g, 2, NG), ss, h) for ss in (sc, s3) for h in range(2)]
+        ):
+            arrive(ref, vc_s.at[j, i], vc_r.at[j, i], shard=sc)
+
+    for j in range(2):
+        k_arrive_z(j, 0)
+        k_forward(j, 2)
+        k_arrive_z(j, 1)
+        k_forward(j, 3)
+        k_arrive_y(j, 1)
+        k_forward(j, 1)
+        arrive(weights_of[j].at[sc], kc_s.at[j, 4], kc_r.at[j, 4], shard=sc)
+        kv_block(j, sc, False)
+        kv_block(j, s2, False)
+        for role in (0, 2, 3, 1):
+            k_arrive_core(j, role)
+        kv_block(j, s3, False)
+        cached[j][pl.ds(pl.multiple_of(MOST + (g * NS + s) * tok, tok), tok), :] = (acc_kv[j] * scale[...]).astype(
+            bf16
+        )
+        own = slot(j, g, s)
+        send(own, own, vy_s.at[j], vy_r.at[j], shard=s2)
+        v_sides(j, s, 0)
+        v_core(j, own, 0)
 
     def decode_project():
         acc = jnp.zeros((NS * rows, qcols), f32)
@@ -303,7 +332,9 @@
         for i in range(NT):
             xi = xu[i]
             acc += jnp.dot(xi, wq[s, i * piece : (i + 1) * piece, :], preferred_element_type=f32)
-            acc2 += jnp.dot(xi, wkv[s, i * piece : (i + 1) * piece, :], preferred_element_type=f32)
+            part = slice(i * piece, (i + 1) * piece)
+            joined = jnp.concatenate([wk[s, part, :], wv[s, part, :]], axis=1)
+            acc2 += jnp.dot(xi, joined, preferred_element_type=f32)
             xf = xi.astype(f32)
             square += jnp.sum(xf * xf, axis=1, keepdims=True)
         wide = jnp.broadcast_to(square, (NS * rows, HD))
@@ -319,7 +350,10 @@
             copies.append(c)
         return copies
 
+    load_wq.wait()
     b_copies = decode_project()
+    q_send_y(0)
+    q_send_y(1)
 
     load_raw.wait()
     def separate(i, c):
@@ -333,65 +367,64 @@
                 cv[row + j, dst, :] = split[128:, j * HD : (j + 1) * HD]
         return c
 
-    lax.fori_loop(0, 2 * ck.shape[1] // 256, separate, 0)
-    arrive(wq.at[sc], qc_s.at[8], qc_r.at[8], shard=sc)
-    q_block(sc, False)
-
     for i in range(tok // QT):
         q_pos = s * tok + i * QT + lax.broadcasted_iota(jnp.int32, (QT, KW), 0)
         k_pos = s * tok + i * QT - MOST + lax.broadcasted_iota(jnp.int32, (QT, KW), 1)
         start = jnp.where(q_pos >= b1, b1, jnp.where(q_pos >= b0, b0, 0))
         bias[i] = jnp.where((k_pos >= start) & (k_pos <= q_pos), 0.0, -1e30)
 
-    arrive(slot(g, s2), vy_s.at[0], vy_r.at[0], shard=s2)
-    v_sides(s2, 2)
-    v_core(slot(g, s2), 1)
-    v_pass(s, 0, 2)
-    v_pass(s2, 2, 4)
-    v_last(s, 0, 6)
-    v_last(s2, 2, 8)
-    for i, ref in enumerate(
-        [slot(g, sc), slot(g, s3)]
-        + [slot(gg, ss) for ss in (sc, s3) for gg in (below, above)]
-        + [half_slot(up(g, 2, NG), ss, h) for ss in (sc, s3) for h in range(2)]
-    ):
-        arrive(ref, vc_s.at[i], vc_r.at[i], shard=sc)
+    v_theirs(0)
+    v_pass(0, s, 0, 2)
+    v_theirs(1)
+    v_pass(1, s, 0, 2)
+    lax.fori_loop(0, 2 * ck.shape[1] // 256, separate, 0)
+    v_last(0, s, 0, 6)
+    v_pass(0, s2, 2, 4)
+    v_last(1, s, 0, 6)
+    v_pass(1, s2, 2, 4)
+    v_last(0, s2, 2, 8)
+    v_core_ready(0)
+
+    def splat(flag):
+        return jnp.broadcast_to(flag, (HD, HD)).astype(f32).astype(bf16)
+
+    at_spot = [splat((spot == j).astype(jnp.int32)) for j in range(spots)]
+    takes = [splat(is_new[row]) for row in range(rows)]
+
+    def place(j):
+        stored = (ck, cv)[j]
+
+        def part(i, c):
+            dst = pl.ds(pl.multiple_of(i * HD, HD), HD)
+            window = jnp.zeros((HD, HD), bf16)
+            for n in range(spots):
+                src = pl.ds(pl.multiple_of((1 + n) * MOST + i * HD, HD), HD)
+                window = window + cached[j][src, :] * at_spot[n]
+            for row in range(rows):
+                stored[row, dst, :] = stored[row, dst, :] * (1 - takes[row]) + window * takes[row]
+            return c
+
+        lax.fori_loop(0, 2 * MOST // HD, part, 0)
+
+    place(0)
+    v_last(1, s2, 2, 8)
+    v_core_ready(1)
+    place(1)
     q_arrive_y(0)
     q_forward_z(0)
     q_forward(0)
-
-    def splat(flag):
-        return jnp.broadcast_to(flag, (HD, HD)).astype(f32).astype(bf16)
-
-    at_spot = [splat((spot == j).astype(jnp.int32)) for j in range(spots)]
-    at_spot = [jnp.concatenate([v, v], axis=1) for v in at_spot]
-    takes = [splat(is_new[row]) for row in range(rows)]
-
-    def place(i, c):
-        dst = pl.ds(pl.multiple_of(i * HD, HD), HD)
-        window = jnp.zeros((HD, 2 * HD), bf16)
-        for j in range(spots):
-            src = pl.ds(pl.multiple_of((1 + j) * MOST + i * HD, HD), HD)
-            window = window + kv[src, :] * at_spot[j]
-        for row in range(rows):
-            old = 1 - takes[row]
-            ck[row, dst, :] = ck[row, dst, :] * old + window[:, :HD] * takes[row]
-            cv[row, dst, :] = cv[row, dst, :] * old + window[:, HD:] * takes[row]
-        return c
-
-    lax.fori_loop(0, 2 * MOST // HD, place, 0)
 
     def attend(u, c):
         h = lax.rem(u, heads)
         i = u // heads
         part = pl.ds(pl.multiple_of(i * QT, QT), QT)
         keys = pl.ds(pl.multiple_of((g * NS + s) * tok + i * QT, QT), KW)
-        scores = lax.dot_general(qh[h, part, :], kv[keys, :HD], TRANS, preferred_element_type=f32)
+        scores = lax.dot_general(qh[h, part, :], kk[keys, :], TRANS, preferred_element_type=f32)
         scores = scores + bias[i]
         high = jnp.max(scores, axis=1, keepdims=True)
         weights = jnp.exp2((scores - high) * (INV_ROOT * LOG2E))
         summed = jnp.sum(weights, axis=1, keepdims=True)
-        mixed = jnp.dot(weights.astype(bf16), kv[keys, HD:], preferred_element_type=f32)
+        mixed = jnp.dot(weights.astype(bf16), vv[keys, :], preferred_element_type=f32)
         cols = pl.ds(pl.multiple_of(h * HD, HD), HD)
         ctx_ref[part, cols] = (mixed / summed).astype(bf16)
         return c
@@ -425,8 +458,11 @@
 
     units = heads * (tok // QT)
     fills = {
-        (0, 1): [s2_early],
-        (0, 3): [lambda: s2_sides(0)],
+        (0, 0): [lambda: q_core(0), lambda: q_block(s, True)],
+        (0, 1): [s2_early, lambda: q_core(1)],
+        (0, 2): [lambda: q_core(2)],
+        (0, 3): [lambda: s2_sides(0), lambda: q_core(3)],
+        (1, 0): [q_core_ready, lambda: q_block(sc, False)],
         (1, 1): [lambda: s2_sides(1)],
         (2, 0): [s2_last, lambda: q_block(s2, False)],
         (2, 1): [s3_ready, lambda: q_block(s3, False)],
@@ -579,16 +615,18 @@
     bw = qcols + 3 * HD
     scratch = dict(
         xv=vm((tok, width), bf16),
-        wkv=vm((NS, dblk, 2 * HD), bf16),
+        wk=vm((NS, dblk, HD), bf16),
+        wv=vm((NS, dblk, HD), bf16),
         wq=vm((NS, dblk, qcols), bf16),
         wo=vm(wo.shape, bf16),
         raw=vm(cache.shape, bf16),
         ck=vm((rows, CACHE, HD), bf16),
         cv=vm((rows, CACHE, HD), bf16),
-        kv=vm((MOST + NG * NS * tok, 2 * HD), bf16),
+        kk=vm((MOST + NG * NS * tok, HD), bf16),
+        vv=vm((MOST + NG * NS * tok, HD), bf16),
         qh=vm((heads, tok, HD), bf16),
         acc_q=vm((tok, qcols), f32),
-        acc_kv=vm((tok, 2 * HD), f32),
+        acc_kv=vm((2, tok, HD), f32),
         scale=vm((tok, HD), f32),
         bias=vm((tok // QT, QT, KW), f32),
         kraw=vm((2 * dblk, HD), bf16),
@@ -610,24 +648,24 @@
         e_send=vm((STEPS, NS, rows, dblk), f32),
         e_recv=vm((STEPS, NS, rows, dblk), f32),
         lsem=dma((5,)),
-        ky_s=dma((2,)),
-        ky_r=dma((2,)),
-        kz_s=dma((2,)),
-        kz_r=dma((2,)),
-        kc_s=dma((5,)),
-        kc_r=dma((5,)),
+        ky_s=dma((2, 2)),
+        ky_r=dma((2, 2)),
+        kz_s=dma((2, 2)),
+        kz_r=dma((2, 2)),
+        kc_s=dma((2, 5)),
+        kc_r=dma((2, 5)),
         qy_s=dma((2,)),
         qy_r=dma((2,)),
         qz_s=dma((6,)),
         qz_r=dma((6,)),
-        qc_s=dma((9,)),
-        qc_r=dma((9,)),
-        vy_s=dma((1,)),
-        vy_r=dma((1,)),
-        vz_s=dma((8,)),
-        vz_r=dma((8,)),
-        vc_s=dma((10,)),
-        vc_r=dma((10,)),
+        qc_s=dma((12,)),
+        qc_r=dma((12,)),
+        vy_s=dma((2,)),
+        vy_r=dma((2,)),
+        vz_s=dma((2, 8)),
+        vz_r=dma((2, 8)),
+        vc_s=dma((2, 10)),
+        vc_r=dma((2, 10)),
         a_s=dma((NS - 1,)),
         a_r=dma((NS,)),
         b_s=dma((NS - 1,)),

time: 142 us -> 136 us (0.958)
  Pallas kernels: 137 us -> 131 us
    pallas_call x1, Pallas kernels: 137 us -> 131 us  [layer(): pl.pallas_call(functools.partial(kernel, tuple(scratch)), out_shape=(jax....]
where the time goes in v4:
time: 136 us
  Pallas kernels  131 us (96%)
  local copies, waits for them, and re-layouts  4.01 us (3%)
    pallas_call x1, Pallas kernels, layer(): pl.pallas_call(functools.partial(kernel, tuple(scratch)), out_shape=(jax....  131 us
    unnamed x2, local copies, waits for them, and re-layouts  4.01 us

profile of v4, /device:TPU:1, one launch (start us, length us, event | category | flops | bytes accessed | tf_op | source)
XLA Modules:
  0.0 135.9 jit_solution(2752656022544768561)
XLA Ops:
  0.6 131.2 %attention_layer.1 = (bf16[512,1024]{1,0:T(8,128)(2,1)}, bf16[4,4,8192]{2,1,0:T(4,128)(2,1)}) custom-call(s32[4,3]{1,0:T(4,128)} %lens_ref.1, s32[4]{0:T(128)} %rowp_ref.1, s32[4]{0:T(128)} %clen_ref.1, bf16[4,8192]{1,0:T(4,128)(2,1)} %ds_ref.1, bf16[512,8192]{1,0:T(8,128)(2,1)} %x_hbm.1, bf16[4096,128]{1,0:T(8,128)(2,1)} %bitcast.3, ...), custom_call_target="tpu_custom_call" | custom-call | tf_op jit(solution)/shard_map/attention_layer/pallas_call | solution.py:687
  131.9 2.3 %copy.13 = bf16[512,1024]{1,0:T(8,128)(2,1)} copy(bf16[512,1024]{1,0:T(8,128)(2,1)} %get-tuple-element.4) | data formatting | bytes 2097152
  134.1 1.7 %copy.14 = bf16[4,4,8192]{2,1,0:T(4,128)(2,1)} copy(bf16[4,4,8192]{2,1,0:T(4,128)(2,1)} %get-tuple-element.5) | data formatting | bytes 524288

commit v5 on v4

--- a/solution.py
+++ b/solution.py
@@ -48,6 +48,7 @@
     width = NS * dblk
     quarter = dblk // NG
     half = quarter // 2
+    wide = qcols // 2
 
     def up(base, d, n):
         return lax.rem(base + d, n)
@@ -75,13 +76,17 @@
 
     load_wkv = load(wkv_hbm, r["kraw"], 1)
     load_x = load(x_hbm, xv, 0)
-    load_wq = load(wq_hbm, wq.at[s], 2)
 
     barrier = pltpu.get_barrier_semaphore()
-    for d in range(1, NS):
-        pl.semaphore_signal(barrier, inc=1, device_id={"shard": up(s, d, NS)}, device_id_type=MESH)
-    for d in range(1, NG):
-        pl.semaphore_signal(barrier, inc=1, device_id={"group": up(g, d, NG)}, device_id_type=MESH)
+    flat = g * NS + s
+    everyone = NG * NS
+
+    def flat_peer(d):
+        f = up(flat, d, everyone)
+        return f, {"group": f // NS, "shard": lax.rem(f, NS)}
+
+    for d in range(1, everyone):
+        pl.semaphore_signal(barrier, inc=1, device_id=flat_peer(d)[1], device_id_type=MESH)
     for d in range(1, NT):
         pl.semaphore_signal(barrier, inc=1, device_id={"tensor": up(t, d, NT)}, device_id_type=MESH)
 
@@ -127,7 +132,7 @@
     ds = r["ds"]
     for i in range(NS):
         ds[i] = ds_ref[:, i * dblk : (i + 1) * dblk].astype(f32)
-    pl.semaphore_wait(barrier, NS - 1 + NG - 1 + NT - 1)
+    pl.semaphore_wait(barrier, everyone - 1 + NT - 1)
 
     weights_of, cached = (wk, wv), (kk, vv)
 
@@ -135,7 +140,10 @@
         return weights_of[j].at[blk, pl.ds(pl.multiple_of(q * quarter, quarter), quarter)]
 
     def qrows(blk, q, h):
-        return wq.at[blk, pl.ds(pl.multiple_of(q * quarter + h * half, half), half)]
+        return wq.at[blk, pl.ds(pl.multiple_of(q * quarter, quarter), quarter), h * wide : (h + 1) * wide]
+
+    def qhalf(blk, q, h, n):
+        return wq.at[blk, pl.ds(pl.multiple_of(q * quarter + n * half, half), half), h * wide : (h + 1) * wide]
 
     q_of = [g, up(g, 2, NG), up(g, 3, NG), up(g, 1, NG)]
     ky_s, ky_r, kz_s, kz_r, kc_s, kc_r = (r[n] for n in ("ky_s", "ky_r", "kz_s", "kz_r", "kc_s", "kc_r"))
@@ -190,11 +198,15 @@
         arrive(qrows(s2, g, i), qy_s.at[i], qy_r.at[i], shard=s2)
 
     def q_second(h):
-        ref = qrows(s2, q_of[2 + h], h)
-        send(ref, ref, qz_s.at[4 + h], qz_r.at[4 + h], group=up(g, 1 + 2 * h, NG))
+        for n in range(2):
+            ref = qhalf(s2, q_of[2 + n], h, n)
+            i = 4 + 2 * h + n
+            send(ref, ref, qz_s.at[i], qz_r.at[i], group=up(g, 1 + 2 * n, NG))
 
     def q_arrive_second(h):
-        arrive(qrows(s2, q_of[1], h), qz_s.at[4 + h], qz_r.at[4 + h], group=q_of[2 + h])
+        for n in range(2):
+            i = 4 + 2 * h + n
+            arrive(qhalf(s2, q_of[1], h, n), qz_s.at[i], qz_r.at[i], group=q_of[2 + n])
 
     def q_forward_z(h):
         ref = qrows(s2, g, h)
@@ -218,18 +230,17 @@
         prod = jnp.dot(x_block(blk), weights_of[j][blk], preferred_element_type=f32)
         acc_kv[j] = prod if first else acc_kv[j] + prod
 
-    def q_block(blk, first, lo=0, hi=None):
-        hi = qcols // 256 if hi is None else hi
-
+    def q_block(blk, h, first=False):
         def part(n, c):
             cols = pl.ds(pl.multiple_of(n * 256, 256), 256)
             prod = jnp.dot(x_block(blk), wq[blk, :, cols], preferred_element_type=f32)
             acc_q[:, cols] = prod if first else acc_q[:, cols] + prod
             return c
 
-        lax.fori_loop(lo, hi, part, 0)
+        lax.fori_loop(h * wide // 256, (h + 1) * wide // 256, part, 0)
 
     load_x.wait()
+    load_wq = load(wq_hbm, wq.at[s], 2)
     load_raw = load(cache_hbm, raw, 3)
     load_wo = load(wo_hbm, wo, 4)
 
@@ -240,90 +251,27 @@
         scale[part, :] = jnp.broadcast_to(lax.rsqrt(mean + EPSILON), (32, HD))
         return c
 
-    for j in range(2):
-        kv_block(j, s, True)
-    k_arrive_y(0, 0)
-    k_forward_z(0)
-    k_forward(0, 0)
-    lax.fori_loop(0, tok // 32, squares, 0)
-    k_arrive_y(1, 0)
-    k_forward_z(1)
-    k_forward(1, 0)
-
-    for d in range(1, NS):
-        src = up(s, NS - d, NS)
-        arrive(a_recv.at[src], r["a_s"].at[d - 1], r["a_r"].at[src], shard=src)
-    x0 = jnp.concatenate([a_recv[i] for i in range(NS)], axis=0)
-    for i in range(NT):
-        xu[i] = x0[:, i * piece : (i + 1) * piece].astype(bf16)
-    mine = pl.ds(pl.multiple_of(t * piece, piece), piece)
-    state[...] = jnp.concatenate([a_recv[i, :, mine] for i in range(NS)], axis=0)
-
-    def slot(j, gg, ss):
-        return cached[j].at[pl.ds(pl.multiple_of(MOST + (gg * NS + ss) * tok, tok), tok)]
-
-    def half_slot(j, gg, ss, h):
-        n = tok // 2
-        return cached[j].at[pl.ds(pl.multiple_of(MOST + (gg * NS + ss) * tok + h * n, n), n)]
-
-    vy_s, vy_r, vz_s, vz_r, vc_s, vc_r = (r[n] for n in ("vy_s", "vy_r", "vz_s", "vz_r", "vc_s", "vc_r"))
-    below, above = up(g, 3, NG), up(g, 1, NG)
-
-    def v_core(j, ref, i):
-        send(ref, ref, vc_s.at[j, i], vc_r.at[j, i], shard=sc)
-
-    def v_sides(j, ss, i):
-        ref = slot(j, g, ss)
-        send(ref, ref, vz_s.at[j, i], vz_r.at[j, i], group=above)
-        send(ref, ref, vz_s.at[j, i + 1], vz_r.at[j, i + 1], group=below)
-
-    def v_pass(j, ss, i, core):
-        for h, (source, target) in enumerate([(below, above), (above, below)]):
-            arrive(slot(j, source, ss), vz_s.at[j, i + h], vz_r.at[j, i + h], group=source)
-            ref = half_slot(j, source, ss, h)
-            send(ref, ref, vz_s.at[j, i + 4 + h], vz_r.at[j, i + 4 + h], group=target)
-            v_core(j, slot(j, source, ss), core + h)
-
-    def v_last(j, ss, i, core):
-        for h, source in enumerate([below, above]):
-            ref = half_slot(j, up(g, 2, NG), ss, h)
-            arrive(ref, vz_s.at[j, i + 4 + h], vz_r.at[j, i + 4 + h], group=source)
-            v_core(j, ref, core + h)
-
-    def v_theirs(j):
-        ref = slot(j, g, s2)
-        arrive(ref, vy_s.at[j], vy_r.at[j], shard=s2)
-        v_sides(j, s2, 2)
-        v_core(j, ref, 1)
-
-    def v_core_ready(j):
-        for i, ref in enumerate(
-            [slot(j, g, sc), slot(j, g, s3)]
-            + [slot(j, gg, ss) for ss in (sc, s3) for gg in (below, above)]
-            + [half_slot(j, up(g, 2, NG), ss, h) for ss in (sc, s3) for h in range(2)]
-        ):
-            arrive(ref, vc_s.at[j, i], vc_r.at[j, i], shard=sc)
-
-    for j in range(2):
-        k_arrive_z(j, 0)
-        k_forward(j, 2)
-        k_arrive_z(j, 1)
-        k_forward(j, 3)
-        k_arrive_y(j, 1)
-        k_forward(j, 1)
-        arrive(weights_of[j].at[sc], kc_s.at[j, 4], kc_r.at[j, 4], shard=sc)
-        kv_block(j, sc, False)
-        kv_block(j, s2, False)
-        for role in (0, 2, 3, 1):
-            k_arrive_core(j, role)
-        kv_block(j, s3, False)
-        cached[j][pl.ds(pl.multiple_of(MOST + (g * NS + s) * tok, tok), tok), :] = (acc_kv[j] * scale[...]).astype(
-            bf16
-        )
-        own = slot(j, g, s)
-        send(own, own, vy_s.at[j], vy_r.at[j], shard=s2)
-        v_sides(j, s, 0)
-        v_core(j, own, 0)
+    def all_shards(src_of, dst, ssem, rsem):
+        copies = []
+        for d in range(1, NS):
+            p = up(s, d, NS)
+            c = remote(src_of(p), dst, ssem.at[d - 1], rsem, shard=p)
+            c.start()
+            copies.append(c)
+        return copies
+
+    def all_tensors(src_of, dst, ssem, rsem):
+        copies = []
+        for d in (4, 6, 2, 5, 3, 7, 1):
+            p = up(t, d, NT)
+            c = remote(src_of(p), dst, ssem.at[d - 1], rsem, tensor=p)
+            c.start()
+            copies.append(c)
+        return copies
+
+    def settle(copies):
+        for c in copies:
+            c.wait_send()
 
     def decode_project():
         acc = jnp.zeros((NS * rows, qcols), f32)
@@ -350,8 +298,202 @@
             copies.append(c)
         return copies
 
+    def take_fresh(k):
+        total = b_send[s]
+        for d in range(1, NS):
+            src = up(s, NS - d, NS)
+            arrive(b_recv.at[src], r["b_s"].at[d - 1], r["b_r"].at[src], shard=src)
+            total = total + b_recv[src]
+        norm = lax.rsqrt(total[:, qcols + 2 * HD : qcols + 2 * HD + 1] / width + EPSILON)
+        fresh = (total[:, : qcols + 2 * HD] * norm).astype(bf16).astype(f32)
+        fkv[k] = fresh[:, qcols:]
+        for row in range(rows):
+            for h in range(heads):
+                qs[row, h : h + 1, :] = fresh[row : row + 1, h * HD : (h + 1) * HD]
+
+    cpos = lax.broadcasted_iota(jnp.int32, (heads, ck.shape[1]), 1)
+
+    def attend_stored(row):
+        valid = (cpos >= low[row]) & (cpos < high[row])
+        scores = lax.dot_general(qs[row].astype(bf16), ck[row], TRANS, preferred_element_type=f32) * INV_ROOT
+        scores = jnp.where(valid, scores, -1e30)
+        top = jnp.max(scores, axis=1, keepdims=True)
+        weights = jnp.where(valid, jnp.exp(scores - top), 0.0)
+        summed = jnp.sum(weights, axis=1, keepdims=True)
+        return top, summed, jnp.dot(weights.astype(bf16), cv[row], preferred_element_type=f32)
+
+    def join_fresh(k, row, old, summed, mixed):
+        q = qs[row]
+        top = old
+        news = []
+        for j in range(k + 1):
+            new = jnp.sum(q * fkv[j, row : row + 1, :HD], axis=1, keepdims=True) * INV_ROOT
+            news.append(new)
+            top = jnp.maximum(top, new)
+        rescale = jnp.exp(old - top)
+        summed = summed * rescale
+        mixed = mixed * rescale
+        for j in range(k + 1):
+            weight = jnp.exp(news[j] - top)
+            summed = summed + weight
+            mixed = mixed + weight.astype(bf16).astype(f32) * fkv[j, row : row + 1, HD:]
+        context = (mixed / summed).astype(bf16).astype(f32)
+        for h in range(heads):
+            c_send[row : row + 1, h * HD : (h + 1) * HD] = context[h : h + 1]
+
+    n_send, n_recv, m_send, m_recv, part0 = (r[n] for n in ("n_send", "n_recv", "m_send", "m_recv", "part0"))
+    takes32 = [jnp.broadcast_to(is_new[row], (heads, HD)).astype(f32) for row in range(rows)]
+
+    def ask():
+        q = jnp.zeros((heads, HD), f32)
+        for row in range(rows):
+            q = q + qs[row] * takes32[row]
+        n_send[:, :HD] = q
+        n_send[:, HD : 2 * HD] = jnp.broadcast_to(begin, (heads, HD)).astype(f32)
+        n_send[:, 2 * HD :] = jnp.broadcast_to(begin + sum(sizes), (heads, HD)).astype(f32)
+        for d in (10, 9, 11, 6, 5, 7, 8, 2, 14, 4, 12, 13, 3, 15, 1):
+            send(n_send, n_recv.at[flat], r["n_s"].at[d - 1], r["n_r"].at[flat], **flat_peer(d)[1])
+        n_recv[flat] = n_send[...]
+
+    def answer():
+        for d in range(1, everyone):
+            f, where = flat_peer(d)
+            arrive(n_recv.at[f], r["n_s"].at[d - 1], r["n_r"].at[f], **where)
+        asked = n_recv[...].reshape(everyone * heads, 3 * HD)
+        here = pl.ds(pl.multiple_of(MOST + flat * tok, tok), tok)
+        pos = (flat * tok + lax.broadcasted_iota(jnp.int32, (everyone * heads, tok), 1)).astype(f32)
+        valid = (pos >= asked[:, HD : HD + 1]) & (pos < asked[:, 2 * HD : 2 * HD + 1])
+        scores = lax.dot_general(asked[:, :HD].astype(bf16), kk[here, :], TRANS, preferred_element_type=f32)
+        scores = jnp.where(valid, scores * INV_ROOT, -1e30)
+        top = jnp.max(scores, axis=1, keepdims=True)
+        weights = jnp.where(valid, jnp.exp(scores - top), 0.0)
+        summed = jnp.sum(weights, axis=1, keepdims=True)
+        mixed = jnp.dot(weights.astype(bf16), vv[here, :], preferred_element_type=f32)
+        shape = (everyone, heads, HD)
+        m_send[:, :, :HD] = mixed.reshape(shape)
+        m_send[:, :, HD : 2 * HD] = jnp.broadcast_to(top, mixed.shape).reshape(shape)
+        m_send[:, :, 2 * HD :] = jnp.broadcast_to(summed, mixed.shape).reshape(shape)
+        for d in (10, 9, 11, 6, 5, 7, 8, 2, 14, 4, 12, 13, 3, 15, 1):
+            f, where = flat_peer(d)
+            send(m_send.at[f], m_recv.at[flat], r["m_s"].at[d - 1], r["m_r"].at[flat], **where)
+        m_recv[flat] = m_send[flat]
+
+    def first_context():
+        for d in range(1, everyone):
+            f, where = flat_peer(d)
+            arrive(m_recv.at[f], r["m_s"].at[d - 1], r["m_r"].at[f], **where)
+        top = m_recv[0, :, HD : 2 * HD]
+        for i in range(1, everyone):
+            top = jnp.maximum(top, m_recv[i, :, HD : 2 * HD])
+        summed = jnp.zeros((heads, HD), f32)
+        mixed = jnp.zeros((heads, HD), f32)
+        for i in range(everyone):
+            rescale = jnp.exp(m_recv[i, :, HD : 2 * HD] - top)
+            summed = summed + m_recv[i, :, 2 * HD :] * rescale
+            mixed = mixed + m_recv[i, :, :HD] * rescale
+        for row in range(rows):
+            new = takes32[row] > 0
+            mine = [part0[row, :, i * HD : (i + 1) * HD] for i in range(3)]
+            join_fresh(
+                0,
+                row,
+                jnp.where(new, top, mine[0])[:, :1],
+                jnp.where(new, summed, mine[1])[:, :1],
+                jnp.where(new, mixed, mine[2]),
+            )
+
+    for j in range(2):
+        kv_block(j, s, True)
+    k_arrive_y(0, 0)
+    k_forward_z(0)
+    k_forward(0, 0)
+
+    for d in range(1, NS):
+        src = up(s, NS - d, NS)
+        arrive(a_recv.at[src], r["a_s"].at[d - 1], r["a_r"].at[src], shard=src)
+    x0 = jnp.concatenate([a_recv[i] for i in range(NS)], axis=0)
+    for i in range(NT):
+        xu[i] = x0[:, i * piece : (i + 1) * piece].astype(bf16)
+    mine = pl.ds(pl.multiple_of(t * piece, piece), piece)
+    state[...] = jnp.concatenate([a_recv[i, :, mine] for i in range(NS)], axis=0)
+
     load_wq.wait()
     b_copies = decode_project()
+    k_arrive_y(1, 0)
+    k_forward_z(1)
+    k_forward(1, 0)
+    lax.fori_loop(0, tok // 32, squares, 0)
+
+    def slot(j, gg, ss):
+        return cached[j].at[pl.ds(pl.multiple_of(MOST + (gg * NS + ss) * tok, tok), tok)]
+
+    def half_slot(j, gg, ss, h):
+        n = tok // 2
+        return cached[j].at[pl.ds(pl.multiple_of(MOST + (gg * NS + ss) * tok + h * n, n), n)]
+
+    vy_s, vy_r, vz_s, vz_r, vc_s, vc_r = (r[n] for n in ("vy_s", "vy_r", "vz_s", "vz_r", "vc_s", "vc_r"))
+    below, above = up(g, 3, NG), up(g, 1, NG)
+
+    def v_core(j, ref, i):
+        send(ref, ref, vc_s.at[j, i], vc_r.at[j, i], shard=sc)
+
+    def v_sides(j, ss, i):
+        ref = slot(j, g, ss)
+        send(ref, ref, vz_s.at[j, i], vz_r.at[j, i], group=above)
+        send(ref, ref, vz_s.at[j, i + 1], vz_r.at[j, i + 1], group=below)
+
+    def v_pass(j, ss, i, core):
+        for h, (source, target) in enumerate([(below, above), (above, below)]):
+            arrive(slot(j, source, ss), vz_s.at[j, i + h], vz_r.at[j, i + h], group=source)
+            ref = half_slot(j, source, ss, h)
+            send(ref, ref, vz_s.at[j, i + 4 + h], vz_r.at[j, i + 4 + h], group=target)
+            v_core(j, slot(j, source, ss), core + h)
+
+    def v_last(j, ss, i, core):
+        for h, source in enumerate([below, above]):
+            ref = half_slot(j, up(g, 2, NG), ss, h)
+            arrive(ref, vz_s.at[j, i + 4 + h], vz_r.at[j, i + 4 + h], group=source)
+            v_core(j, ref, core + h)
+
+    def v_theirs(j):
+        ref = slot(j, g, s2)
+        arrive(ref, vy_s.at[j], vy_r.at[j], shard=s2)
+        v_sides(j, s2, 2)
+        v_core(j, ref, 1)
+
+    def v_core_ready(j):
+        for i, ref in enumerate(
+            [slot(j, g, sc), slot(j, g, s3)]
+            + [slot(j, gg, ss) for ss in (sc, s3) for gg in (below, above)]
+            + [half_slot(j, up(g, 2, NG), ss, h) for ss in (sc, s3) for h in range(2)]
+        ):
+            arrive(ref, vc_s.at[j, i], vc_r.at[j, i], shard=sc)
+
+    for j in range(2):
+        k_arrive_z(j, 0)
+        k_forward(j, 2)
+        k_arrive_z(j, 1)
+        k_forward(j, 3)
+        k_arrive_y(j, 1)
+        k_forward(j, 1)
+        arrive(weights_of[j].at[sc], kc_s.at[j, 4], kc_r.at[j, 4], shard=sc)
+        kv_block(j, sc, False)
+        kv_block(j, s2, False)
+        for role in (0, 2, 3, 1):
+            k_arrive_core(j, role)
+        kv_block(j, s3, False)
+        cached[j][pl.ds(pl.multiple_of(MOST + (g * NS + s) * tok, tok), tok), :] = (acc_kv[j] * scale[...]).astype(
+            bf16
+        )
+        own = slot(j, g, s)
+        send(own, own, vy_s.at[j], vy_r.at[j], shard=s2)
+        v_sides(j, s, 0)
+        v_core(j, own, 0)
+        if j == 0:
+            take_fresh(0)
+            ask()
+
+    answer()
     q_send_y(0)
     q_send_y(1)
 
@@ -367,23 +509,20 @@
                 cv[row + j, dst, :] = split[128:, j * HD : (j + 1) * HD]
         return c
 
+    lax.fori_loop(0, 2 * ck.shape[1] // 256, separate, 0)
+    v_theirs(0)
+    v_pass(0, s, 0, 2)
+    for row in range(rows):
+        for i, v in enumerate(attend_stored(row)):
+            part0[row, :, i * HD : (i + 1) * HD] = jnp.broadcast_to(v, (heads, HD))
+    v_theirs(1)
+    v_pass(1, s, 0, 2)
+
     for i in range(tok // QT):
         q_pos = s * tok + i * QT + lax.broadcasted_iota(jnp.int32, (QT, KW), 0)
         k_pos = s * tok + i * QT - MOST + lax.broadcasted_iota(jnp.int32, (QT, KW), 1)
         start = jnp.where(q_pos >= b1, b1, jnp.where(q_pos >= b0, b0, 0))
         bias[i] = jnp.where((k_pos >= start) & (k_pos <= q_pos), 0.0, -1e30)
-
-    v_theirs(0)
-    v_pass(0, s, 0, 2)
-    v_theirs(1)
-    v_pass(1, s, 0, 2)
-    lax.fori_loop(0, 2 * ck.shape[1] // 256, separate, 0)
-    v_last(0, s, 0, 6)
-    v_pass(0, s2, 2, 4)
-    v_last(1, s, 0, 6)
-    v_pass(1, s2, 2, 4)
-    v_last(0, s2, 2, 8)
-    v_core_ready(0)
 
     def splat(flag):
         return jnp.broadcast_to(flag, (HD, HD)).astype(f32).astype(bf16)
@@ -406,17 +545,9 @@
 
         lax.fori_loop(0, 2 * MOST // HD, part, 0)
 
-    place(0)
-    v_last(1, s2, 2, 8)
-    v_core_ready(1)
-    place(1)
-    q_arrive_y(0)
-    q_forward_z(0)
-    q_forward(0)
-
     def attend(u, c):
-        h = lax.rem(u, heads)
-        i = u // heads
+        h = u // (tok // QT)
+        i = lax.rem(u, tok // QT)
         part = pl.ds(pl.multiple_of(i * QT, QT), QT)
         keys = pl.ds(pl.multiple_of((g * NS + s) * tok + i * QT, QT), KW)
         scores = lax.dot_general(qh[h, part, :], kk[keys, :], TRANS, preferred_element_type=f32)
@@ -432,72 +563,60 @@
     def attend_units(lo, hi):
         lax.fori_loop(lo, hi, attend, 0)
 
-    def finish_queries():
-        for h in range(heads):
+    def finish_queries(half):
+        for h in range(half * heads // 2, (half + 1) * heads // 2):
             qh[h] = (acc_q[:, h * HD : (h + 1) * HD] * scale[...]).astype(bf16)
 
-    def s2_early():
-        q_arrive_y(1)
-        q_forward_z(1)
-        q_forward(1)
-
-    def s2_sides(h):
+    def q_stage_y(h):
+        q_arrive_y(h)
+        q_forward_z(h)
+        q_forward(h)
+
+    def q_stage_z(h):
         for i in (h, 2 + h):
             q_arrive_z(i)
             q_forward(4 + i)
         q_second(h)
 
-    def s2_last():
-        for h in range(2):
-            q_arrive_second(h)
-            q_forward(2 + h)
-
-    def s3_ready():
-        for i in range(8):
-            q_arrive_core(i)
+    def q_stage_last(h):
+        q_arrive_second(h)
+        q_forward(2 + h)
+
+    def q_rest(h):
+        q_block(s2, h)
+        for role in range(4):
+            q_arrive_core(2 * role + h)
+        q_block(s3, h)
+
+    def in_place():
+        for j in range(2):
+            v_core_ready(j)
+            place(j)
 
     units = heads * (tok // QT)
+    per = units // 2
     fills = {
-        (0, 0): [lambda: q_core(0), lambda: q_block(s, True)],
-        (0, 1): [s2_early, lambda: q_core(1)],
-        (0, 2): [lambda: q_core(2)],
-        (0, 3): [lambda: s2_sides(0), lambda: q_core(3)],
-        (1, 0): [q_core_ready, lambda: q_block(sc, False)],
-        (1, 1): [lambda: s2_sides(1)],
-        (2, 0): [s2_last, lambda: q_block(s2, False)],
-        (2, 1): [s3_ready, lambda: q_block(s3, False)],
-        (2, 2): [finish_queries, lambda: attend_units(0, 2)],
-        (2, 3): [lambda: attend_units(2, 5)],
-        (3, 0): [lambda: attend_units(5, 8)],
-        (3, 1): [lambda: attend_units(8, 12)],
-        (3, 2): [lambda: attend_units(12, units)],
+        (0, 0): [lambda: v_last(0, s, 0, 6), lambda: v_last(1, s, 0, 6)],
+        (0, 1): [lambda: v_pass(0, s2, 2, 4), lambda: v_pass(1, s2, 2, 4), lambda: q_core(0)],
+        (0, 2): [lambda: v_last(0, s2, 2, 8), lambda: v_last(1, s2, 2, 8), lambda: q_stage_y(0)],
+        (0, 3): [in_place],
+        (1, 0): [lambda: q_block(s, 0, True), lambda: q_block(s, 1, True)],
+        (1, 1): [lambda: q_stage_z(0), lambda: q_stage_y(1), lambda: q_core(1), lambda: q_core(2)],
+        (1, 2): [lambda: q_core(3)],
+        (1, 3): [lambda: q_stage_last(0), q_core_ready, lambda: q_block(sc, 0), lambda: q_block(sc, 1)],
+        (2, 0): [lambda: q_stage_z(1), lambda: q_rest(0)],
+        (2, 1): [lambda: finish_queries(0), lambda: attend_units(0, 2)],
+        (2, 2): [lambda: attend_units(2, 5)],
+        (2, 3): [lambda: attend_units(5, per)],
+        (3, 0): [lambda: q_stage_last(1), lambda: q_rest(1)],
+        (3, 1): [lambda: finish_queries(1), lambda: attend_units(per, per + 2)],
+        (3, 2): [lambda: attend_units(per + 2, per + 5)],
+        (3, 3): [lambda: attend_units(per + 5, units)],
     }
 
     def fill(k, i):
         for task in fills.get((k, i), []):
             task()
-
-    def all_shards(src_of, dst, ssem, rsem):
-        copies = []
-        for d in range(1, NS):
-            p = up(s, d, NS)
-            c = remote(src_of(p), dst, ssem.at[d - 1], rsem, shard=p)
-            c.start()
-            copies.append(c)
-        return copies
-
-    def all_tensors(src_of, dst, ssem, rsem):
-        copies = []
-        for d in (4, 6, 2, 5, 3, 7, 1):
-            p = up(t, d, NT)
-            c = remote(src_of(p), dst, ssem.at[d - 1], rsem, tensor=p)
-            c.start()
-            copies.append(c)
-        return copies
-
-    def settle(copies):
-        for c in copies:
-            c.wait_send()
 
     u_send, u_recv = r["u_send"], r["u_recv"]
 
@@ -516,42 +635,14 @@
         sent.extend(all_shards(lambda p: e_send.at[k, p], e_recv.at[k, s], r["e_s"].at[k], r["e_r"].at[k, s]))
         e_recv[k, s] = e_send[k, s]
 
-    cpos = lax.broadcasted_iota(jnp.int32, (heads, ck.shape[1]), 1)
     load_wo.wait()
     for k in range(STEPS):
-        total = b_send[s]
-        for d in range(1, NS):
-            src = up(s, NS - d, NS)
-            arrive(b_recv.at[src], r["b_s"].at[d - 1], r["b_r"].at[src], shard=src)
-            total = total + b_recv[src]
-        norm = lax.rsqrt(total[:, qcols + 2 * HD : qcols + 2 * HD + 1] / width + EPSILON)
-        fresh = (total[:, : qcols + 2 * HD] * norm).astype(bf16).astype(f32)
-        fkv[k] = fresh[:, qcols:]
-        for row in range(rows):
-            for h in range(heads):
-                qs[row, h : h + 1, :] = fresh[row : row + 1, h * HD : (h + 1) * HD]
-        for row in range(rows):
-            q = qs[row]
-            valid = (cpos >= low[row]) & (cpos < high[row])
-            scores = lax.dot_general(q.astype(bf16), ck[row], TRANS, preferred_element_type=f32) * INV_ROOT
-            scores = jnp.where(valid, scores, -1e30)
-            top = jnp.max(scores, axis=1, keepdims=True)
-            news = []
-            for j in range(k + 1):
-                new = jnp.sum(q * fkv[j, row : row + 1, :HD], axis=1, keepdims=True) * INV_ROOT
-                news.append(new)
-                top = jnp.maximum(top, new)
-            weights = jnp.where(valid, jnp.exp(scores - top), 0.0)
-            summed = jnp.sum(weights, axis=1, keepdims=True)
-            mixed = jnp.dot(weights.astype(bf16), cv[row], preferred_element_type=f32)
-            for j in range(k + 1):
-                weight = jnp.exp(news[j] - top)
-                summed = summed + weight
-                mixed = mixed + weight.astype(bf16).astype(f32) * fkv[j, row : row + 1, HD:]
-            context = (mixed / summed).astype(bf16).astype(f32)
-            for h in range(heads):
-                c_send[row : row + 1, h * HD : (h + 1) * HD] = context[h : h + 1]
-
+        if k == 0:
+            first_context()
+        else:
+            take_fresh(k)
+            for row in range(rows):
+                join_fresh(k, row, *attend_stored(row))
         c_copies = all_shards(lambda p: c_send, c_recv.at[s], r["c_s"], r["c_r"].at[s])
         c_recv[s] = c_send[...]
         settle(b_copies)
@@ -579,6 +670,7 @@
             settle(d_copies)
             fill(k, 2)
             spread_update(k)
+            fill(k, 3)
             break
         after = state[...] + update
         state[...] = after
@@ -602,6 +694,17 @@
         for i in range(NS):
             out_ref[k, :, i * dblk : (i + 1) * dblk] = e_recv[k, i].astype(bf16)
     settle(sent)
+
+
+def write_out(context, updates, context_out, updates_out, sem):
+    copies = [
+        pltpu.make_async_copy(context, context_out, sem.at[0]),
+        pltpu.make_async_copy(updates, updates_out, sem.at[1]),
+    ]
+    for c in copies:
+        c.start()
+    for c in copies:
+        c.wait()
 
 
 def layer(lens, row_prompt, cache_len, states, x, wkv, wq, wo, cache):
@@ -656,8 +759,8 @@
         kc_r=dma((2, 5)),
         qy_s=dma((2,)),
         qy_r=dma((2,)),
-        qz_s=dma((6,)),
-        qz_r=dma((6,)),
+        qz_s=dma((8,)),
+        qz_r=dma((8,)),
         qc_s=dma((12,)),
         qc_r=dma((12,)),
         vy_s=dma((2,)),
@@ -666,6 +769,15 @@
         vz_r=dma((2, 8)),
         vc_s=dma((2, 10)),
         vc_r=dma((2, 10)),
+        n_send=vm((heads, 3 * HD), f32),
+        n_recv=vm((NG * NS, heads, 3 * HD), f32),
+        m_send=vm((NG * NS, heads, 3 * HD), f32),
+        m_recv=vm((NG * NS, heads, 3 * HD), f32),
+        part0=vm((rows, heads, 3 * HD), f32),
+        n_s=dma((NG * NS - 1,)),
+        n_r=dma((NG * NS,)),
+        m_s=dma((NG * NS - 1,)),
+        m_r=dma((NG * NS,)),
         a_s=dma((NS - 1,)),
         a_r=dma((NS,)),
         b_s=dma((NS - 1,)),
@@ -713,7 +825,7 @@
 ):
     dblk = w_query.shape[0]
     rows = decode_states.shape[0]
-    return layer(
+    context, updates = layer(
         prompt_lens,
         row_prompt,
         cache_len,
@@ -724,6 +836,16 @@
         w_out,
         kv_cache.reshape(rows, 2 * CACHE, HD),
     )
+    hbm = pl.BlockSpec(memory_space=pl.ANY)
+    return pl.pallas_call(
+        write_out,
+        out_shape=tuple(jax.ShapeDtypeStruct(v.shape, v.dtype) for v in (context, updates)),
+        in_specs=[hbm, hbm],
+        out_specs=(hbm, hbm),
+        scratch_shapes=[pltpu.SemaphoreType.DMA((2,))],
+        compiler_params=pltpu.CompilerParams(vmem_limit_bytes=62 * 1024 * 1024),
+        name="write_out",
+    )(context, updates)
 
 
 def solution(mesh):

time: 136 us -> 188 us (1.38)
  Pallas kernels: 131 us -> 187 us
  local copies, waits for them, and re-layouts: 4.01 us -> 0 us
    pallas_call x0 -> x1, Pallas kernels: none -> 40.8 us  [body(): pl.pallas_call(write_out, out_shape=tuple((jax.ShapeDtypeStruct(v.shape,...]
    pallas_call x1, Pallas kernels: 131 us -> 146 us  [layer(): pl.pallas_call(functools.partial(kernel, tuple(scratch)), out_shape=(jax....]
    unnamed x2 -> x0, local copies, waits for them, and re-layouts: 4.01 us -> none
where the time goes in v5:
time: 188 us
  Pallas kernels  187 us (99%)
    pallas_call x1, Pallas kernels, layer(): pl.pallas_call(functools.partial(kernel, tuple(scratch)), out_shape=(jax....  146 us
    pallas_call x1, Pallas kernels, body(): pl.pallas_call(write_out, out_shape=tuple((jax.ShapeDtypeStruct(v.shape,...  40.8 us

profile of v5, /device:TPU:1, one launch (start us, length us, event | category | flops | bytes accessed | tf_op | source)
XLA Modules:
  0.0 187.8 jit_solution(7220176127625984094)
XLA Ops:
  0.6 146.2 %attention_layer.1 = (bf16[512,1024]{1,0:T(8,128)(2,1)}, bf16[4,4,8192]{2,1,0:T(4,128)(2,1)}) custom-call(s32[4,3]{1,0:T(4,128)} %lens_ref.1, s32[4]{0:T(128)} %rowp_ref.1, s32[4]{0:T(128)} %clen_ref.1, bf16[4,8192]{1,0:T(4,128)(2,1)} %ds_ref.1, bf16[512,8192]{1,0:T(8,128)(2,1)} %x_hbm.1, bf16[4096,128]{1,0:T(8,128)(2,1)} %bitcast.3, ...), custom_call_target="tpu_custom_call" | custom-call | tf_op jit(solution)/shard_map/attention_layer/pallas_call | solution.py:799
  146.8 40.8 %write_out.1 = (bf16[512,1024]{1,0:T(8,128)(2,1)}, bf16[4,4,8192]{2,1,0:T(4,128)(2,1)}) custom-call(bf16[512,1024]{1,0:T(8,128)(2,1)} %get-tuple-element.4.context, bf16[4,4,8192]{2,1,0:T(4,128)(2,1)} %get-tuple-element.5.updates), custom_call_target="tpu_custom_call" | custom-call | tf_op jit(solution)/shard_map/write_out/pallas_call | solution.py:840

commit v6 on v5

--- a/solution.py
+++ b/solution.py
@@ -149,9 +149,15 @@
     ky_s, ky_r, kz_s, kz_r, kc_s, kc_r = (r[n] for n in ("ky_s", "ky_r", "kz_s", "kz_r", "kc_s", "kc_r"))
     qy_s, qy_r, qz_s, qz_r, qc_s, qc_r = (r[n] for n in ("qy_s", "qy_r", "qz_s", "qz_r", "qc_s", "qc_r"))
 
-    for i, j in ((0, 0), (0, 1), (1, 0), (1, 1)):
-        ref = krows(j, s, q_of[i])
-        send(ref, ref, ky_s.at[j, i], ky_r.at[j, i], shard=s2)
+    def y_start(src, ssem, rsem):
+        c = remote(src, src, ssem, rsem, shard=s2)
+        c.start()
+        return c
+
+    def k_send_y(j, i):
+        return y_start(krows(j, s, q_of[i]), ky_s.at[j, i], ky_r.at[j, i])
+
+    y_copy = k_send_y(0, 0)
     for j in range(2):
         ref = weights_of[j].at[s]
         send(ref, ref, kc_s.at[j, 4], kc_r.at[j, 4], shard=sc)
@@ -191,8 +197,7 @@
             arrive(ref, qc_s.at[8 + q], qc_r.at[8 + q], shard=sc)
 
     def q_send_y(i):
-        ref = qrows(s, g, i)
-        send(ref, ref, qy_s.at[i], qy_r.at[i], shard=s2)
+        return y_start(qrows(s, g, i), qy_s.at[i], qy_r.at[i])
 
     def q_arrive_y(i):
         arrive(qrows(s2, g, i), qy_s.at[i], qy_r.at[i], shard=s2)
@@ -402,11 +407,15 @@
                 jnp.where(new, mixed, mine[2]),
             )
 
+    y_copy.wait_send()
+    y_copy = k_send_y(1, 0)
     for j in range(2):
         kv_block(j, s, True)
     k_arrive_y(0, 0)
     k_forward_z(0)
     k_forward(0, 0)
+    y_copy.wait_send()
+    y_copy = k_send_y(0, 1)
 
     for d in range(1, NS):
         src = up(s, NS - d, NS)
@@ -417,12 +426,13 @@
     mine = pl.ds(pl.multiple_of(t * piece, piece), piece)
     state[...] = jnp.concatenate([a_recv[i, :, mine] for i in range(NS)], axis=0)
 
-    load_wq.wait()
-    b_copies = decode_project()
     k_arrive_y(1, 0)
     k_forward_z(1)
     k_forward(1, 0)
-    lax.fori_loop(0, tok // 32, squares, 0)
+    y_copy.wait_send()
+    y_copy = k_send_y(1, 1)
+    load_wq.wait()
+    b_copies = decode_project()
 
     def slot(j, gg, ss):
         return cached[j].at[pl.ds(pl.multiple_of(MOST + (gg * NS + ss) * tok, tok), tok)]
@@ -469,13 +479,15 @@
         ):
             arrive(ref, vc_s.at[j, i], vc_r.at[j, i], shard=sc)
 
-    for j in range(2):
+    def k_gather(j):
         k_arrive_z(j, 0)
         k_forward(j, 2)
         k_arrive_z(j, 1)
         k_forward(j, 3)
         k_arrive_y(j, 1)
         k_forward(j, 1)
+
+    def v_make(j):
         arrive(weights_of[j].at[sc], kc_s.at[j, 4], kc_r.at[j, 4], shard=sc)
         kv_block(j, sc, False)
         kv_block(j, s2, False)
@@ -486,16 +498,27 @@
             bf16
         )
         own = slot(j, g, s)
-        send(own, own, vy_s.at[j], vy_r.at[j], shard=s2)
+        c = y_start(own, vy_s.at[j], vy_r.at[j])
         v_sides(j, s, 0)
         v_core(j, own, 0)
-        if j == 0:
-            take_fresh(0)
-            ask()
-
+        return c
+
+    lax.fori_loop(0, tok // 32, squares, 0)
+    k_gather(0)
+    y_copy.wait_send()
+    y_copy = v_make(0)
+    k_gather(1)
+    take_fresh(0)
+    ask()
+    y_copy.wait_send()
+    y_copy = v_make(1)
+    v_theirs(0)
+    v_pass(0, s, 0, 2)
     answer()
-    q_send_y(0)
-    q_send_y(1)
+    y_copy.wait_send()
+    q_copies = [q_send_y(0)]
+    v_theirs(1)
+    v_pass(1, s, 0, 2)
 
     load_raw.wait()
     def separate(i, c):
@@ -510,19 +533,18 @@
         return c
 
     lax.fori_loop(0, 2 * ck.shape[1] // 256, separate, 0)
-    v_theirs(0)
-    v_pass(0, s, 0, 2)
     for row in range(rows):
         for i, v in enumerate(attend_stored(row)):
             part0[row, :, i * HD : (i + 1) * HD] = jnp.broadcast_to(v, (heads, HD))
-    v_theirs(1)
-    v_pass(1, s, 0, 2)
-
-    for i in range(tok // QT):
-        q_pos = s * tok + i * QT + lax.broadcasted_iota(jnp.int32, (QT, KW), 0)
-        k_pos = s * tok + i * QT - MOST + lax.broadcasted_iota(jnp.int32, (QT, KW), 1)
-        start = jnp.where(q_pos >= b1, b1, jnp.where(q_pos >= b0, b0, 0))
-        bias[i] = jnp.where((k_pos >= start) & (k_pos <= q_pos), 0.0, -1e30)
+    v_last(0, s, 0, 6)
+    v_pass(0, s2, 2, 4)
+
+    def build_mask():
+        for i in range(tok // QT):
+            q_pos = s * tok + i * QT + lax.broadcasted_iota(jnp.int32, (QT, KW), 0)
+            k_pos = s * tok + i * QT - MOST + lax.broadcasted_iota(jnp.int32, (QT, KW), 1)
+            start = jnp.where(q_pos >= b1, b1, jnp.where(q_pos >= b0, b0, 0))
+            bias[i] = jnp.where((k_pos >= start) & (k_pos <= q_pos), 0.0, -1e30)
 
     def splat(flag):
         return jnp.broadcast_to(flag, (HD, HD)).astype(f32).astype(bf16)
@@ -595,23 +617,27 @@
 
     units = heads * (tok // QT)
     per = units // 2
+    def q_next():
+        q_copies[0].wait_send()
+        q_copies.append(q_send_y(1))
+
     fills = {
-        (0, 0): [lambda: v_last(0, s, 0, 6), lambda: v_last(1, s, 0, 6)],
-        (0, 1): [lambda: v_pass(0, s2, 2, 4), lambda: v_pass(1, s2, 2, 4), lambda: q_core(0)],
-        (0, 2): [lambda: v_last(0, s2, 2, 8), lambda: v_last(1, s2, 2, 8), lambda: q_stage_y(0)],
+        (0, 0): [lambda: v_last(1, s, 0, 6), lambda: v_pass(1, s2, 2, 4)],
+        (0, 1): [lambda: v_last(0, s2, 2, 8), lambda: v_last(1, s2, 2, 8), lambda: q_core(0), lambda: q_core(1)],
+        (0, 2): [q_next, lambda: q_stage_y(0)],
         (0, 3): [in_place],
-        (1, 0): [lambda: q_block(s, 0, True), lambda: q_block(s, 1, True)],
-        (1, 1): [lambda: q_stage_z(0), lambda: q_stage_y(1), lambda: q_core(1), lambda: q_core(2)],
-        (1, 2): [lambda: q_core(3)],
-        (1, 3): [lambda: q_stage_last(0), q_core_ready, lambda: q_block(sc, 0), lambda: q_block(sc, 1)],
-        (2, 0): [lambda: q_stage_z(1), lambda: q_rest(0)],
-        (2, 1): [lambda: finish_queries(0), lambda: attend_units(0, 2)],
-        (2, 2): [lambda: attend_units(2, 5)],
-        (2, 3): [lambda: attend_units(5, per)],
-        (3, 0): [lambda: q_stage_last(1), lambda: q_rest(1)],
-        (3, 1): [lambda: finish_queries(1), lambda: attend_units(per, per + 2)],
-        (3, 2): [lambda: attend_units(per + 2, per + 5)],
-        (3, 3): [lambda: attend_units(per + 5, units)],
+        (1, 0): [lambda: q_core(2), lambda: q_core(3), lambda: q_block(s, 0, True), lambda: q_block(s, 1, True)],
+        (1, 1): [lambda: q_stage_y(1), build_mask],
+        (1, 2): [lambda: q_stage_z(0)],
+        (1, 3): [q_core_ready, lambda: q_block(sc, 0), lambda: q_block(sc, 1)],
+        (2, 0): [lambda: q_stage_last(0)],
+        (2, 1): [lambda: q_stage_z(1), lambda: q_rest(0)],
+        (2, 2): [lambda: finish_queries(0), lambda: attend_units(0, 2)],
+        (2, 3): [lambda: attend_units(2, 5)],
+        (3, 0): [lambda: q_stage_last(1), lambda: attend_units(5, per)],
+        (3, 1): [lambda: q_rest(1)],
+        (3, 2): [lambda: finish_queries(1), lambda: attend_units(per, per + 3)],
+        (3, 3): [lambda: attend_units(per + 3, units)],
     }
 
     def fill(k, i):
@@ -693,18 +719,13 @@
             arrive(e_recv.at[k, src], r["e_s"].at[k, d - 1], r["e_r"].at[k, src], shard=src)
         for i in range(NS):
             out_ref[k, :, i * dblk : (i + 1) * dblk] = e_recv[k, i].astype(bf16)
+    q_copies[1].wait_send()
     settle(sent)
 
 
-def write_out(context, updates, context_out, updates_out, sem):
-    copies = [
-        pltpu.make_async_copy(context, context_out, sem.at[0]),
-        pltpu.make_async_copy(updates, updates_out, sem.at[1]),
-    ]
-    for c in copies:
-        c.start()
-    for c in copies:
-        c.wait()
+def write_out(context, updates, context_out, updates_out):
+    context_out[...] = context[...]
+    updates_out[...] = updates[...]
 
 
 def layer(lens, row_prompt, cache_len, states, x, wkv, wq, wo, cache):
@@ -836,14 +857,12 @@
         w_out,
         kv_cache.reshape(rows, 2 * CACHE, HD),
     )
-    hbm = pl.BlockSpec(memory_space=pl.ANY)
+    vmem = pl.BlockSpec(memory_space=pltpu.VMEM)
     return pl.pallas_call(
         write_out,
         out_shape=tuple(jax.ShapeDtypeStruct(v.shape, v.dtype) for v in (context, updates)),
-        in_specs=[hbm, hbm],
-        out_specs=(hbm, hbm),
-        scratch_shapes=[pltpu.SemaphoreType.DMA((2,))],
-        compiler_params=pltpu.CompilerParams(vmem_limit_bytes=62 * 1024 * 1024),
+        in_specs=[vmem, vmem],
+        out_specs=(vmem, vmem),
         name="write_out",
     )(context, updates)
 

time: 188 us -> 138 us (0.73)
  Pallas kernels: 187 us -> 137 us
    pallas_call x1, Pallas kernels: 40.8 us -> 2.38 us  [body(): pl.pallas_call(write_out, out_shape=tuple((jax.ShapeDtypeStruct(v.shape,...]
    pallas_call x1, Pallas kernels: 146 us -> 135 us  [layer(): pl.pallas_call(functools.partial(kernel, tuple(scratch)), out_shape=(jax....]
where the time goes in v6:
time: 138 us
  Pallas kernels  137 us (99%)
    pallas_call x1, Pallas kernels, layer(): pl.pallas_call(functools.partial(kernel, tuple(scratch)), out_shape=(jax....  135 us

profile of v6, /device:TPU:1, one launch (start us, length us, event | category | flops | bytes accessed | tf_op | source)
XLA Modules:
  0.0 137.9 jit_solution(17381696478301288675)
XLA Ops:
  0.6 134.8 %attention_layer.1 = (bf16[512,1024]{1,0:T(8,128)(2,1)}, bf16[4,4,8192]{2,1,0:T(4,128)(2,1)}) custom-call(s32[4,3]{1,0:T(4,128)} %lens_ref.1, s32[4]{0:T(128)} %rowp_ref.1, s32[4]{0:T(128)} %clen_ref.1, bf16[4,8192]{1,0:T(4,128)(2,1)} %ds_ref.1, bf16[512,8192]{1,0:T(8,128)(2,1)} %x_hbm.1, bf16[4096,128]{1,0:T(8,128)(2,1)} %bitcast.3, ...), custom_call_target="tpu_custom_call" | custom-call | tf_op jit(solution)/shard_map/attention_layer/pallas_call | solution.py:820
  135.5 2.4 %write_out.1 = (bf16[512,1024]{1,0:T(8,128)(2,1)}, bf16[4,4,8192]{2,1,0:T(4,128)(2,1)}) custom-call(bf16[512,1024]{1,0:T(8,128)(2,1)} %get-tuple-element.4.context, bf16[4,4,8192]{2,1,0:T(4,128)(2,1)} %get-tuple-element.5.updates), custom_call_target="tpu_custom_call" | custom-call | tf_op jit(solution)/shard_map/write_out/pallas_call | solution.py:861

commit v7 on v4

--- a/solution.py
+++ b/solution.py
@@ -184,7 +184,9 @@
 
     def q_send_y(i):
         ref = qrows(s, g, i)
-        send(ref, ref, qy_s.at[i], qy_r.at[i], shard=s2)
+        c = remote(ref, ref, qy_s.at[i], qy_r.at[i], shard=s2)
+        c.start()
+        return c
 
     def q_arrive_y(i):
         arrive(qrows(s2, g, i), qy_s.at[i], qy_r.at[i], shard=s2)
@@ -352,8 +354,7 @@
 
     load_wq.wait()
     b_copies = decode_project()
-    q_send_y(0)
-    q_send_y(1)
+    q_copy = q_send_y(0)
 
     load_raw.wait()
     def separate(i, c):
@@ -408,6 +409,8 @@
 
     place(0)
     v_last(1, s2, 2, 8)
+    q_copy.wait_send()
+    q_copy = q_send_y(1)
     v_core_ready(1)
     place(1)
     q_arrive_y(0)
@@ -459,8 +462,8 @@
     units = heads * (tok // QT)
     fills = {
         (0, 0): [lambda: q_core(0), lambda: q_block(s, True)],
-        (0, 1): [s2_early, lambda: q_core(1)],
-        (0, 2): [lambda: q_core(2)],
+        (0, 1): [lambda: q_core(1)],
+        (0, 2): [s2_early, lambda: q_core(2)],
         (0, 3): [lambda: s2_sides(0), lambda: q_core(3)],
         (1, 0): [q_core_ready, lambda: q_block(sc, False)],
         (1, 1): [lambda: s2_sides(1)],
@@ -469,8 +472,9 @@
         (2, 2): [finish_queries, lambda: attend_units(0, 2)],
         (2, 3): [lambda: attend_units(2, 5)],
         (3, 0): [lambda: attend_units(5, 8)],
-        (3, 1): [lambda: attend_units(8, 12)],
-        (3, 2): [lambda: attend_units(12, units)],
+        (3, 1): [lambda: attend_units(8, 11)],
+        (3, 2): [lambda: attend_units(11, 13)],
+        (3, 3): [lambda: attend_units(13, units)],
     }
 
     def fill(k, i):
@@ -579,6 +583,7 @@
             settle(d_copies)
             fill(k, 2)
             spread_update(k)
+            fill(k, 3)
             break
         after = state[...] + update
         state[...] = after
@@ -601,7 +606,13 @@
             arrive(e_recv.at[k, src], r["e_s"].at[k, d - 1], r["e_r"].at[k, src], shard=src)
         for i in range(NS):
             out_ref[k, :, i * dblk : (i + 1) * dblk] = e_recv[k, i].astype(bf16)
+    q_copy.wait_send()
     settle(sent)
+
+
+def write_out(context, updates, context_out, updates_out):
+    context_out[...] = context[...]
+    updates_out[...] = updates[...]
 
 
 def layer(lens, row_prompt, cache_len, states, x, wkv, wq, wo, cache):
@@ -713,7 +724,7 @@
 ):
     dblk = w_query.shape[0]
     rows = decode_states.shape[0]
-    return layer(
+    context, updates = layer(
         prompt_lens,
         row_prompt,
         cache_len,
@@ -724,6 +735,14 @@
         w_out,
         kv_cache.reshape(rows, 2 * CACHE, HD),
     )
+    vmem = pl.BlockSpec(memory_space=pltpu.VMEM)
+    return pl.pallas_call(
+        write_out,
+        out_shape=tuple(jax.ShapeDtypeStruct(v.shape, v.dtype) for v in (context, updates)),
+        in_specs=[vmem, vmem],
+        out_specs=(vmem, vmem),
+        name="write_out",
+    )(context, updates)
 
 
 def solution(mesh):

time: 136 us -> 138 us (1.015)
  Pallas kernels: 131 us -> 137 us
  local copies, waits for them, and re-layouts: 4.01 us -> 0 us
    unnamed x2 -> x0, local copies, waits for them, and re-layouts: 4.01 us -> none
    pallas_call x1, Pallas kernels: 131 us -> 135 us  [layer(): pl.pallas_call(functools.partial(kernel, tuple(scratch)), out_shape=(jax....]
    pallas_call x0 -> x1, Pallas kernels: none -> 2.38 us  [body(): pl.pallas_call(write_out, out_shape=tuple((jax.ShapeDtypeStruct(v.shape,...]
where the time goes in v7:
time: 138 us
  Pallas kernels  137 us (99%)
    pallas_call x1, Pallas kernels, layer(): pl.pallas_call(functools.partial(kernel, tuple(scratch)), out_shape=(jax....  135 us

profile of v7, /device:TPU:1, one launch (start us, length us, event | category | flops | bytes accessed | tf_op | source)
XLA Modules:
  0.0 137.7 jit_solution(1945367743632010127)
XLA Ops:
  0.6 134.7 %attention_layer.1 = (bf16[512,1024]{1,0:T(8,128)(2,1)}, bf16[4,4,8192]{2,1,0:T(4,128)(2,1)}) custom-call(s32[4,3]{1,0:T(4,128)} %lens_ref.1, s32[4]{0:T(128)} %rowp_ref.1, s32[4]{0:T(128)} %clen_ref.1, bf16[4,8192]{1,0:T(4,128)(2,1)} %ds_ref.1, bf16[512,8192]{1,0:T(8,128)(2,1)} %x_hbm.1, bf16[4096,128]{1,0:T(8,128)(2,1)} %bitcast.3, ...), custom_call_target="tpu_custom_call" | custom-call | tf_op jit(solution)/shard_map/attention_layer/pallas_call | solution.py:698
  135.3 2.4 %write_out.1 = (bf16[512,1024]{1,0:T(8,128)(2,1)}, bf16[4,4,8192]{2,1,0:T(4,128)(2,1)}) custom-call(bf16[512,1024]{1,0:T(8,128)(2,1)} %get-tuple-element.4.context, bf16[4,4,8192]{2,1,0:T(4,128)(2,1)} %get-tuple-element.5.updates), custom_call_target="tpu_custom_call" | custom-call | tf_op jit(solution)/shard_map/write_out/pallas_call | solution.py:739

commit v8 on v4

--- a/solution.py
+++ b/solution.py
@@ -602,6 +602,11 @@
         for i in range(NS):
             out_ref[k, :, i * dblk : (i + 1) * dblk] = e_recv[k, i].astype(bf16)
     settle(sent)
+
+
+def write_out(context, updates, context_out, updates_out):
+    context_out[...] = context[...]
+    updates_out[...] = updates[...]
 
 
 def layer(lens, row_prompt, cache_len, states, x, wkv, wq, wo, cache):
@@ -713,7 +718,7 @@
 ):
     dblk = w_query.shape[0]
     rows = decode_states.shape[0]
-    return layer(
+    context, updates = layer(
         prompt_lens,
         row_prompt,
         cache_len,
@@ -724,6 +729,14 @@
         w_out,
         kv_cache.reshape(rows, 2 * CACHE, HD),
     )
+    vmem = pl.BlockSpec(memory_space=pltpu.VMEM)
+    return pl.pallas_call(
+        write_out,
+        out_shape=tuple(jax.ShapeDtypeStruct(v.shape, v.dtype) for v in (context, updates)),
+        in_specs=[vmem, vmem],
+        out_specs=(vmem, vmem),
+        name="write_out",
+    )(context, updates)
 
 
 def solution(mesh):

time: 136 us -> 134 us (0.985)
  local copies, waits for them, and re-layouts: 4.01 us -> 0 us
  Pallas kernels: 131 us -> 134 us
    unnamed x2 -> x0, local copies, waits for them, and re-layouts: 4.01 us -> none
    pallas_call x0 -> x1, Pallas kernels: none -> 2.38 us  [body(): pl.pallas_call(write_out, out_shape=tuple((jax.ShapeDtypeStruct(v.shape,...]
where the time goes in v8:
time: 134 us
  Pallas kernels  134 us (100%)
    pallas_call x1, Pallas kernels, layer(): pl.pallas_call(functools.partial(kernel, tuple(scratch)), out_shape=(jax....  131 us

profile of v8, /device:TPU:1, one launch (start us, length us, event | category | flops | bytes accessed | tf_op | source)
XLA Modules:
  0.0 134.3 jit_solution(3227992368615970556)
XLA Ops:
  0.6 131.2 %attention_layer.1 = (bf16[512,1024]{1,0:T(8,128)(2,1)}, bf16[4,4,8192]{2,1,0:T(4,128)(2,1)}) custom-call(s32[4,3]{1,0:T(4,128)} %lens_ref.1, s32[4]{0:T(128)} %rowp_ref.1, s32[4]{0:T(128)} %clen_ref.1, bf16[4,8192]{1,0:T(4,128)(2,1)} %ds_ref.1, bf16[512,8192]{1,0:T(8,128)(2,1)} %x_hbm.1, bf16[4096,128]{1,0:T(8,128)(2,1)} %bitcast.3, ...), custom_call_target="tpu_custom_call" | custom-call | tf_op jit(solution)/shard_map/attention_layer/pallas_call | solution.py:692
  131.9 2.4 %write_out.1 = (bf16[512,1024]{1,0:T(8,128)(2,1)}, bf16[4,4,8192]{2,1,0:T(4,128)(2,1)}) custom-call(bf16[512,1024]{1,0:T(8,128)(2,1)} %get-tuple-element.4.context, bf16[4,4,8192]{2,1,0:T(4,128)(2,1)} %get-tuple-element.5.updates), custom_call_target="tpu_custom_call" | custom-call | tf_op jit(solution)/shard_map/write_out/pallas_call | solution.py:733
